TPU v7x, 256 devices: a whole 4x4x8 slice. The times are simulated.
256 devices in a mesh: section: 4 (over x), row: 4 (over y), col: 16 (over z, core).
Axes of the slice: x: 4, y: 4, z: 8, core: 2. Of those that a mesh axis runs over, the one named last changes fastest.
Arguments:
- hidden_in: bfloat16 [2, 256, 8192], P(None, None, 'col'), may hold values from -24 to 24
- lengths: int32 [2, 32], replicated, may hold values from 1 to 64, 256 in all within a row
- gain: float32 [4, 8192], P('section', 'col'), may hold values from 0.1 to 1.9
- w_query: bfloat16 [4, 8192, 8192], P('section', 'col', 'row'), may hold values from -0.09375 to 0.09375
- w_pair: bfloat16 [4, 8192, 2048], P('section', 'col', 'row'), may hold values from -0.0625 to 0.0625
- w_out: bfloat16 [4, 8192, 8192], P('section', 'row', 'col'), may hold values from -0.0625 to 0.0625
Outputs:
- hidden_states: bfloat16 [4, 2, 256, 8192], P('section', None, None, 'col')
Inputs may be any that keep to these rules, and one draw needn't show every extreme that they name: Each row of lengths sums to 256, and its largest entry is exactly 64.
All inputs are finite; a program needn't handle non-finite values.
Results may differ from a plain program's by a relative error of at most 0.019.
Values may be sent and summed in bfloat16 or wider, within the bound.
No kernel may reach another device: no remote copies, remote signals or barrier semaphores. Data moves between devices by JAX's collectives and lax.ppermute only.
A program may use at most 64 MiB of HBM per device.

v0:
```python
import jax
import jax.numpy as jnp
from jax import lax
from jax.sharding import PartitionSpec as P

HEADS = 64
KV_HEADS = 8
HEAD = 128


ROPE_BASE = 500000.0
EPSILON = 1e-05


def shifted(value, axis, steps):
    count = lax.axis_size(axis)
    first, last = (max(0, -steps), min(count, count - steps))
    return lax.ppermute(value, axis, [(source, source + steps) for source in range(first, last)])


def segment_info(lengths_row, total):
    token_ids = jnp.arange(total, dtype=jnp.int32)
    ends = jnp.cumsum(lengths_row)
    after = (token_ids[:, None] >= ends[None, :]).astype(jnp.int32)
    seg_ids = jnp.sum(after, axis=1)
    starts = jnp.sum(after * lengths_row[None, :], axis=1)
    return (seg_ids, token_ids - starts)


def rotate(values, positions):
    half = values.shape[-1] // 2
    exponent = jnp.arange(half, dtype=jnp.float32) * (2.0 / values.shape[-1])
    freqs = jnp.power(jnp.float32(ROPE_BASE), -exponent)
    angles = positions.astype(jnp.float32)[:, None] * freqs[None, :]
    cosine = jnp.cos(angles)[:, None, :]
    sine = jnp.sin(angles)[:, None, :]
    first = values[..., :half]
    second = values[..., half:]
    return jnp.concatenate(
        [first * cosine - second * sine, second * cosine + first * sine], axis=-1
    )


def attend(queries, keys, values, query_seg, query_pos, key_seg, key_pos):
    scale = queries.shape[-1] ** (-0.5)
    scores = jnp.einsum("qhgd,khd->hgqk", queries, keys, preferred_element_type=jnp.float32) * scale
    allowed = (query_seg[:, None] == key_seg[None, :]) & (key_pos[None, :] <= query_pos[:, None])
    raised = jnp.where(allowed[None, None], jnp.exp(scores), jnp.float32(0.0))
    weights = (raised / jnp.sum(raised, axis=-1, keepdims=True)).astype(jnp.bfloat16)
    mixed = jnp.einsum("hgqk,khd->qhgd", weights, values, preferred_element_type=jnp.float32)
    return mixed.astype(jnp.bfloat16)


def local(hidden_in, lengths, gain, w_query, w_pair, w_out):
    split = 1
    micro, tok, width = hidden_in.shape
    rows = tok // split
    units = micro * split
    sections = lax.axis_size("section")
    section = lax.axis_index("section")
    col_size = lax.axis_size("col")
    col_index = lax.axis_index("col")
    gain_row = gain[0]
    query_w = w_query[0]
    pair_w = w_pair[0]
    out_w = w_out[0]
    head_dim = HEAD
    kv_local = pair_w.shape[1] // (2 * head_dim)
    group = HEADS // KV_HEADS
    full_width = width * col_size
    seg_all, pos_all = jax.vmap(lambda lengths_row: segment_info(lengths_row, tok))(lengths)

    def layer(block_in, seg_row, pos_row):
        wide = block_in.astype(jnp.float32)
        scaled = (wide * gain_row[None, :]).astype(jnp.bfloat16)
        squares = jnp.sum(wide * wide, axis=1)
        query_part = jnp.dot(scaled, query_w, preferred_element_type=jnp.float32)
        pair_part = jnp.dot(scaled, pair_w, preferred_element_type=jnp.float32)
        pair_sum, square_sum = lax.psum((pair_part, squares), "col")
        query_sum = lax.psum_scatter(query_part, "col", scatter_dimension=1, tiled=True)
        inverse = lax.rsqrt(square_sum / full_width + EPSILON)
        queries = rotate(
            (query_sum * inverse[:, None]).reshape(rows, -1, head_dim), pos_row
        ).astype(jnp.bfloat16)
        pairs = (pair_sum * inverse[:, None]).reshape(rows, kv_local, 2, head_dim)
        own = jnp.stack([rotate(pairs[:, :, 0], pos_row), pairs[:, :, 1]], axis=2).astype(
            jnp.bfloat16
        )
        queries = queries.reshape(rows, 1, -1, head_dim)
        keys_all = own
        pick = col_index * queries.shape[2] // group
        keys_all = lax.dynamic_slice_in_dim(keys_all, pick, 1, 1)
        mixed = attend(
            queries, keys_all[:, :, 0], keys_all[:, :, 1], seg_row, pos_row, seg_row, pos_row
        )
        mixed = mixed.reshape(rows, -1)
        partial_value = jnp.dot(
            lax.all_gather(mixed, "col", axis=1, tiled=True),
            out_w,
            preferred_element_type=jnp.float32,
        )
        branch = lax.psum(partial_value, "row")
        return ((wide + branch).astype(jnp.bfloat16), own)

    outputs = jnp.zeros((micro, tok, width), jnp.bfloat16)
    incoming = jnp.zeros((rows, width), jnp.bfloat16)
    earlier = jnp.zeros((rows, kv_local, 2, head_dim), jnp.bfloat16)

    def tick(step, carry):
        incoming, earlier, outputs = carry
        unit = step - section
        live = (unit >= 0) & (unit < units)
        held = jnp.clip(unit, 0, units - 1)
        micro_id = held // split
        part = held % split
        base = part * rows
        source = lax.dynamic_index_in_dim(hidden_in, micro_id, 0, keepdims=False)
        block_in = jnp.where(section == 0, source, incoming)
        seg_row = lax.dynamic_index_in_dim(seg_all, micro_id, 0, keepdims=False)
        pos_row = lax.dynamic_index_in_dim(pos_all, micro_id, 0, keepdims=False)
        result, current = layer(block_in, seg_row, pos_row)
        previous = lax.dynamic_slice(outputs, (micro_id, base, jnp.int32(0)), (1, rows, width))
        kept = jnp.where(live, result[None], previous)
        outputs = lax.dynamic_update_slice(outputs, kept, (micro_id, base, jnp.int32(0)))
        passed = shifted(result, "section", 1)
        return (passed, current, outputs)

    final = lax.fori_loop(0, units + sections - 1, tick, (incoming, earlier, outputs))
    return final[2][None]


def solution(mesh):
    in_specs = (
        P(None, None, "col"),
        P(),
        P("section", "col"),
        P("section", "col", "row"),
        P("section", "col", "row"),
        P("section", "row", "col"),
    )
    out_specs = P("section", None, None, "col")
    return jax.shard_map(local, mesh=mesh, in_specs=in_specs, out_specs=out_specs, check_vma=False)
```

profile of v0, /device:TPU:1, one launch (start us, length us, event | category | flops | bytes accessed | tf_op | source)
XLA Modules:
  0.0 1390.1 jit_solution(11391388081969102924)
XLA Ops:
  8.3 1374.2 %while.18 = (s32[]{:T(128)}, bf16[256,512]{1,0:T(8,128)(2,1)S(1)}, bf16[2,256,512]{2,1,0:T(8,128)(2,1)S(1)}, pred[]{:T(512)}, s32[]{:T(128)}, /*index=5*/bf16[2,...) while((s32[]{:T(128)}, bf16[256,512]{1,0:T(8,128)(2,1)S(1)}, ...), condition=%wide.region_10.11_spmd, body=%wide.region_3.10_spmd.sunk | while | flops 1245217408 | bytes 52267256 | solution.py:128
  14.1 27.4 %psum.48 = f32[256]{0:T(256)S(1)} all-reduce(f32[256]{0:T(256)S(1)} %get-tuple-element.539), channel_id=1, replica_groups=mesh['section'=4,'row'=4,'col'=16] {'col'}, use_global_device_ids=true, to_apply=%region_6.6 | all-reduce | flops 256 | bytes 2048 | tf_op jit(solution)/shard_map/while/body/eval_jaxpr/psum | solution.py:79
  42.1 83.3 %all-reduce.3.cloned.1.call-done = f32[256,512]{1,0:T(8,128)} async-done(((f32[256,512]{1,0:T(8,128)}), f32[256,512]{1,0:T(8,128)}) %all-reduce.3.cloned.1.call-update) | async-done | bytes 524304 | tf_op jit(solution)/shard_map/while/body/eval_jaxpr/psum | solution.py:79
  127.7 56.9 %reduce-scatter.2.cloned.1.call-done = f32[256,128]{1,0:T(8,128)} async-done(((f32[256,2048]{1,0:T(8,128)}), f32[256,128]{1,0:T(8,128)}) %reduce-scatter.2.cloned.1.call-update) | async-done | bytes 131088 | tf_op jit(solution)/shard_map/while/body/eval_jaxpr/reduce_scatter | solution.py:80
  187.5 40.5 %all-gather.5.cloned.1.call-done = bf16[256,1,1,2048]{0,3,2,1:T(8,128)(2,1)} async-done(((bf16[256,1,1,128]{0,3,2,1:T(8,128)(2,1)}), bf16[256,1,1,2048]{0,3,2,1:T(8,128)(2,1)}) %all-gather.5.cloned.1.call-update) | async-done | bytes 1048592 | tf_op jit(solution)/shard_map/while/body/eval_jaxpr/all_gather | solution.py:98
  230.8 44.7 %all-reduce.5.cloned.1.call-done = f32[256,512]{1,0:T(8,128)} async-done(((f32[256,512]{1,0:T(8,128)}), f32[256,512]{1,0:T(8,128)}) %all-reduce.5.cloned.1.call-update) | async-done | bytes 524304 | tf_op jit(solution)/shard_map/while/body/eval_jaxpr/psum | solution.py:102
  316.1 84.5 %all-reduce.3.cloned.1.call-done = f32[256,512]{1,0:T(8,128)} async-done(((f32[256,512]{1,0:T(8,128)}), f32[256,512]{1,0:T(8,128)}) %all-reduce.3.cloned.1.call-update) | async-done | bytes 524304 | tf_op jit(solution)/shard_map/while/body/eval_jaxpr/psum | solution.py:79
  403.0 56.8 %reduce-scatter.2.cloned.1.call-done = f32[256,128]{1,0:T(8,128)} async-done(((f32[256,2048]{1,0:T(8,128)}), f32[256,128]{1,0:T(8,128)}) %reduce-scatter.2.cloned.1.call-update) | async-done | bytes 131088 | tf_op jit(solution)/shard_map/while/body/eval_jaxpr/reduce_scatter | solution.py:80
  462.6 40.3 %all-gather.5.cloned.1.call-done = bf16[256,1,1,2048]{0,3,2,1:T(8,128)(2,1)} async-done(((bf16[256,1,1,128]{0,3,2,1:T(8,128)(2,1)}), bf16[256,1,1,2048]{0,3,2,1:T(8,128)(2,1)}) %all-gather.5.cloned.1.call-update) | async-done | bytes 1048592 | tf_op jit(solution)/shard_map/while/body/eval_jaxpr/all_gather | solution.py:98
  505.7 44.7 %all-reduce.5.cloned.1.call-done = f32[256,512]{1,0:T(8,128)} async-done(((f32[256,512]{1,0:T(8,128)}), f32[256,512]{1,0:T(8,128)}) %all-reduce.5.cloned.1.call-update) | async-done | bytes 524304 | tf_op jit(solution)/shard_map/while/body/eval_jaxpr/psum | solution.py:102
  563.5 26.9 %psum.48 = f32[256]{0:T(256)S(1)} all-reduce(f32[256]{0:T(256)S(1)} %get-tuple-element.539), channel_id=1, replica_groups=mesh['section'=4,'row'=4,'col'=16] {'col'}, use_global_device_ids=true, to_apply=%region_6.6 | all-reduce | flops 256 | bytes 2048 | tf_op jit(solution)/shard_map/while/body/eval_jaxpr/psum | solution.py:79
  591.0 84.4 %all-reduce.3.cloned.1.call-done = f32[256,512]{1,0:T(8,128)} async-done(((f32[256,512]{1,0:T(8,128)}), f32[256,512]{1,0:T(8,128)}) %all-reduce.3.cloned.1.call-update) | async-done | bytes 524304 | tf_op jit(solution)/shard_map/while/body/eval_jaxpr/psum | solution.py:79
  677.7 56.8 %reduce-scatter.2.cloned.1.call-done = f32[256,128]{1,0:T(8,128)} async-done(((f32[256,2048]{1,0:T(8,128)}), f32[256,128]{1,0:T(8,128)}) %reduce-scatter.2.cloned.1.call-update) | async-done | bytes 131088 | tf_op jit(solution)/shard_map/while/body/eval_jaxpr/reduce_scatter | solution.py:80
  737.3 40.5 %all-gather.5.cloned.1.call-done = bf16[256,1,1,2048]{0,3,2,1:T(8,128)(2,1)} async-done(((bf16[256,1,1,128]{0,3,2,1:T(8,128)(2,1)}), bf16[256,1,1,2048]{0,3,2,1:T(8,128)(2,1)}) %all-gather.5.cloned.1.call-update) | async-done | bytes 1048592 | tf_op jit(solution)/shard_map/while/body/eval_jaxpr/all_gather | solution.py:98
  780.6 44.7 %all-reduce.5.cloned.1.call-done = f32[256,512]{1,0:T(8,128)} async-done(((f32[256,512]{1,0:T(8,128)}), f32[256,512]{1,0:T(8,128)}) %all-reduce.5.cloned.1.call-update) | async-done | bytes 524304 | tf_op jit(solution)/shard_map/while/body/eval_jaxpr/psum | solution.py:102
  838.4 26.9 %psum.48 = f32[256]{0:T(256)S(1)} all-reduce(f32[256]{0:T(256)S(1)} %get-tuple-element.539), channel_id=1, replica_groups=mesh['section'=4,'row'=4,'col'=16] {'col'}, use_global_device_ids=true, to_apply=%region_6.6 | all-reduce | flops 256 | bytes 2048 | tf_op jit(solution)/shard_map/while/body/eval_jaxpr/psum | solution.py:79
  865.9 84.5 %all-reduce.3.cloned.1.call-done = f32[256,512]{1,0:T(8,128)} async-done(((f32[256,512]{1,0:T(8,128)}), f32[256,512]{1,0:T(8,128)}) %all-reduce.3.cloned.1.call-update) | async-done | bytes 524304 | tf_op jit(solution)/shard_map/while/body/eval_jaxpr/psum | solution.py:79
  952.8 56.8 %reduce-scatter.2.cloned.1.call-done = f32[256,128]{1,0:T(8,128)} async-done(((f32[256,2048]{1,0:T(8,128)}), f32[256,128]{1,0:T(8,128)}) %reduce-scatter.2.cloned.1.call-update) | async-done | bytes 131088 | tf_op jit(solution)/shard_map/while/body/eval_jaxpr/reduce_scatter | solution.py:80
  1012.4 40.3 %all-gather.5.cloned.1.call-done = bf16[256,1,1,2048]{0,3,2,1:T(8,128)(2,1)} async-done(((bf16[256,1,1,128]{0,3,2,1:T(8,128)(2,1)}), bf16[256,1,1,2048]{0,3,2,1:T(8,128)(2,1)}) %all-gather.5.cloned.1.call-update) | async-done | bytes 1048592 | tf_op jit(solution)/shard_map/while/body/eval_jaxpr/all_gather | solution.py:98
  1055.5 44.7 %all-reduce.5.cloned.1.call-done = f32[256,512]{1,0:T(8,128)} async-done(((f32[256,512]{1,0:T(8,128)}), f32[256,512]{1,0:T(8,128)}) %all-reduce.5.cloned.1.call-update) | async-done | bytes 524304 | tf_op jit(solution)/shard_map/while/body/eval_jaxpr/psum | solution.py:102
  1140.8 84.5 %all-reduce.3.cloned.1.call-done = f32[256,512]{1,0:T(8,128)} async-done(((f32[256,512]{1,0:T(8,128)}), f32[256,512]{1,0:T(8,128)}) %all-reduce.3.cloned.1.call-update) | async-done | bytes 524304 | tf_op jit(solution)/shard_map/while/body/eval_jaxpr/psum | solution.py:79
  1227.7 56.8 %reduce-scatter.2.cloned.1.call-done = f32[256,128]{1,0:T(8,128)} async-done(((f32[256,2048]{1,0:T(8,128)}), f32[256,128]{1,0:T(8,128)}) %reduce-scatter.2.cloned.1.call-update) | async-done | bytes 131088 | tf_op jit(solution)/shard_map/while/body/eval_jaxpr/reduce_scatter | solution.py:80
  1287.3 40.3 %all-gather.5.cloned.1.call-done = bf16[256,1,1,2048]{0,3,2,1:T(8,128)(2,1)} async-done(((bf16[256,1,1,128]{0,3,2,1:T(8,128)(2,1)}), bf16[256,1,1,2048]{0,3,2,1:T(8,128)(2,1)}) %all-gather.5.cloned.1.call-update) | async-done | bytes 1048592 | tf_op jit(solution)/shard_map/while/body/eval_jaxpr/all_gather | solution.py:98
  1330.4 44.7 %all-reduce.5.cloned.1.call-done = f32[256,512]{1,0:T(8,128)} async-done(((f32[256,512]{1,0:T(8,128)}), f32[256,512]{1,0:T(8,128)}) %all-reduce.5.cloned.1.call-update) | async-done | bytes 524304 | tf_op jit(solution)/shard_map/while/body/eval_jaxpr/psum | solution.py:102
  (204 shorter events, 163.3 us)
Async XLA Ops:
  8.3 117.1 %all-reduce.3.cloned.1.call-start = ((), (), s32[]{:S(2)}) async-start(), calls=%async_computation.2 | async-start | bytes 1048576 | tf_op jit(solution)/shard_map/while/body/eval_jaxpr/psum | solution.py:79
  11.8 172.8 %reduce-scatter.2.cloned.1.call-start = ((), (), s32[]{:S(2)}) async-start(), calls=%async_computation.1 | async-start | bytes 2228224 | tf_op jit(solution)/shard_map/while/body/eval_jaxpr/reduce_scatter | solution.py:80
  14.0 214.0 %all-gather.5.cloned.1.call-start = ((), (), s32[]{:S(2)}) async-start(), calls=%async_computation.3 | async-start | bytes 1114112 | tf_op jit(solution)/shard_map/while/body/eval_jaxpr/all_gather | solution.py:98
  187.4 88.1 %all-reduce.5.cloned.1.call-start = ((), (), s32[]{:S(2)}) async-start(), calls=%async_computation.4 | async-start | bytes 1048576 | tf_op jit(solution)/shard_map/while/body/eval_jaxpr/psum | solution.py:102
  276.7 6.2 collective-permute-start
  282.9 117.7 %all-reduce.3.cloned.1.call-start = ((), (), s32[]{:S(2)}) async-start(), calls=%async_computation.2 | async-start | bytes 1048576 | tf_op jit(solution)/shard_map/while/body/eval_jaxpr/psum | solution.py:79
  286.4 173.4 %reduce-scatter.2.cloned.1.call-start = ((), (), s32[]{:S(2)}) async-start(), calls=%async_computation.1 | async-start | bytes 2228224 | tf_op jit(solution)/shard_map/while/body/eval_jaxpr/reduce_scatter | solution.py:80
  288.6 214.4 %all-gather.5.cloned.1.call-start = ((), (), s32[]{:S(2)}) async-start(), calls=%async_computation.3 | async-start | bytes 1114112 | tf_op jit(solution)/shard_map/while/body/eval_jaxpr/all_gather | solution.py:98
  462.6 87.9 %all-reduce.5.cloned.1.call-start = ((), (), s32[]{:S(2)}) async-start(), calls=%async_computation.4 | async-start | bytes 1048576 | tf_op jit(solution)/shard_map/while/body/eval_jaxpr/psum | solution.py:102
  551.6 6.2 collective-permute-start
  557.8 117.5 %all-reduce.3.cloned.1.call-start = ((), (), s32[]{:S(2)}) async-start(), calls=%async_computation.2 | async-start | bytes 1048576 | tf_op jit(solution)/shard_map/while/body/eval_jaxpr/psum | solution.py:79
  561.3 173.2 %reduce-scatter.2.cloned.1.call-start = ((), (), s32[]{:S(2)}) async-start(), calls=%async_computation.1 | async-start | bytes 2228224 | tf_op jit(solution)/shard_map/while/body/eval_jaxpr/reduce_scatter | solution.py:80
  563.5 214.4 %all-gather.5.cloned.1.call-start = ((), (), s32[]{:S(2)}) async-start(), calls=%async_computation.3 | async-start | bytes 1114112 | tf_op jit(solution)/shard_map/while/body/eval_jaxpr/all_gather | solution.py:98
  737.3 88.1 %all-reduce.5.cloned.1.call-start = ((), (), s32[]{:S(2)}) async-start(), calls=%async_computation.4 | async-start | bytes 1048576 | tf_op jit(solution)/shard_map/while/body/eval_jaxpr/psum | solution.py:102
  826.5 6.2 collective-permute-start
  832.7 117.7 %all-reduce.3.cloned.1.call-start = ((), (), s32[]{:S(2)}) async-start(), calls=%async_computation.2 | async-start | bytes 1048576 | tf_op jit(solution)/shard_map/while/body/eval_jaxpr/psum | solution.py:79
  836.2 173.4 %reduce-scatter.2.cloned.1.call-start = ((), (), s32[]{:S(2)}) async-start(), calls=%async_computation.1 | async-start | bytes 2228224 | tf_op jit(solution)/shard_map/while/body/eval_jaxpr/reduce_scatter | solution.py:80
  838.4 214.3 %all-gather.5.cloned.1.call-start = ((), (), s32[]{:S(2)}) async-start(), calls=%async_computation.3 | async-start | bytes 1114112 | tf_op jit(solution)/shard_map/while/body/eval_jaxpr/all_gather | solution.py:98
  1012.4 87.9 %all-reduce.5.cloned.1.call-start = ((), (), s32[]{:S(2)}) async-start(), calls=%async_computation.4 | async-start | bytes 1048576 | tf_op jit(solution)/shard_map/while/body/eval_jaxpr/psum | solution.py:102
  1107.6 117.7 %all-reduce.3.cloned.1.call-start = ((), (), s32[]{:S(2)}) async-start(), calls=%async_computation.2 | async-start | bytes 1048576 | tf_op jit(solution)/shard_map/while/body/eval_jaxpr/psum | solution.py:79
  1111.1 173.4 %reduce-scatter.2.cloned.1.call-start = ((), (), s32[]{:S(2)}) async-start(), calls=%async_computation.1 | async-start | bytes 2228224 | tf_op jit(solution)/shard_map/while/body/eval_jaxpr/reduce_scatter | solution.py:80
  1113.2 214.4 %all-gather.5.cloned.1.call-start = ((), (), s32[]{:S(2)}) async-start(), calls=%async_computation.3 | async-start | bytes 1114112 | tf_op jit(solution)/shard_map/while/body/eval_jaxpr/all_gather | solution.py:98
  1287.2 87.9 %all-reduce.5.cloned.1.call-start = ((), (), s32[]{:S(2)}) async-start(), calls=%async_computation.4 | async-start | bytes 1048576 | tf_op jit(solution)/shard_map/while/body/eval_jaxpr/psum | solution.py:102
  1376.3 6.2 collective-permute-start
  (17 other events, 544.2 us)
Sparse Core Ops, SparseCore 0:
  12.0 113.3 all-reduce.2
  127.9 56.7 reduce-scatter.1
  187.6 40.4 all-gather.4
  230.9 44.5 all-reduce.4
  286.5 114.0 all-reduce.2
  403.0 56.7 reduce-scatter.1
  462.7 40.1 all-gather.4
  505.8 44.5 all-reduce.4
  561.4 113.9 all-reduce.2
  677.7 56.7 reduce-scatter.1
  737.4 40.3 all-gather.4
  780.7 44.5 all-reduce.4
  836.3 114.0 all-reduce.2
  952.8 56.7 reduce-scatter.1
  1012.5 40.1 all-gather.4
  1055.6 44.5 all-reduce.4
  1111.2 114.0 all-reduce.2
  1227.7 56.7 reduce-scatter.1
  1287.4 40.1 all-gather.4
  1330.5 44.5 all-reduce.4
where the time goes:
time: 1390 us
  waiting for transfers between devices  1150 us (83%)
  blocking collectives  135 us (10%)
  matrix products  40.7 us (3%)
  other arithmetic  31.7 us (2%)
  starting transfers between devices  15.3 us (1%)
    psum x5, waiting for transfers between devices, layer(): pair_sum, square_sum = lax.psum((pair_part, squares), 'col')  421 us
    reduce_scatter x5, waiting for transfers between devices, layer(): lax.psum_scatter(query_part, 'col', scatter_dimension=1, tiled=True)  284 us
    psum x5, waiting for transfers between devices, layer(): branch = lax.psum(partial_value, 'row')  224 us
    all_gather x5, waiting for transfers between devices, layer(): lax.all_gather(mixed, 'col', axis=1, tiled=True)  202 us
    psum x5, blocking collectives, layer(): pair_sum, square_sum = lax.psum((pair_part, squares), 'col')  135 us
  transfers between devices with their start and end apart: 25, of which 25 were waited for; matrix products, arithmetic and copies ran while one was open for 2% of the time, Pallas kernels for 0%

commit v1 on v0

v1 whole, which is shorter than its diff:
```python
import jax
import jax.numpy as jnp
from jax import lax
from jax.experimental import pallas as pl
from jax.experimental.pallas import tpu as pltpu
from jax.sharding import Mesh
from jax.sharding import PartitionSpec as P

HEAD = 128
WIDTH = 8192
TOK = 256
LAYERS = 4
ROPE_BASE = 500000.0
EPSILON = 1e-05

CHIPS = 8
OWN = TOK // CHIPS
HALO = 64
WINDOW = HALO + OWN
PACK = 2 * OWN + WINDOW
GRID = 16
PART = TOK // GRID

bf16 = jnp.bfloat16
f32 = jnp.float32
VMEM = pl.BlockSpec(memory_space=pltpu.VMEM)
PARAMS = pltpu.CompilerParams(vmem_limit_bytes=40 * 1024 * 1024)


def call(kernel, outs, args, flops):
    nbytes = sum(a.size * a.dtype.itemsize for a in args)
    return pl.pallas_call(
        kernel,
        out_shape=outs,
        in_specs=[VMEM] * len(args),
        out_specs=jax.tree.map(lambda _: VMEM, outs),
        compiler_params=PARAMS,
        cost_estimate=pl.CostEstimate(flops=flops, bytes_accessed=nbytes, transcendentals=0),
    )(*args)


def project_kernel(x_ref, near_ref, far_ref, out_ref):
    x = x_ref[...]
    half = x.shape[1] // 2
    y = jnp.dot(x[:, :half], near_ref[...], preferred_element_type=f32)
    y = y + jnp.dot(x[:, half:], far_ref[...], preferred_element_type=f32)
    gram = lax.dot_general(x, x, (((1,), (1,)), ((), ())), preferred_element_type=f32)
    rows = lax.broadcasted_iota(jnp.int32, gram.shape, 0)
    cols = lax.broadcasted_iota(jnp.int32, gram.shape, 1)
    squares = jnp.sum(jnp.where(rows == cols, gram, 0.0), axis=0, keepdims=True)
    first = lax.broadcasted_iota(jnp.int32, (16, TOK), 0) == 0
    kv = y[:, 512:768]
    zero = jnp.zeros((16, TOK), f32)
    for d in range(CHIPS):
        own = slice(OWN * d, OWN * (d + 1))
        out_ref[d, 0:OWN, :] = y[own, 0:256].astype(bf16)
        out_ref[d, OWN : 2 * OWN, :] = y[own, 256:512].astype(bf16)
        begin = OWN * d - HALO
        for r in range(0, WINDOW, 16):
            t = begin + r
            block = kv[t : t + 16] if t >= 0 else zero
            if r == 0:
                block = jnp.where(first, squares, block)
            out_ref[d, 2 * OWN + r : 2 * OWN + r + 16, :] = block.astype(bf16)


def attend_kernel(place_ref, recv_ref, cos_ref, sin_ref, mask_ref, out_ref):
    total = recv_ref[0].astype(f32)
    for d in range(1, CHIPS):
        total = total + recv_ref[d].astype(f32)
    squares = total[2 * OWN : 2 * OWN + 1, :]
    inverse_row = lax.rsqrt(squares * (1.0 / WIDTH) + EPSILON)
    token = lax.broadcasted_iota(jnp.int32, (WINDOW, TOK), 0) + (place_ref[0] * OWN - HALO)
    lane = lax.broadcasted_iota(jnp.int32, (WINDOW, TOK), 1)
    inverse = jnp.sum(jnp.where(token == lane, inverse_row, 0.0), axis=1, keepdims=True)
    cosine = cos_ref[...]
    sine = sin_ref[...]

    def rope(v, c, s):
        return (v * c + pltpu.roll(v, HEAD // 2, 1) * s).astype(bf16)

    scaled = total[2 * OWN :, :] * inverse
    keys = rope(scaled[:, :HEAD], cosine, sine)
    values = scaled[:, HEAD:].astype(bf16)
    own_inverse = inverse[HALO:]
    queries = []
    for h in range(4):
        rows = slice((h // 2) * OWN, (h // 2 + 1) * OWN)
        lanes = slice((h % 2) * HEAD, (h % 2 + 1) * HEAD)
        queries.append(rope(total[rows, lanes] * own_inverse, cosine[HALO:], sine[HALO:]))
    queries = jnp.concatenate(queries, axis=0)
    scores = lax.dot_general(queries, keys, (((1,), (1,)), ((), ())), preferred_element_type=f32)
    raised = jnp.where(mask_ref[...] > 0.0, jnp.exp(scores * (HEAD**-0.5)), 0.0)
    weights = (raised / jnp.sum(raised, axis=1, keepdims=True)).astype(bf16)
    mixed = jnp.dot(weights, values, preferred_element_type=f32).astype(bf16)
    for d in range(CHIPS):
        for h in range(4):
            out_ref[d, :, h * HEAD : (h + 1) * HEAD] = mixed[h * OWN : (h + 1) * OWN]


def out_kernel(mixed_ref, near_ref, far_ref, out_ref):
    mixed = mixed_ref[...]
    half = near_ref.shape[1]
    out_ref[:, :half] = jnp.dot(mixed, near_ref[...], preferred_element_type=f32).astype(bf16)
    out_ref[:, half:] = jnp.dot(mixed, far_ref[...], preferred_element_type=f32).astype(bf16)


def sum_kernel(recv_ref, held_ref, out_ref, own_ref):
    total = held_ref[...].astype(f32)
    for d in range(GRID):
        total = total + recv_ref[d].astype(f32)
    own = total.astype(bf16)
    own_ref[...] = own
    for d in range(GRID):
        out_ref[d] = own


def segment_info(lengths_row, total):
    token_ids = jnp.arange(total, dtype=jnp.int32)
    ends = jnp.cumsum(lengths_row)
    after = (token_ids[:, None] >= ends[None, :]).astype(jnp.int32)
    seg_ids = jnp.sum(after, axis=1)
    starts = jnp.sum(after * lengths_row[None, :], axis=1)
    return (seg_ids, token_ids - starts)


def swap(value):
    return lax.ppermute(value, "core", [(0, 1), (1, 0)])


def exchange(value, axis):
    return lax.all_to_all(value, axis, 0, 0, tiled=True)


def local(hidden_in, lengths, gain, w_query, w_pair, w_out):
    section = lax.axis_index("section")
    place = lax.axis_index("z")
    core = lax.axis_index("core")
    grid_place = section * 4 + lax.axis_index("row")

    queries_w = w_query[0].reshape(512, 4, 512).transpose(1, 0, 2)
    pairs_w = jnp.repeat(w_pair[0].reshape(512, 2, 256).transpose(1, 0, 2), 2, axis=0)
    send_in = jnp.concatenate([queries_w, pairs_w], axis=2).astype(f32) * gain[0][None, :, None]
    near_in = exchange(send_in.astype(bf16), "section")
    far_in = swap(near_in)
    near_out = exchange(w_out[0].reshape(4, 512, 512), "section")
    far_out = swap(near_out)

    mine = lax.dynamic_index_in_dim(hidden_in, core, 0, keepdims=False)
    theirs = lax.dynamic_index_in_dim(hidden_in, 1 - core, 0, keepdims=False)
    x = jnp.concatenate([mine, swap(theirs)], axis=1)
    held = lax.dynamic_slice_in_dim(x, grid_place * PART, PART, 0)

    seg, pos = segment_info(lax.dynamic_index_in_dim(lengths, core, 0, keepdims=False), TOK)
    seg_window = lax.dynamic_slice_in_dim(jnp.pad(seg, (HALO, 0), constant_values=-1), place * OWN, WINDOW)
    pos_window = lax.dynamic_slice_in_dim(jnp.pad(pos, (HALO, 0)), place * OWN, WINDOW)
    exponent = jnp.arange(HEAD // 2, dtype=f32) * (2.0 / HEAD)
    freqs = jnp.power(f32(ROPE_BASE), -exponent)
    angles = pos_window.astype(f32)[:, None] * freqs[None, :]
    cosine = jnp.cos(angles)
    sine = jnp.sin(angles)
    cosine = jnp.concatenate([cosine, cosine], axis=1)
    sine = jnp.concatenate([-sine, sine], axis=1)
    allowed = (seg_window[HALO:, None] == seg_window[None, :]) & (pos_window[None, :] <= pos_window[HALO:, None])
    mask = jnp.tile(allowed.astype(f32), (4, 1))
    place_arg = place.reshape(1).astype(jnp.int32)

    def attend(recv):
        return pl.pallas_call(
            attend_kernel,
            out_shape=jax.ShapeDtypeStruct((CHIPS, OWN, 512), bf16),
            in_specs=[pl.BlockSpec(memory_space=pltpu.SMEM)] + [VMEM] * 4,
            out_specs=VMEM,
            compiler_params=PARAMS,
            cost_estimate=pl.CostEstimate(flops=10_000_000, bytes_accessed=1_000_000, transcendentals=20_000),
        )(place_arg, recv, cosine, sine, mask)

    states = []
    for layer in range(LAYERS):
        packed = call(
            project_kernel,
            jax.ShapeDtypeStruct((CHIPS, PACK, 256), bf16),
            (x, near_in[layer], far_in[layer]),
            2 * 256 * 1024 * 1024,
        )
        mixed = exchange(attend(exchange(packed, "z")), "z").reshape(TOK, 512)
        branch = call(
            out_kernel,
            jax.ShapeDtypeStruct((TOK, 1024), bf16),
            (mixed, near_out[layer], far_out[layer]),
            2 * 256 * 512 * 1024,
        )
        copies, held = call(
            sum_kernel,
            (jax.ShapeDtypeStruct((GRID, PART, 1024), bf16), jax.ShapeDtypeStruct((PART, 1024), bf16)),
            (exchange(branch.reshape(GRID, PART, 1024), ("section", "row")), held),
            256 * 1024,
        )
        x = exchange(copies, ("section", "row")).reshape(TOK, 1024)
        states.append(x)

    kept = states[0]
    for layer in range(1, LAYERS):
        kept = jnp.where(section == layer, states[layer], kept)
    ours = kept[:, :512]
    other = swap(kept[:, 512:])
    final = jnp.where(core == 0, jnp.stack([ours, other]), jnp.stack([other, ours]))
    return final[None]


def solution(mesh):
    split = Mesh(mesh.devices.reshape(4, 4, 8, 2), ("section", "row", "z", "core"))
    col = ("z", "core")
    in_specs = (
        P(None, None, col),
        P(),
        P("section", col),
        P("section", col, "row"),
        P("section", col, "row"),
        P("section", "row", col),
    )
    out_specs = P("section", None, None, col)
    return jax.shard_map(local, mesh=split, in_specs=in_specs, out_specs=out_specs, check_vma=False)
```

time: 1390 us -> 366 us (0.26)
  waiting for transfers between devices: 1150 us -> 72.4 us
  blocking collectives: 135 us -> 205 us
  matrix products: 40.7 us -> 0 us
  starting transfers between devices: 15.3 us -> 47.1 us
  other arithmetic: 31.7 us -> 3.53 us
  local copies, waits for them, and re-layouts: 5.17 us -> 24.1 us
    psum x10 -> x0, waiting for transfers between devices: 645 us -> none  [the longest x5 421 us: layer(): pair_sum, square_sum = lax.psum((pair_part, squares), 'col')]
    reduce_scatter x5 -> x0, waiting for transfers between devices: 284 us -> none  [layer(): lax.psum_scatter(query_part, 'col', scatter_dimension=1, tiled=True)]
    all_to_all x0 -> x13, blocking collectives: none -> 205 us  [exchange(): return lax.all_to_all(value, axis, 0, 0, tiled=True)]
    all_gather x5 -> x0, waiting for transfers between devices: 202 us -> none  [layer(): lax.all_gather(mixed, 'col', axis=1, tiled=True)]
    psum x5 -> x0, blocking collectives: 135 us -> none  [layer(): pair_sum, square_sum = lax.psum((pair_part, squares), 'col')]
    all_to_all x0 -> x5, waiting for transfers between devices: none -> 70.1 us  [exchange(): return lax.all_to_all(value, axis, 0, 0, tiled=True)]
    dot_general x25 -> x0, matrix products: 40.7 us -> none  [the longest x5 13.7 us: layer(): jnp.dot(lax.all_gather(mixed, 'col', axis=1, tiled=True), out_w, preferre...]
    all_to_all x0 -> x5, starting transfers between devices: none -> 25.2 us  [exchange(): return lax.all_to_all(value, axis, 0, 0, tiled=True)]
  transfers between devices with their start and end apart: 25 -> 9, of which waited for: 25 -> 7; matrix products, arithmetic and copies ran while one was open for 2% -> 4% of each run, Pallas kernels for 0% -> 1%
where the time goes in v1:
time: 366 us; the launch traced here: 365 us
  blocking collectives  205 us (56%)
  waiting for transfers between devices  72.4 us (20%)
  starting transfers between devices  47.1 us (13%)
  local copies, waits for them, and re-layouts  24.1 us (7%)
  Pallas kernels  12.4 us (3%)
    all_to_all x13, blocking collectives, exchange(): return lax.all_to_all(value, axis, 0, 0, tiled=True)  205 us
    all_to_all x5, waiting for transfers between devices, exchange(): return lax.all_to_all(value, axis, 0, 0, tiled=True)  70.1 us
    all_to_all x5, starting transfers between devices, exchange(): return lax.all_to_all(value, axis, 0, 0, tiled=True)  25.2 us
    ppermute x4, starting transfers between devices, swap(): return lax.ppermute(value, 'core', [(0, 1), (1, 0)])  21.9 us
    pallas_call x12, Pallas kernels, call(): pl.pallas_call(kernel, out_shape=outs, in_specs=[VMEM] * len(args), out_s...  8.41 us
    unnamed x37, local copies, waits for them, and re-layouts  7.56 us
  transfers between devices with their start and end apart: 9, of which 7 were waited for; matrix products, arithmetic and copies ran while one was open for 4% of the time, Pallas kernels for 1%

profile of v1, /device:TPU:1, one launch (start us, length us, event | category | flops | bytes accessed | tf_op | source)
XLA Modules:
  0.0 364.6 jit_solution(13975009660602293074)
XLA Ops:
  3.9 4.2 %copy.14 = bf16[512,4,512]{2,0,1:T(8,128)(2,1)} copy(bf16[512,4,512]{0,2,1:T(8,128)(2,1)} %bitcast.81) | data formatting | bytes 4194304 | tf_op jit(solution)/shard_map/reshape;squeeze | solution.py:141
  10.6 40.5 %all_to_all.90 = bf16[4,512,768]{2,1,0:T(8,128)(2,1)} all-to-all(bf16[4,512,768]{2,1,0:T(8,128)(2,1)S(1)} %multiply_convert_fusion), channel_id=1, replica_groups=mesh['section'=4,'row'=4,'z'=8,'core'=2] {'section'}, dimensions={0} | all-to-all | bytes 6291456 | tf_op jit(solution)/shard_map/all_to_all | solution.py:132
  53.9 4.5 %all-to-all-start.3 = ((bf16[4,512,512]{2,1,0:T(8,128)(2,1)}), bf16[4,512,512]{2,1,0:T(8,128)(2,1)}, u32[]{:S(2)}, u32[]{:S(2)}) async-start(bf16[4,512,512]{2,1,0:T(8,128)(2,1)} %bitcast.83), calls=%async_computation.3 | async-start | bytes 4194304 | tf_op jit(solution)/shard_map/all_to_all | solution.py:132
  60.2 24.6 %all-to-all-done.3 = bf16[4,512,512]{2,1,0:T(8,128)(2,1)} async-done(((bf16[4,512,512]{2,1,0:T(8,128)(2,1)}), bf16[4,512,512]{2,1,0:T(8,128)(2,1)}, u32[]{:S(2)}, u32[]{:S(2)}) %all-to-all-start.3) | async-done | bytes 2097184 | tf_op jit(solution)/shard_map/all_to_all | solution.py:132
  93.5 8.2 %all-to-all-start.1 = ((bf16[8,160,256]{2,1,0:T(8,128)(2,1)}), bf16[8,160,256]{2,1,0:T(8,128)(2,1)}, u32[]{:S(2)}, u32[]{:S(2)}) async-start(bf16[8,160,256]{2,1,0:T(8,128)(2,1)} %shard_map.64), calls=%async_computation.1 | async-start | bytes 1310720 | tf_op jit(solution)/shard_map/all_to_all | solution.py:132
  102.5 20.0 %all-to-all-done.1.recv_ref = bf16[8,160,256]{2,1,0:T(8,128)(2,1)} async-done(((bf16[8,160,256]{2,1,0:T(8,128)(2,1)}), bf16[8,160,256]{2,1,0:T(8,128)(2,1)}, u32[]{:S(2)}, u32[]{:S(2)}) %all-to-all-start.1) | async-done | bytes 655392 | tf_op jit(solution)/shard_map/all_to_all | solution.py:132
  124.9 4.1 %all-to-all-start.2 = ((bf16[8,32,512]{2,1,0:T(8,128)(2,1)}), bf16[8,32,512]{2,1,0:T(8,128)(2,1)}, u32[]{:S(2)}, u32[]{:S(2)}) async-start(bf16[8,32,512]{2,1,0:T(8,128)(2,1)} %shard_map.65), calls=%async_computation.2 | async-start | bytes 524288 | tf_op jit(solution)/shard_map/all_to_all | solution.py:132
  134.5 6.7 %all-to-all-done.2 = bf16[8,32,512]{2,1,0:T(8,128)(2,1)} async-done(((bf16[8,32,512]{2,1,0:T(8,128)(2,1)}), bf16[8,32,512]{2,1,0:T(8,128)(2,1)}, u32[]{:S(2)}, u32[]{:S(2)}) %all-to-all-start.2) | async-done | bytes 262176 | tf_op jit(solution)/shard_map/all_to_all | solution.py:132
  144.4 4.9 %all-to-all-start.4 = ((bf16[16,16,1024]{2,1,0:T(8,128)(2,1)}), bf16[16,16,1024]{2,1,0:T(8,128)(2,1)S(1)}, u32[]{:S(2)}, u32[]{:S(2)}) async-start(bf16[16,16,1024]{2,1,0:T(8,128)(2,1)} %bitcast.17), calls=%async_computation.4 | async-start | bytes 1048576 | tf_op jit(solution)/shard_map/all_to_all | solution.py:132
  150.1 9.6 %all-to-all-done.4.recv_ref = bf16[16,16,1024]{2,1,0:T(8,128)(2,1)S(1)} async-done(((bf16[16,16,1024]{2,1,0:T(8,128)(2,1)}), bf16[16,16,1024]{2,1,0:T(8,128)(2,1)S(1)}, u32[]{:S(2)}, u32[]{:S(2)}) %all-to-all-start.4) | async-done | bytes 524320 | tf_op jit(solution)/shard_map/all_to_all | solution.py:132
  159.8 12.8 %all_to_all.91 = bf16[16,16,1024]{2,1,0:T(8,128)(2,1)S(1)} all-to-all(bf16[16,16,1024]{2,1,0:T(8,128)(2,1)S(1)} %get-tuple-element.12), channel_id=1, replica_groups=mesh['section'=4,'row'=4,'z'=8,'core'=2] {'section','row'}, dimensions={0} | all-to-all | bytes 1048576 | tf_op jit(solution)/shard_map/all_to_all | solution.py:132
  174.4 19.1 %all_to_all.92.recv_ref = bf16[8,160,256]{2,1,0:T(8,128)(2,1)S(1)} all-to-all(bf16[8,160,256]{2,1,0:T(8,128)(2,1)S(1)} %shard_map.68), channel_id=1, replica_groups=mesh['section'=4,'row'=4,'z'=8,'core'=2] {'z'}, dimensions={0} | all-to-all | bytes 1310720 | tf_op jit(solution)/shard_map/all_to_all | solution.py:132
  194.1 12.2 %all_to_all.93 = bf16[8,32,512]{2,1,0:T(8,128)(2,1)S(1)} all-to-all(bf16[8,32,512]{2,1,0:T(8,128)(2,1)S(1)} %shard_map.69), channel_id=1, replica_groups=mesh['section'=4,'row'=4,'z'=8,'core'=2] {'z'}, dimensions={0} | all-to-all | bytes 524288 | tf_op jit(solution)/shard_map/all_to_all | solution.py:132
  206.7 12.2 %all_to_all.94.recv_ref = bf16[16,16,1024]{2,1,0:T(8,128)(2,1)S(1)} all-to-all(bf16[16,16,1024]{2,1,0:T(8,128)(2,1)S(1)} %bitcast.70), channel_id=1, replica_groups=mesh['section'=4,'row'=4,'z'=8,'core'=2] {'section','row'}, dimensions={0} | all-to-all | bytes 1048576 | tf_op jit(solution)/shard_map/all_to_all | solution.py:132
  219.0 12.0 %all_to_all.95 = bf16[16,16,1024]{2,1,0:T(8,128)(2,1)S(1)} all-to-all(bf16[16,16,1024]{2,1,0:T(8,128)(2,1)S(1)} %get-tuple-element.14), channel_id=1, replica_groups=mesh['section'=4,'row'=4,'z'=8,'core'=2] {'section','row'}, dimensions={0} | all-to-all | bytes 1048576 | tf_op jit(solution)/shard_map/all_to_all | solution.py:132
  231.8 16.1 %all_to_all.96.recv_ref = bf16[8,160,256]{2,1,0:T(8,128)(2,1)S(1)} all-to-all(bf16[8,160,256]{2,1,0:T(8,128)(2,1)S(1)} %shard_map.72), channel_id=1, replica_groups=mesh['section'=4,'row'=4,'z'=8,'core'=2] {'z'}, dimensions={0} | all-to-all | bytes 1310720 | tf_op jit(solution)/shard_map/all_to_all | solution.py:132
  248.5 11.7 %all_to_all.97 = bf16[8,32,512]{2,1,0:T(8,128)(2,1)S(1)} all-to-all(bf16[8,32,512]{2,1,0:T(8,128)(2,1)S(1)} %shard_map.73), channel_id=1, replica_groups=mesh['section'=4,'row'=4,'z'=8,'core'=2] {'z'}, dimensions={0} | all-to-all | bytes 524288 | tf_op jit(solution)/shard_map/all_to_all | solution.py:132
  260.7 11.9 %all_to_all.98.recv_ref = bf16[16,16,1024]{2,1,0:T(8,128)(2,1)S(1)} all-to-all(bf16[16,16,1024]{2,1,0:T(8,128)(2,1)S(1)} %bitcast.71), channel_id=1, replica_groups=mesh['section'=4,'row'=4,'z'=8,'core'=2] {'section','row'}, dimensions={0} | all-to-all | bytes 1048576 | tf_op jit(solution)/shard_map/all_to_all | solution.py:132
  272.7 13.8 %all_to_all.99 = bf16[16,16,1024]{2,1,0:T(8,128)(2,1)S(1)} all-to-all(bf16[16,16,1024]{2,1,0:T(8,128)(2,1)S(1)} %get-tuple-element.16), channel_id=1, replica_groups=mesh['section'=4,'row'=4,'z'=8,'core'=2] {'section','row'}, dimensions={0} | all-to-all | bytes 1048576 | tf_op jit(solution)/shard_map/all_to_all | solution.py:132
  287.2 15.9 %all_to_all.100.recv_ref = bf16[8,160,256]{2,1,0:T(8,128)(2,1)S(1)} all-to-all(bf16[8,160,256]{2,1,0:T(8,128)(2,1)S(1)} %shard_map.76), channel_id=1, replica_groups=mesh['section'=4,'row'=4,'z'=8,'core'=2] {'z'}, dimensions={0} | all-to-all | bytes 1310720 | tf_op jit(solution)/shard_map/all_to_all | solution.py:132
  303.7 14.5 %all_to_all.101 = bf16[8,32,512]{2,1,0:T(8,128)(2,1)S(1)} all-to-all(bf16[8,32,512]{2,1,0:T(8,128)(2,1)S(1)} %shard_map.77), channel_id=1, replica_groups=mesh['section'=4,'row'=4,'z'=8,'core'=2] {'z'}, dimensions={0} | all-to-all | bytes 524288 | tf_op jit(solution)/shard_map/all_to_all | solution.py:132
  318.7 11.9 %all_to_all.102.recv_ref = bf16[16,16,1024]{2,1,0:T(8,128)(2,1)S(1)} all-to-all(bf16[16,16,1024]{2,1,0:T(8,128)(2,1)S(1)} %bitcast.72), channel_id=1, replica_groups=mesh['section'=4,'row'=4,'z'=8,'core'=2] {'section','row'}, dimensions={0} | all-to-all | bytes 1048576 | tf_op jit(solution)/shard_map/all_to_all | solution.py:132
  335.1 9.2 %all-to-all-done.17 = bf16[16,16,1024]{2,1,0:T(8,128)(2,1)S(1)} async-done(((bf16[16,16,1024]{2,1,0:T(8,128)(2,1)}), bf16[16,16,1024]{2,1,0:T(8,128)(2,1)S(1)}, u32[]{:S(2)}, u32[]{:S(2)}) %all-to-all-start.17) | async-done | bytes 524320 | tf_op jit(solution)/shard_map/all_to_all | solution.py:132
  344.6 18.0 %collective-permute-start.3 = (bf16[256,512]{1,0:T(8,128)(2,1)S(1)}, bf16[256,512]{1,0:T(8,128)(2,1)S(1)}, u32[]{:S(2)}, u32[]{:S(2)}) collective-permute-start(bf16[256,512]{1,0:T(8,128)(2,1)S(1)} %get-tuple-element.40), channel_id=1, source_target_pairs={{0,1},{1,0},{2,3},{3,2},{4,5},{5,4},{6,7},{7,6},{8,9},{9,8},{10,11... | collective-permute-start | bytes 786440 | tf_op jit(solution)/shard_map/ppermute | solution.py:128
  (90 shorter events, 45.6 us)
Async XLA Ops:
  3.9 4.2 %copy-start.15 = (bf16[1,512,512]{2,1,0:T(8,128)(2,1)S(1)}, bf16[1,512,512]{2,1,0:T(8,128)(2,1)}, u32[]{:S(2)}) copy-start(bf16[1,512,512]{2,1,0:T(8,128)(2,1)} %param.10) | copy-start | bytes 1572868
  3.9 4.5 %copy-start.16 = (f32[1,512]{1,0:T(1,128)S(1)}, f32[1,512]{1,0:T(1,128)}, u32[]{:S(2)}) copy-start(f32[1,512]{1,0:T(1,128)} %param.8) | copy-start | bytes 6148
  51.1 7.3 %copy-start.14 = (bf16[2,256,512]{2,1,0:T(8,128)(2,1)S(1)}, bf16[2,256,512]{2,1,0:T(8,128)(2,1)}, u32[]{:S(2)}) copy-start(bf16[2,256,512]{2,1,0:T(8,128)(2,1)} %param.6) | copy-start | bytes 1572868
  51.1 7.6 %copy-start.17 = (s32[2,32]{1,0:T(2,128)S(1)}, s32[2,32]{1,0:T(2,128)}, u32[]{:S(2)}) copy-start(s32[2,32]{1,0:T(2,128)} %param.7) | copy-start | bytes 772
  51.1 37.5 %collective-permute-start.1 = (bf16[4,512,768]{2,1,0:T(8,128)(2,1)}, bf16[4,512,768]{2,1,0:T(8,128)(2,1)}, u32[]{:S(2)}, u32[]{:S(2)}) collective-permute-start(bf16[4,512,768]{2,1,0:T(8,128)(2,1)} %all_to_all.90), channel_id=1, source_target_pairs={{0,1},{1,0},{2,3},{3,2},{4,5},{5,4},{6,7},{7,6},{8,9},{9,8},{10,11... | collective-permute-start | bytes 9437192 | tf_op jit(solution)/shard_map/ppermute | solution.py:128
  53.9 30.9 %all-to-all-start.3 = ((bf16[4,512,512]{2,1,0:T(8,128)(2,1)}), bf16[4,512,512]{2,1,0:T(8,128)(2,1)}, u32[]{:S(2)}, u32[]{:S(2)}) async-start(bf16[4,512,512]{2,1,0:T(8,128)(2,1)} %bitcast.83), calls=%async_computation.3 | async-start | bytes 4194304 | tf_op jit(solution)/shard_map/all_to_all | solution.py:132
  58.5 26.3 %copy-start.12 = (bf16[256,512]{1,0:T(8,128)(2,1)}, bf16[256,512]{1,0:T(8,128)(2,1)S(1)}, u32[]{:S(2)}) copy-start(bf16[256,512]{1,0:T(8,128)(2,1)S(1)} %get-tuple-element.41) | copy-start | bytes 786436
  58.5 1.6 collective-permute-start
  60.1 24.7 %copy-start.13 = (bf16[256,512]{1,0:T(8,128)(2,1)}, bf16[256,512]{1,0:T(8,128)(2,1)S(1)}, u32[]{:S(2)}) copy-start(bf16[256,512]{1,0:T(8,128)(2,1)S(1)} %collective-permute-done) | copy-start | bytes 786436
  84.8 46.8 %collective-permute-start.2 = (bf16[4,512,512]{2,1,0:T(8,128)(2,1)}, bf16[4,512,512]{2,1,0:T(8,128)(2,1)}, u32[]{:S(2)}, u32[]{:S(2)}) collective-permute-start(bf16[4,512,512]{2,1,0:T(8,128)(2,1)} %all-to-all-done.3), channel_id=1, source_target_pairs={{0,1},{1,0},{2,3},{3,2},{4,5},{5,4},{6,7},{7,6},{8,9},{9,8},{10,11... | collective-permute-start | bytes 6291464 | tf_op jit(solution)/shard_map/ppermute | solution.py:128
  93.5 29.1 %all-to-all-start.1 = ((bf16[8,160,256]{2,1,0:T(8,128)(2,1)}), bf16[8,160,256]{2,1,0:T(8,128)(2,1)}, u32[]{:S(2)}, u32[]{:S(2)}) async-start(bf16[8,160,256]{2,1,0:T(8,128)(2,1)} %shard_map.64), calls=%async_computation.1 | async-start | bytes 1310720 | tf_op jit(solution)/shard_map/all_to_all | solution.py:132
  102.4 22.5 %copy-start.9 = (f32[96,128]{1,0:T(8,128)}, f32[96,128]{1,0:T(8,128)S(1)}, u32[]{:S(2)}) copy-start(f32[96,128]{1,0:T(8,128)S(1)} %pad_maximum_fusion.2.sin_ref) | copy-start | bytes 147460
  124.9 16.3 %all-to-all-start.2 = ((bf16[8,32,512]{2,1,0:T(8,128)(2,1)}), bf16[8,32,512]{2,1,0:T(8,128)(2,1)}, u32[]{:S(2)}, u32[]{:S(2)}) async-start(bf16[8,32,512]{2,1,0:T(8,128)(2,1)} %shard_map.65), calls=%async_computation.2 | async-start | bytes 524288 | tf_op jit(solution)/shard_map/all_to_all | solution.py:132
  144.4 15.2 %all-to-all-start.4 = ((bf16[16,16,1024]{2,1,0:T(8,128)(2,1)}), bf16[16,16,1024]{2,1,0:T(8,128)(2,1)S(1)}, u32[]{:S(2)}, u32[]{:S(2)}) async-start(bf16[16,16,1024]{2,1,0:T(8,128)(2,1)} %bitcast.17), calls=%async_computation.4 | async-start | bytes 1048576 | tf_op jit(solution)/shard_map/all_to_all | solution.py:132
  159.7 33.9 %copy-start.10 = (f32[96,128]{1,0:T(8,128)S(1)}, f32[96,128]{1,0:T(8,128)}, u32[]{:S(2)}) copy-start(f32[96,128]{1,0:T(8,128)} %copy-done.9) | copy-start | bytes 147460
  159.8 46.5 %copy-start.6 = (bf16[512,512]{1,0:T(8,128)(2,1)S(1)}, bf16[512,512]{1,0:T(8,128)(2,1)}, u32[]{:S(2)}) copy-start(bf16[512,512]{1,0:T(8,128)(2,1)} %get-tuple-element.37.near_ref) | copy-start | bytes 1572868
  159.8 46.5 %copy-start.7 = (bf16[512,512]{1,0:T(8,128)(2,1)S(1)}, bf16[512,512]{1,0:T(8,128)(2,1)}, u32[]{:S(2)}) copy-start(bf16[512,512]{1,0:T(8,128)(2,1)} %get-tuple-element.33.far_ref) | copy-start | bytes 1572868
  193.5 37.5 %copy-start = (bf16[512,768]{1,0:T(8,128)(2,1)S(1)}, bf16[512,768]{1,0:T(8,128)(2,1)}, u32[]{:S(2)}) copy-start(bf16[512,768]{1,0:T(8,128)(2,1)} %get-tuple-element.28.near_ref) | copy-start | bytes 2359300
  193.5 37.5 %copy-start.1 = (bf16[512,768]{1,0:T(8,128)(2,1)S(1)}, bf16[512,768]{1,0:T(8,128)(2,1)}, u32[]{:S(2)}) copy-start(bf16[512,768]{1,0:T(8,128)(2,1)} %get-tuple-element.24.far_ref) | copy-start | bytes 2359300
  219.0 41.2 %copy-start.5 = (bf16[512,512]{1,0:T(8,128)(2,1)S(1)}, bf16[512,512]{1,0:T(8,128)(2,1)}, u32[]{:S(2)}) copy-start(bf16[512,512]{1,0:T(8,128)(2,1)} %get-tuple-element.32.far_ref) | copy-start | bytes 1572868
  272.7 45.6 %copy-start.3 = (bf16[512,512]{1,0:T(8,128)(2,1)S(1)}, bf16[512,512]{1,0:T(8,128)(2,1)}, u32[]{:S(2)}) copy-start(bf16[512,512]{1,0:T(8,128)(2,1)} %get-tuple-element.35.near_ref) | copy-start | bytes 1572868
  272.7 45.6 %copy-start.4 = (bf16[512,512]{1,0:T(8,128)(2,1)S(1)}, bf16[512,512]{1,0:T(8,128)(2,1)}, u32[]{:S(2)}) copy-start(bf16[512,512]{1,0:T(8,128)(2,1)} %get-tuple-element.31.far_ref) | copy-start | bytes 1572868
  331.5 12.8 %all-to-all-start.17 = ((bf16[16,16,1024]{2,1,0:T(8,128)(2,1)}), bf16[16,16,1024]{2,1,0:T(8,128)(2,1)S(1)}, u32[]{:S(2)}, u32[]{:S(2)}) async-start(bf16[16,16,1024]{2,1,0:T(8,128)(2,1)} %get-tuple-element.18), calls=%async_computation.17 | async-start | bytes 1048576 | tf_op jit(solution)/shard_map/all_to_all | solution.py:132
  344.6 19.1 %collective-permute-start.3 = (bf16[256,512]{1,0:T(8,128)(2,1)S(1)}, bf16[256,512]{1,0:T(8,128)(2,1)S(1)}, u32[]{:S(2)}, u32[]{:S(2)}) collective-permute-start(bf16[256,512]{1,0:T(8,128)(2,1)S(1)} %get-tuple-element.40), channel_id=1, source_target_pairs={{0,1},{1,0},{2,3},{3,2},{4,5},{5,4},{6,7},{7,6},{8,9},{9,8},{10,11... | collective-permute-start | bytes 786440 | tf_op jit(solution)/shard_map/ppermute | solution.py:128
  (3 other events, 3.8 us)

commit v2 on v1

--- a/solution.py
+++ b/solution.py
@@ -115,6 +115,60 @@
         out_ref[d] = own
 
 
+def weigh_kernel(dest_ref, query_ref, pair_ref, gain_ref, out_ref):
+    rows = lax.broadcasted_iota(jnp.int32, (128, 128), 0)
+    cols = lax.broadcasted_iota(jnp.int32, (128, 128), 1)
+    scale = jnp.sum(jnp.where(rows == cols, gain_ref[...], 0.0), axis=1, keepdims=True)
+    out_ref[:, :512] = (query_ref[0].astype(f32) * scale).astype(bf16)
+    out_ref[:, 512:] = (pair_ref[0].astype(f32) * scale).astype(bf16)
+
+
+def weigh(w_query, w_pair, gain, dest):
+    return pl.pallas_call(
+        weigh_kernel,
+        out_shape=jax.ShapeDtypeStruct((512, 768), bf16),
+        grid_spec=pltpu.PrefetchScalarGridSpec(
+            num_scalar_prefetch=1,
+            grid=(4,),
+            in_specs=[
+                pl.BlockSpec((1, 128, 512), lambda i, d: (0, i, d[0])),
+                pl.BlockSpec((1, 128, 256), lambda i, d: (0, i, d[0] // 2)),
+                pl.BlockSpec((1, 128), lambda i, d: (0, i)),
+            ],
+            out_specs=pl.BlockSpec((128, 768), lambda i, d: (i, 0)),
+        ),
+        compiler_params=PARAMS,
+        cost_estimate=pl.CostEstimate(flops=1_000_000, bytes_accessed=1_600_000, transcendentals=0),
+    )(dest.reshape(1).astype(jnp.int32), w_query, w_pair, gain)
+
+
+def pick_kernel(index_ref, *refs):
+    *sources, out_ref, sem = refs
+    for i, source in enumerate(sources):
+
+        @pl.when(index_ref[0] == i)
+        def _():
+            copy = pltpu.make_async_copy(source, out_ref, sem)
+            copy.start()
+            copy.wait()
+
+
+def pick(arrays, index):
+    return pl.pallas_call(
+        pick_kernel,
+        out_shape=jax.ShapeDtypeStruct(arrays[0].shape, arrays[0].dtype),
+        in_specs=[pl.BlockSpec(memory_space=pltpu.SMEM)] + [pl.BlockSpec(memory_space=pl.ANY)] * len(arrays),
+        out_specs=pl.BlockSpec(memory_space=pl.ANY),
+        scratch_shapes=[pltpu.SemaphoreType.DMA],
+        compiler_params=PARAMS,
+        cost_estimate=pl.CostEstimate(flops=0, bytes_accessed=1_500_000, transcendentals=0),
+    )(index.reshape(1).astype(jnp.int32), *arrays)
+
+
+def rotated(value, steps, first):
+    return lax.ppermute(value, "section", [(s, (s + steps) % 4) for s in range(first, 4)])
+
+
 def segment_info(lengths_row, total):
     token_ids = jnp.arange(total, dtype=jnp.int32)
     ends = jnp.cumsum(lengths_row)
@@ -138,13 +192,14 @@
     core = lax.axis_index("core")
     grid_place = section * 4 + lax.axis_index("row")
 
-    queries_w = w_query[0].reshape(512, 4, 512).transpose(1, 0, 2)
-    pairs_w = jnp.repeat(w_pair[0].reshape(512, 2, 256).transpose(1, 0, 2), 2, axis=0)
-    send_in = jnp.concatenate([queries_w, pairs_w], axis=2).astype(f32) * gain[0][None, :, None]
-    near_in = exchange(send_in.astype(bf16), "section")
+    blocks_in = [weigh(w_query, w_pair, gain, (section + k) % 4) for k in range(4)]
+    blocks_out = [lax.dynamic_slice(w_out, (0, 512 * ((section + k) % 4), 0), (1, 512, 512))[0] for k in range(4)]
+    first_in = [blocks_in[0]] + [lax.ppermute(blocks_in[k], "section", [(0, k)]) for k in range(1, 4)]
+    near_in = pick(first_in, section)
     far_in = swap(near_in)
-    near_out = exchange(w_out[0].reshape(4, 512, 512), "section")
-    far_out = swap(near_out)
+    turn = [(section - layer) % 4 for layer in range(LAYERS)]
+    ready, *blocks_out = lax.optimization_barrier((near_in, *blocks_out))
+    moved_out = [blocks_out[0]] + [rotated(blocks_out[k], k, 0) for k in range(1, 4)]
 
     mine = lax.dynamic_index_in_dim(hidden_in, core, 0, keepdims=False)
     theirs = lax.dynamic_index_in_dim(hidden_in, 1 - core, 0, keepdims=False)
@@ -177,17 +232,25 @@
 
     states = []
     for layer in range(LAYERS):
+        if layer > 0:
+            near_in = pick(moved_in, turn[layer])
+            far_in = swap(near_in)
         packed = call(
             project_kernel,
             jax.ShapeDtypeStruct((CHIPS, PACK, 256), bf16),
-            (x, near_in[layer], far_in[layer]),
+            (x, near_in, far_in),
             2 * 256 * 1024 * 1024,
         )
+        if layer == 0:
+            packed, *blocks_in = lax.optimization_barrier((packed, *blocks_in))
+            moved_in = [blocks_in[0]] + [rotated(blocks_in[k], k, 1) for k in range(1, 4)]
+        near_out = pick(moved_out, turn[layer])
+        far_out = swap(near_out)
         mixed = exchange(attend(exchange(packed, "z")), "z").reshape(TOK, 512)
         branch = call(
             out_kernel,
             jax.ShapeDtypeStruct((TOK, 1024), bf16),
-            (mixed, near_out[layer], far_out[layer]),
+            (mixed, near_out, far_out),
             2 * 256 * 512 * 1024,
         )
         copies, held = call(

time: 366 us -> 465 us (1.27)
  blocking collectives: 205 us -> 19.4 us
  waiting for transfers between devices: 72.4 us -> 173 us
  Pallas kernels: 12.4 us -> 109 us
  starting transfers between devices: 47.1 us -> 134 us
    all_to_all x13 -> x1, blocking collectives: 205 us -> 19.4 us  [exchange(): return lax.all_to_all(value, axis, 0, 0, tiled=True)]
    pallas_call x0 -> x12, Pallas kernels: none -> 84.2 us  [the longest x8 78.1 us: pick(): pl.pallas_call(pick_kernel, out_shape=jax.ShapeDtypeStruct(arrays[0].shap...]
    all_to_all x5 -> x15, starting transfers between devices: 25.2 us -> 95.8 us  [exchange(): return lax.all_to_all(value, axis, 0, 0, tiled=True)]
    all_to_all x5 -> x15, waiting for transfers between devices: 70.1 us -> 125 us  [exchange(): return lax.all_to_all(value, axis, 0, 0, tiled=True)]
    ppermute x0 -> x9, waiting for transfers between devices: none -> 45.2 us  [the longest x3 22.9 us: local(): lax.ppermute(blocks_in[k], 'section', [(0, k)])]
    ppermute x0 -> x9, starting transfers between devices: none -> 20.9 us  [the longest x6 10.8 us: rotated(): lax.ppermute(value, 'section', [(s, (s + steps) % 4) for s in range(first...]
    unnamed x37 -> x78, local copies, waits for them, and re-layouts: 7.56 us -> 17.8 us
    pallas_call x12, Pallas kernels: 8.41 us -> 18.6 us  [call(): pl.pallas_call(kernel, out_shape=outs, in_specs=[VMEM] * len(args), out_s...]
  transfers between devices with their start and end apart: 9 -> 34, of which waited for: 7 -> 18; matrix products, arithmetic and copies ran while one was open for 4% -> 1% of each run, Pallas kernels for 1% -> 20%
where the time goes in v2:
time: 465 us; the launch traced here: 462 us
  waiting for transfers between devices  173 us (37%)
  starting transfers between devices  134 us (29%)
  Pallas kernels  109 us (23%)
  local copies, waits for them, and re-layouts  20.9 us (4%)
  blocking collectives  19.4 us (4%)
  other arithmetic  4.96 us (1%)
    all_to_all x15, waiting for transfers between devices, exchange(): return lax.all_to_all(value, axis, 0, 0, tiled=True)  125 us
    all_to_all x15, starting transfers between devices, exchange(): return lax.all_to_all(value, axis, 0, 0, tiled=True)  95.8 us
    pallas_call x8, Pallas kernels, pick(): pl.pallas_call(pick_kernel, out_shape=jax.ShapeDtypeStruct(arrays[0].shap...  78.1 us
    ppermute x3, waiting for transfers between devices, local(): lax.ppermute(blocks_in[k], 'section', [(0, k)])  22.9 us
    ppermute x6, waiting for transfers between devices, rotated(): lax.ppermute(value, 'section', [(s, (s + steps) % 4) for s in range(first...  22.2 us
    all_to_all x1, blocking collectives, exchange(): return lax.all_to_all(value, axis, 0, 0, tiled=True)  19.4 us
    pallas_call x12, Pallas kernels, call(): pl.pallas_call(kernel, out_shape=outs, in_specs=[VMEM] * len(args), out_s...  18.6 us
    unnamed x78, local copies, waits for them, and re-layouts  17.8 us
  transfers between devices with their start and end apart: 34, of which 18 were waited for; matrix products, arithmetic and copies ran while one was open for 1% of the time, Pallas kernels for 20%

profile of v2, /device:TPU:1, one launch (start us, length us, event | category | flops | bytes accessed | tf_op | source)
XLA Modules:
  0.0 462.0 jit_solution(7345244562687864090)
XLA Ops:
  25.6 16.9 %collective-permute-done.2.refs_2_ = bf16[512,768]{1,0:T(8,128)(2,1)} collective-permute-done((bf16[512,768]{1,0:T(8,128)(2,1)}, bf16[512,768]{1,0:T(8,128)(2,1)}, u32[]{:S(2)}, u32[]{:S(2)}) %collective-permute-start.2) | collective-permute-done | bytes 786464 | tf_op jit(solution)/shard_map/ppermute | solution.py:197
  48.1 8.2 %all-to-all-start = ((bf16[8,160,256]{2,1,0:T(8,128)(2,1)}), bf16[8,160,256]{2,1,0:T(8,128)(2,1)S(1)}, u32[]{:S(2)}, u32[]{:S(2)}) async-start(bf16[8,160,256]{2,1,0:T(8,128)(2,1)} %shard_map.69), calls=%async_computation | async-start | bytes 1310720 | tf_op jit(solution)/shard_map/all_to_all | solution.py:186
  73.5 13.7 %collective-permute-done.6.refs_2_ = bf16[512,512]{1,0:T(8,128)(2,1)S(1)} collective-permute-done((bf16[512,512]{1,0:T(8,128)(2,1)S(1)}, bf16[512,512]{1,0:T(8,128)(2,1)S(1)}, u32[]{:S(2)}, u32[]{:S(2)}) %collective-permute-start.6) | collective-permute-done | bytes 524320 | tf_op jit(solution)/shard_map/ppermute | solution.py:169
  103.9 12.4 %all-to-all-done.1 = bf16[8,32,512]{2,1,0:T(8,128)(2,1)S(1)} async-done(((bf16[8,32,512]{2,1,0:T(8,128)(2,1)}), bf16[8,32,512]{2,1,0:T(8,128)(2,1)S(1)}, u32[]{:S(2)}, u32[]{:S(2)}) %all-to-all-start.1) | async-done | bytes 262176 | tf_op jit(solution)/shard_map/all_to_all | solution.py:186
  118.7 10.6 %all-to-all-start.2 = ((bf16[16,16,1024]{2,1,0:T(8,128)(2,1)}), bf16[16,16,1024]{2,1,0:T(8,128)(2,1)S(1)}, u32[]{:S(2)}, u32[]{:S(2)}) async-start(bf16[16,16,1024]{2,1,0:T(8,128)(2,1)} %bitcast.16), calls=%async_computation.2 | async-start | bytes 1048576 | tf_op jit(solution)/shard_map/all_to_all | solution.py:186
  131.8 24.9 %shard_map.74.near_ref = bf16[512,768]{1,0:T(8,128)(2,1)} custom-call(s32[1]{0:T(128)} %bitcast.18.index_ref, bf16[512,768]{1,0:T(8,128)(2,1)S(1)} %shard_map.64.refs_0_, bf16[512,768]{1,0:T(8,128)(2,1)} %collective-permute-done.9.refs_1_, bf16[512,768]{1,0:T(8,128)(2,1)} %collective-permute-done.10.refs_2_, bf16[512,768]{1,0:T(8,128)(2,1)} %collective-permute-done.11.refs_3_), custom_call_target="tpu_custom_call" | custom-call | bytes 1500000 | tf_op jit(solution)/shard_map/pallas_call | solution.py:157
  159.9 8.3 %all-to-all-start.3 = ((bf16[16,16,1024]{2,1,0:T(8,128)(2,1)}), bf16[16,16,1024]{2,1,0:T(8,128)(2,1)S(1)}, u32[]{:S(2)}, u32[]{:S(2)}) async-start(bf16[16,16,1024]{2,1,0:T(8,128)(2,1)} %copy-done.20), calls=%async_computation.3 | async-start | bytes 1048576 | tf_op jit(solution)/shard_map/all_to_all | solution.py:186
  168.2 10.1 %all-to-all-done.3 = bf16[16,16,1024]{2,1,0:T(8,128)(2,1)S(1)} async-done(((bf16[16,16,1024]{2,1,0:T(8,128)(2,1)}), bf16[16,16,1024]{2,1,0:T(8,128)(2,1)S(1)}, u32[]{:S(2)}, u32[]{:S(2)}) %all-to-all-start.3) | async-done | bytes 524320 | tf_op jit(solution)/shard_map/all_to_all | solution.py:186
  181.3 6.7 %all-to-all-start.4 = ((bf16[8,160,256]{2,1,0:T(8,128)(2,1)}), bf16[8,160,256]{2,1,0:T(8,128)(2,1)}, u32[]{:S(2)}, u32[]{:S(2)}) async-start(bf16[8,160,256]{2,1,0:T(8,128)(2,1)} %copy-done.5), calls=%async_computation.4 | async-start | bytes 1310720 | tf_op jit(solution)/shard_map/all_to_all | solution.py:186
  191.5 14.8 %all-to-all-done.4.recv_ref = bf16[8,160,256]{2,1,0:T(8,128)(2,1)} async-done(((bf16[8,160,256]{2,1,0:T(8,128)(2,1)}), bf16[8,160,256]{2,1,0:T(8,128)(2,1)}, u32[]{:S(2)}, u32[]{:S(2)}) %all-to-all-start.4) | async-done | bytes 655392 | tf_op jit(solution)/shard_map/all_to_all | solution.py:186
  213.5 9.4 %all-to-all-done.5 = bf16[8,32,512]{2,1,0:T(8,128)(2,1)} async-done(((bf16[8,32,512]{2,1,0:T(8,128)(2,1)}), bf16[8,32,512]{2,1,0:T(8,128)(2,1)}, u32[]{:S(2)}, u32[]{:S(2)}) %all-to-all-start.5) | async-done | bytes 262176 | tf_op jit(solution)/shard_map/all_to_all | solution.py:186
  225.4 9.1 %all-to-all-start.6 = ((bf16[16,16,1024]{2,1,0:T(8,128)(2,1)}), bf16[16,16,1024]{2,1,0:T(8,128)(2,1)}, u32[]{:S(2)}, u32[]{:S(2)}) async-start(bf16[16,16,1024]{2,1,0:T(8,128)(2,1)} %bitcast.48), calls=%async_computation.6 | async-start | bytes 1048576 | tf_op jit(solution)/shard_map/all_to_all | solution.py:186
  234.5 24.9 %shard_map.80.near_ref = bf16[512,768]{1,0:T(8,128)(2,1)} custom-call(s32[1]{0:T(128)} %bitcast.22.index_ref, bf16[512,768]{1,0:T(8,128)(2,1)S(1)} %shard_map.64.refs_0_, bf16[512,768]{1,0:T(8,128)(2,1)} %collective-permute-done.9.refs_1_, bf16[512,768]{1,0:T(8,128)(2,1)} %collective-permute-done.10.refs_2_, bf16[512,768]{1,0:T(8,128)(2,1)} %collective-permute-done.11.refs_3_), custom_call_target="tpu_custom_call" | custom-call | bytes 1500000 | tf_op jit(solution)/shard_map/pallas_call | solution.py:157
  269.9 10.2 %all-to-all-done.7 = bf16[16,16,1024]{2,1,0:T(8,128)(2,1)} async-done(((bf16[16,16,1024]{2,1,0:T(8,128)(2,1)}), bf16[16,16,1024]{2,1,0:T(8,128)(2,1)}, u32[]{:S(2)}, u32[]{:S(2)}) %all-to-all-start.7) | async-done | bytes 524320 | tf_op jit(solution)/shard_map/all_to_all | solution.py:186
  290.6 15.2 %all-to-all-done.8.recv_ref = bf16[8,160,256]{2,1,0:T(8,128)(2,1)} async-done(((bf16[8,160,256]{2,1,0:T(8,128)(2,1)}), bf16[8,160,256]{2,1,0:T(8,128)(2,1)}, u32[]{:S(2)}, u32[]{:S(2)}) %all-to-all-start.8) | async-done | bytes 655392 | tf_op jit(solution)/shard_map/all_to_all | solution.py:186
  313.0 9.4 %all-to-all-done.9 = bf16[8,32,512]{2,1,0:T(8,128)(2,1)} async-done(((bf16[8,32,512]{2,1,0:T(8,128)(2,1)}), bf16[8,32,512]{2,1,0:T(8,128)(2,1)}, u32[]{:S(2)}, u32[]{:S(2)}) %all-to-all-start.9) | async-done | bytes 262176 | tf_op jit(solution)/shard_map/all_to_all | solution.py:186
  324.9 9.4 %all-to-all-start.10 = ((bf16[16,16,1024]{2,1,0:T(8,128)(2,1)}), bf16[16,16,1024]{2,1,0:T(8,128)(2,1)}, u32[]{:S(2)}, u32[]{:S(2)}) async-start(bf16[16,16,1024]{2,1,0:T(8,128)(2,1)} %bitcast.47), calls=%async_computation.10 | async-start | bytes 1048576 | tf_op jit(solution)/shard_map/all_to_all | solution.py:186
  334.3 24.9 %shard_map.86.near_ref = bf16[512,768]{1,0:T(8,128)(2,1)} custom-call(s32[1]{0:T(128)} %bitcast.26.index_ref, bf16[512,768]{1,0:T(8,128)(2,1)S(1)} %shard_map.64.refs_0_, bf16[512,768]{1,0:T(8,128)(2,1)} %collective-permute-done.9.refs_1_, bf16[512,768]{1,0:T(8,128)(2,1)} %collective-permute-done.10.refs_2_, bf16[512,768]{1,0:T(8,128)(2,1)} %collective-permute-done.11.refs_3_), custom_call_target="tpu_custom_call" | custom-call | bytes 1500000 | tf_op jit(solution)/shard_map/pallas_call | solution.py:157
  362.4 6.9 %all-to-all-start.11 = ((bf16[16,16,1024]{2,1,0:T(8,128)(2,1)}), bf16[16,16,1024]{2,1,0:T(8,128)(2,1)S(1)}, u32[]{:S(2)}, u32[]{:S(2)}) async-start(bf16[16,16,1024]{2,1,0:T(8,128)(2,1)} %copy-done.22), calls=%async_computation.11 | async-start | bytes 1048576 | tf_op jit(solution)/shard_map/all_to_all | solution.py:186
  369.2 10.1 %all-to-all-done.11 = bf16[16,16,1024]{2,1,0:T(8,128)(2,1)S(1)} async-done(((bf16[16,16,1024]{2,1,0:T(8,128)(2,1)}), bf16[16,16,1024]{2,1,0:T(8,128)(2,1)S(1)}, u32[]{:S(2)}, u32[]{:S(2)}) %all-to-all-start.11) | async-done | bytes 524320 | tf_op jit(solution)/shard_map/all_to_all | solution.py:186
  389.7 15.2 %all-to-all-done.12.recv_ref = bf16[8,160,256]{2,1,0:T(8,128)(2,1)} async-done(((bf16[8,160,256]{2,1,0:T(8,128)(2,1)}), bf16[8,160,256]{2,1,0:T(8,128)(2,1)}, u32[]{:S(2)}, u32[]{:S(2)}) %all-to-all-start.12) | async-done | bytes 655392 | tf_op jit(solution)/shard_map/all_to_all | solution.py:186
  411.6 9.3 %all-to-all-done.13 = bf16[8,32,512]{2,1,0:T(8,128)(2,1)S(1)} async-done(((bf16[8,32,512]{2,1,0:T(8,128)(2,1)}), bf16[8,32,512]{2,1,0:T(8,128)(2,1)S(1)}, u32[]{:S(2)}, u32[]{:S(2)}) %all-to-all-start.13) | async-done | bytes 262176 | tf_op jit(solution)/shard_map/all_to_all | solution.py:186
  422.3 19.4 %all_to_all.80.recv_ref = bf16[16,16,1024]{2,1,0:T(8,128)(2,1)S(1)} all-to-all(bf16[16,16,1024]{2,1,0:T(8,128)(2,1)S(1)} %bitcast.49), channel_id=1, replica_groups=mesh['section'=4,'row'=4,'z'=8,'core'=2] {'section','row'}, dimensions={0} | all-to-all | bytes 1048576 | tf_op jit(solution)/shard_map/all_to_all | solution.py:186
  446.2 9.1 %all-to-all-done.15 = bf16[16,16,1024]{2,1,0:T(8,128)(2,1)S(1)} async-done(((bf16[16,16,1024]{2,1,0:T(8,128)(2,1)}), bf16[16,16,1024]{2,1,0:T(8,128)(2,1)S(1)}, u32[]{:S(2)}, u32[]{:S(2)}) %all-to-all-start.15) | async-done | bytes 524320 | tf_op jit(solution)/shard_map/all_to_all | solution.py:186
  (173 shorter events, 152.2 us)
Async XLA Ops:
  5.2 20.4 %collective-permute-start.1 = (bf16[512,768]{1,0:T(8,128)(2,1)}, bf16[512,768]{1,0:T(8,128)(2,1)}, u32[]{:S(2)}, u32[]{:S(2)}) collective-permute-start(bf16[512,768]{1,0:T(8,128)(2,1)} %shard_map.65), channel_id=1, source_target_pairs={{0,64},{1,65},{2,66},{3,67},{4,68},{5,69},{6,70},{7,71},{8,72},{9,... | collective-permute-start | bytes 2359304 | tf_op jit(solution)/shard_map/ppermute | solution.py:197
  11.8 30.6 %collective-permute-start.2 = (bf16[512,768]{1,0:T(8,128)(2,1)}, bf16[512,768]{1,0:T(8,128)(2,1)}, u32[]{:S(2)}, u32[]{:S(2)}) collective-permute-start(bf16[512,768]{1,0:T(8,128)(2,1)} %shard_map.66), channel_id=1, source_target_pairs={{0,128},{1,129},{2,130},{3,131},{4,132},{5,133},{6,134},{7,135},{8... | collective-permute-start | bytes 2359304 | tf_op jit(solution)/shard_map/ppermute | solution.py:197
  16.7 25.7 %collective-permute-start.3 = (bf16[512,768]{1,0:T(8,128)(2,1)}, bf16[512,768]{1,0:T(8,128)(2,1)}, u32[]{:S(2)}, u32[]{:S(2)}) collective-permute-start(bf16[512,768]{1,0:T(8,128)(2,1)} %shard_map.67), channel_id=1, source_target_pairs={{0,192},{1,193},{2,194},{3,195},{4,196},{5,197},{6,198},{7,199},{8... | collective-permute-start | bytes 2359304 | tf_op jit(solution)/shard_map/ppermute | solution.py:197
  48.1 45.7 %all-to-all-start = ((bf16[8,160,256]{2,1,0:T(8,128)(2,1)}), bf16[8,160,256]{2,1,0:T(8,128)(2,1)S(1)}, u32[]{:S(2)}, u32[]{:S(2)}) async-start(bf16[8,160,256]{2,1,0:T(8,128)(2,1)} %shard_map.69), calls=%async_computation | async-start | bytes 1310720 | tf_op jit(solution)/shard_map/all_to_all | solution.py:186
  59.4 14.1 %collective-permute-start.5 = (bf16[512,512]{1,0:T(8,128)(2,1)S(1)}, bf16[512,512]{1,0:T(8,128)(2,1)S(1)}, u32[]{:S(2)}, u32[]{:S(2)}) collective-permute-start(bf16[512,512]{1,0:T(8,128)(2,1)S(1)} %get-tuple-element.23), channel_id=1, source_target_pairs={{0,64},{64,128},{128,192},{192,0},{1,65},{65,129},{129,193},{193,1... | collective-permute-start | bytes 1572872 | tf_op jit(solution)/shard_map/ppermute | solution.py:169
  59.5 27.7 %collective-permute-start.6 = (bf16[512,512]{1,0:T(8,128)(2,1)S(1)}, bf16[512,512]{1,0:T(8,128)(2,1)S(1)}, u32[]{:S(2)}, u32[]{:S(2)}) collective-permute-start(bf16[512,512]{1,0:T(8,128)(2,1)S(1)} %get-tuple-element.24), channel_id=1, source_target_pairs={{0,128},{64,192},{128,0},{192,64},{1,129},{65,193},{129,1},{193,65... | collective-permute-start | bytes 1572872 | tf_op jit(solution)/shard_map/ppermute | solution.py:169
  64.3 22.8 %collective-permute-start.7 = (bf16[512,512]{1,0:T(8,128)(2,1)S(1)}, bf16[512,512]{1,0:T(8,128)(2,1)S(1)}, u32[]{:S(2)}, u32[]{:S(2)}) collective-permute-start(bf16[512,512]{1,0:T(8,128)(2,1)S(1)} %get-tuple-element.25), channel_id=1, source_target_pairs={{0,192},{64,0},{128,64},{192,128},{1,193},{65,1},{129,65},{193,129... | collective-permute-start | bytes 1572872 | tf_op jit(solution)/shard_map/ppermute | solution.py:169
  88.0 16.0 %collective-permute-start.8 = (bf16[512,512]{1,0:T(8,128)(2,1)}, bf16[512,512]{1,0:T(8,128)(2,1)}, u32[]{:S(2)}, u32[]{:S(2)}) collective-permute-start(bf16[512,512]{1,0:T(8,128)(2,1)} %shard_map.71.near_ref), channel_id=1, source_target_pairs={{0,1},{1,0},{2,3},{3,2},{4,5},{5,4},{6,7},{7,6},{8,9},{9,8},{10,11... | collective-permute-start | bytes 1572872 | tf_op jit(solution)/shard_map/ppermute | solution.py:182
  89.3 40.1 %collective-permute-start.9 = (bf16[512,768]{1,0:T(8,128)(2,1)}, bf16[512,768]{1,0:T(8,128)(2,1)}, u32[]{:S(2)}, u32[]{:S(2)}) collective-permute-start(bf16[512,768]{1,0:T(8,128)(2,1)} %shard_map.65), channel_id=1, source_target_pairs={{64,128},{128,192},{192,0},{65,129},{129,193},{193,1},{66,130},{13... | collective-permute-start | bytes 2359304 | tf_op jit(solution)/shard_map/ppermute | solution.py:169
  90.5 38.8 %collective-permute-start.10 = (bf16[512,768]{1,0:T(8,128)(2,1)}, bf16[512,768]{1,0:T(8,128)(2,1)}, u32[]{:S(2)}, u32[]{:S(2)}) collective-permute-start(bf16[512,768]{1,0:T(8,128)(2,1)} %shard_map.66), channel_id=1, source_target_pairs={{64,192},{128,0},{192,64},{65,193},{129,1},{193,65},{66,194},{130,... | collective-permute-start | bytes 2359304 | tf_op jit(solution)/shard_map/ppermute | solution.py:169
  91.8 39.9 %collective-permute-start.11 = (bf16[512,768]{1,0:T(8,128)(2,1)}, bf16[512,768]{1,0:T(8,128)(2,1)}, u32[]{:S(2)}, u32[]{:S(2)}) collective-permute-start(bf16[512,768]{1,0:T(8,128)(2,1)} %shard_map.67), channel_id=1, source_target_pairs={{64,0},{128,64},{192,128},{65,1},{129,65},{193,129},{66,2},{130,66... | collective-permute-start | bytes 2359304 | tf_op jit(solution)/shard_map/ppermute | solution.py:169
  97.3 19.0 %all-to-all-start.1 = ((bf16[8,32,512]{2,1,0:T(8,128)(2,1)}), bf16[8,32,512]{2,1,0:T(8,128)(2,1)S(1)}, u32[]{:S(2)}, u32[]{:S(2)}) async-start(bf16[8,32,512]{2,1,0:T(8,128)(2,1)} %copy-done.17), calls=%async_computation.1 | async-start | bytes 524288 | tf_op jit(solution)/shard_map/all_to_all | solution.py:186
  118.7 39.6 %all-to-all-start.2 = ((bf16[16,16,1024]{2,1,0:T(8,128)(2,1)}), bf16[16,16,1024]{2,1,0:T(8,128)(2,1)S(1)}, u32[]{:S(2)}, u32[]{:S(2)}) async-start(bf16[16,16,1024]{2,1,0:T(8,128)(2,1)} %bitcast.16), calls=%async_computation.2 | async-start | bytes 1048576 | tf_op jit(solution)/shard_map/all_to_all | solution.py:186
  159.9 18.5 %all-to-all-start.3 = ((bf16[16,16,1024]{2,1,0:T(8,128)(2,1)}), bf16[16,16,1024]{2,1,0:T(8,128)(2,1)S(1)}, u32[]{:S(2)}, u32[]{:S(2)}) async-start(bf16[16,16,1024]{2,1,0:T(8,128)(2,1)} %copy-done.20), calls=%async_computation.3 | async-start | bytes 1048576 | tf_op jit(solution)/shard_map/all_to_all | solution.py:186
  181.3 25.0 %all-to-all-start.4 = ((bf16[8,160,256]{2,1,0:T(8,128)(2,1)}), bf16[8,160,256]{2,1,0:T(8,128)(2,1)}, u32[]{:S(2)}, u32[]{:S(2)}) async-start(bf16[8,160,256]{2,1,0:T(8,128)(2,1)} %copy-done.5), calls=%async_computation.4 | async-start | bytes 1310720 | tf_op jit(solution)/shard_map/all_to_all | solution.py:186
  188.8 24.6 %collective-permute-start.13 = (bf16[512,512]{1,0:T(8,128)(2,1)}, bf16[512,512]{1,0:T(8,128)(2,1)}, u32[]{:S(2)}, u32[]{:S(2)}) collective-permute-start(bf16[512,512]{1,0:T(8,128)(2,1)} %shard_map.77.near_ref), channel_id=1, source_target_pairs={{0,1},{1,0},{2,3},{3,2},{4,5},{5,4},{6,7},{7,6},{8,9},{9,8},{10,11... | collective-permute-start | bytes 1572872 | tf_op jit(solution)/shard_map/ppermute | solution.py:182
  225.4 35.2 %all-to-all-start.6 = ((bf16[16,16,1024]{2,1,0:T(8,128)(2,1)}), bf16[16,16,1024]{2,1,0:T(8,128)(2,1)}, u32[]{:S(2)}, u32[]{:S(2)}) async-start(bf16[16,16,1024]{2,1,0:T(8,128)(2,1)} %bitcast.48), calls=%async_computation.6 | async-start | bytes 1048576 | tf_op jit(solution)/shard_map/all_to_all | solution.py:186
  263.3 16.8 %all-to-all-start.7 = ((bf16[16,16,1024]{2,1,0:T(8,128)(2,1)}), bf16[16,16,1024]{2,1,0:T(8,128)(2,1)}, u32[]{:S(2)}, u32[]{:S(2)}) async-start(bf16[16,16,1024]{2,1,0:T(8,128)(2,1)} %copy-done.21), calls=%async_computation.7 | async-start | bytes 1048576 | tf_op jit(solution)/shard_map/all_to_all | solution.py:186
  283.2 22.7 %all-to-all-start.8 = ((bf16[8,160,256]{2,1,0:T(8,128)(2,1)}), bf16[8,160,256]{2,1,0:T(8,128)(2,1)}, u32[]{:S(2)}, u32[]{:S(2)}) async-start(bf16[8,160,256]{2,1,0:T(8,128)(2,1)} %copy-done.6), calls=%async_computation.8 | async-start | bytes 1310720 | tf_op jit(solution)/shard_map/all_to_all | solution.py:186
  288.2 24.8 %collective-permute-start.15 = (bf16[512,512]{1,0:T(8,128)(2,1)}, bf16[512,512]{1,0:T(8,128)(2,1)}, u32[]{:S(2)}, u32[]{:S(2)}) collective-permute-start(bf16[512,512]{1,0:T(8,128)(2,1)} %shard_map.83.near_ref), channel_id=1, source_target_pairs={{0,1},{1,0},{2,3},{3,2},{4,5},{5,4},{6,7},{7,6},{8,9},{9,8},{10,11... | collective-permute-start | bytes 1572872 | tf_op jit(solution)/shard_map/ppermute | solution.py:182
  324.9 35.5 %all-to-all-start.10 = ((bf16[16,16,1024]{2,1,0:T(8,128)(2,1)}), bf16[16,16,1024]{2,1,0:T(8,128)(2,1)}, u32[]{:S(2)}, u32[]{:S(2)}) async-start(bf16[16,16,1024]{2,1,0:T(8,128)(2,1)} %bitcast.47), calls=%async_computation.10 | async-start | bytes 1048576 | tf_op jit(solution)/shard_map/all_to_all | solution.py:186
  362.4 17.0 %all-to-all-start.11 = ((bf16[16,16,1024]{2,1,0:T(8,128)(2,1)}), bf16[16,16,1024]{2,1,0:T(8,128)(2,1)S(1)}, u32[]{:S(2)}, u32[]{:S(2)}) async-start(bf16[16,16,1024]{2,1,0:T(8,128)(2,1)} %copy-done.22), calls=%async_computation.11 | async-start | bytes 1048576 | tf_op jit(solution)/shard_map/all_to_all | solution.py:186
  382.3 22.7 %all-to-all-start.12 = ((bf16[8,160,256]{2,1,0:T(8,128)(2,1)}), bf16[8,160,256]{2,1,0:T(8,128)(2,1)}, u32[]{:S(2)}, u32[]{:S(2)}) async-start(bf16[8,160,256]{2,1,0:T(8,128)(2,1)} %copy-done.4), calls=%async_computation.12 | async-start | bytes 1310720 | tf_op jit(solution)/shard_map/all_to_all | solution.py:186
  387.3 24.2 %collective-permute-start.17 = (bf16[512,512]{1,0:T(8,128)(2,1)}, bf16[512,512]{1,0:T(8,128)(2,1)S(1)}, u32[]{:S(2)}, u32[]{:S(2)}) collective-permute-start(bf16[512,512]{1,0:T(8,128)(2,1)} %shard_map.89.near_ref), channel_id=1, source_target_pairs={{0,1},{1,0},{2,3},{3,2},{4,5},{5,4},{6,7},{7,6},{8,9},{9,8},{10,11... | collective-permute-start | bytes 1572872 | tf_op jit(solution)/shard_map/ppermute | solution.py:182
  (49 other events, 334.4 us)

commit v3 on v1

--- a/solution.py
+++ b/solution.py
@@ -24,7 +24,8 @@
 bf16 = jnp.bfloat16
 f32 = jnp.float32
 VMEM = pl.BlockSpec(memory_space=pltpu.VMEM)
-PARAMS = pltpu.CompilerParams(vmem_limit_bytes=40 * 1024 * 1024)
+PARAMS = pltpu.CompilerParams(vmem_limit_bytes=12 * 1024 * 1024)
+STREAM = pltpu.CompilerParams(vmem_limit_bytes=56 * 1024 * 1024)
 
 
 def call(kernel, outs, args, flops):
@@ -39,11 +40,60 @@
     )(*args)
 
 
-def project_kernel(x_ref, near_ref, far_ref, out_ref):
-    x = x_ref[...]
-    half = x.shape[1] // 2
-    y = jnp.dot(x[:, :half], near_ref[...], preferred_element_type=f32)
-    y = y + jnp.dot(x[:, half:], far_ref[...], preferred_element_type=f32)
+def project(x, near, far, layer, far_layer, kept, flag):
+    rows = 256
+    outs = [jax.ShapeDtypeStruct((CHIPS, PACK, 256), bf16)]
+    args = [x, near, far]
+    in_specs = [
+        VMEM,
+        pl.BlockSpec((1, rows, 768), lambda i: (layer, i, 0)),
+        pl.BlockSpec((1, rows, 768), lambda i: (far_layer, i, 0)),
+    ]
+    if kept is not None:
+        outs.append(jax.ShapeDtypeStruct(kept.shape, bf16))
+        args += [kept, flag]
+        in_specs += [VMEM, pl.BlockSpec(memory_space=pltpu.SMEM)]
+    return pl.pallas_call(
+        project_kernel if kept is not None else first_project_kernel,
+        out_shape=outs,
+        grid=(2,),
+        in_specs=in_specs,
+        out_specs=[VMEM] * len(outs),
+        scratch_shapes=[pltpu.VMEM((TOK, 768), f32)],
+        compiler_params=PARAMS,
+        cost_estimate=pl.CostEstimate(flops=2 * 256 * 1024 * 1024, bytes_accessed=3_000_000, transcendentals=0),
+    )(*args)
+
+
+def first_project_kernel(x_ref, near_ref, far_ref, out_ref, sum_ref):
+    project_step(x_ref, near_ref, far_ref, out_ref, sum_ref)
+
+
+def project_kernel(x_ref, near_ref, far_ref, kept_ref, flag_ref, out_ref, next_ref, sum_ref):
+    project_step(x_ref, near_ref, far_ref, out_ref, sum_ref)
+
+    @pl.when(pl.program_id(0) == 0)
+    def _():
+        next_ref[...] = jnp.where(flag_ref[0] == 1, x_ref[...], kept_ref[...])
+
+
+def project_step(x_ref, near_ref, far_ref, out_ref, sum_ref):
+    step = pl.program_id(0)
+    near_x = x_ref[:, pl.ds(pl.multiple_of(step * 256, 256), 256)]
+    far_x = x_ref[:, pl.ds(pl.multiple_of(512 + step * 256, 256), 256)]
+    part = jnp.dot(near_x, near_ref[0], preferred_element_type=f32)
+    part = part + jnp.dot(far_x, far_ref[0], preferred_element_type=f32)
+
+    @pl.when(step == 0)
+    def _():
+        sum_ref[...] = part
+
+    @pl.when(step == 1)
+    def _():
+        pack(x_ref[...], sum_ref[...] + part, out_ref)
+
+
+def pack(x, y, out_ref):
     gram = lax.dot_general(x, x, (((1,), (1,)), ((), ())), preferred_element_type=f32)
     rows = lax.broadcasted_iota(jnp.int32, gram.shape, 0)
     cols = lax.broadcasted_iota(jnp.int32, gram.shape, 1)
@@ -100,9 +150,21 @@
 
 def out_kernel(mixed_ref, near_ref, far_ref, out_ref):
     mixed = mixed_ref[...]
-    half = near_ref.shape[1]
-    out_ref[:, :half] = jnp.dot(mixed, near_ref[...], preferred_element_type=f32).astype(bf16)
-    out_ref[:, half:] = jnp.dot(mixed, far_ref[...], preferred_element_type=f32).astype(bf16)
+    half = near_ref.shape[2]
+    out_ref[:, :half] = jnp.dot(mixed, near_ref[0], preferred_element_type=f32).astype(bf16)
+    out_ref[:, half:] = jnp.dot(mixed, far_ref[0], preferred_element_type=f32).astype(bf16)
+
+
+def spread(mixed, near, far, layer):
+    return pl.pallas_call(
+        out_kernel,
+        out_shape=jax.ShapeDtypeStruct((TOK, 1024), bf16),
+        grid=(1,),
+        in_specs=[VMEM] + [pl.BlockSpec((1, 512, 512), lambda i: (layer, 0, 0))] * 2,
+        out_specs=VMEM,
+        compiler_params=PARAMS,
+        cost_estimate=pl.CostEstimate(flops=2 * 256 * 512 * 1024, bytes_accessed=2_000_000, transcendentals=0),
+    )(mixed, near, far)
 
 
 def sum_kernel(recv_ref, held_ref, out_ref, own_ref):
@@ -115,6 +177,44 @@
         out_ref[d] = own
 
 
+def weigh_kernel(query_ref, pair_ref, gain_ref, out_ref):
+    rows = lax.broadcasted_iota(jnp.int32, (128, 128), 0)
+    cols = lax.broadcasted_iota(jnp.int32, (128, 128), 1)
+    scale = jnp.sum(jnp.where(rows == cols, gain_ref[...], 0.0), axis=1, keepdims=True)
+    for d in range(4):
+        query = query_ref[0, :, 512 * d : 512 * (d + 1)]
+        pair = pair_ref[0, :, 256 * (d // 2) : 256 * (d // 2 + 1)]
+        out_ref[d, :, :512] = (query.astype(f32) * scale).astype(bf16)
+        out_ref[d, :, 512:] = (pair.astype(f32) * scale).astype(bf16)
+
+
+def weigh(w_query, w_pair, gain):
+    return pl.pallas_call(
+        weigh_kernel,
+        out_shape=jax.ShapeDtypeStruct((4, 512, 768), bf16),
+        grid=(4,),
+        in_specs=[
+            pl.BlockSpec((1, 128, 2048), lambda i: (0, i, 0)),
+            pl.BlockSpec((1, 128, 512), lambda i: (0, i, 0)),
+            pl.BlockSpec((1, 128), lambda i: (0, i)),
+        ],
+        out_specs=pl.BlockSpec((4, 128, 768), lambda i: (0, i, 0)),
+        compiler_params=STREAM,
+        cost_estimate=pl.CostEstimate(flops=2_000_000, bytes_accessed=6_000_000, transcendentals=0),
+    )(w_query, w_pair, gain)
+
+
+def choose(arrays, is_index):
+    chosen = arrays[0]
+    for i in range(1, len(arrays)):
+        chosen = jnp.where(is_index[i], arrays[i], chosen)
+    return chosen
+
+
+def rotated(value, steps):
+    return lax.ppermute(value, "section", [(s, (s + steps) % 4) for s in range(4)])
+
+
 def segment_info(lengths_row, total):
     token_ids = jnp.arange(total, dtype=jnp.int32)
     ends = jnp.cumsum(lengths_row)
@@ -138,13 +238,10 @@
     core = lax.axis_index("core")
     grid_place = section * 4 + lax.axis_index("row")
 
-    queries_w = w_query[0].reshape(512, 4, 512).transpose(1, 0, 2)
-    pairs_w = jnp.repeat(w_pair[0].reshape(512, 2, 256).transpose(1, 0, 2), 2, axis=0)
-    send_in = jnp.concatenate([queries_w, pairs_w], axis=2).astype(f32) * gain[0][None, :, None]
-    near_in = exchange(send_in.astype(bf16), "section")
-    far_in = swap(near_in)
-    near_out = exchange(w_out[0].reshape(4, 512, 512), "section")
-    far_out = swap(near_out)
+    near_in = exchange(weigh(w_query, w_pair, gain), "section")
+    far_first = swap(near_in[:1])
+    blocks_out = [lax.dynamic_slice(w_out, (0, 512 * ((section + k) % 4), 0), (1, 512, 512))[0] for k in range(4)]
+    turn = [(section - layer) % 4 for layer in range(LAYERS)]
 
     mine = lax.dynamic_index_in_dim(hidden_in, core, 0, keepdims=False)
     theirs = lax.dynamic_index_in_dim(hidden_in, 1 - core, 0, keepdims=False)
@@ -175,21 +272,29 @@
             cost_estimate=pl.CostEstimate(flops=10_000_000, bytes_accessed=1_000_000, transcendentals=20_000),
         )(place_arg, recv, cosine, sine, mask)
 
-    states = []
+    is_section = [(section == layer).astype(jnp.int32).reshape(1) for layer in range(LAYERS)]
+    is_turn = [[turn[layer] == k for k in range(4)] for layer in range(LAYERS)]
+    near_in, x, held, cosine, sine, mask, place_arg, is_section, is_turn, blocks_out = lax.optimization_barrier(
+        (near_in, x, held, cosine, sine, mask, place_arg, is_section, is_turn, blocks_out)
+    )
+    moved_out = [blocks_out[0]] + [rotated(blocks_out[k], k) for k in range(1, 4)]
+    kept = None
     for layer in range(LAYERS):
-        packed = call(
-            project_kernel,
-            jax.ShapeDtypeStruct((CHIPS, PACK, 256), bf16),
-            (x, near_in[layer], far_in[layer]),
-            2 * 256 * 1024 * 1024,
-        )
-        mixed = exchange(attend(exchange(packed, "z")), "z").reshape(TOK, 512)
-        branch = call(
-            out_kernel,
-            jax.ShapeDtypeStruct((TOK, 1024), bf16),
-            (mixed, near_out[layer], far_out[layer]),
-            2 * 256 * 512 * 1024,
-        )
+        if layer == 0:
+            (packed,) = project(x, near_in, far_first, 0, 0, None, None)
+        elif layer == 1:
+            (packed,) = project(x, near_in, far_in, layer, layer, None, None)
+            kept = x
+        else:
+            packed, kept = project(x, near_in, far_in, layer, layer, kept, is_section[layer - 1])
+        copies = attend(exchange(packed, "z"))
+        if layer == 0:
+            copies, moved_out, rest = lax.optimization_barrier((copies, moved_out, near_in))
+            near_out = jnp.stack([choose(moved_out, is_turn[each]) for each in range(LAYERS)])
+            far_out = swap(near_out)
+            far_in = swap(rest)
+        mixed = exchange(copies, "z").reshape(TOK, 512)
+        branch = spread(mixed, near_out, far_out, layer)
         copies, held = call(
             sum_kernel,
             (jax.ShapeDtypeStruct((GRID, PART, 1024), bf16), jax.ShapeDtypeStruct((PART, 1024), bf16)),
@@ -197,11 +302,8 @@
             256 * 1024,
         )
         x = exchange(copies, ("section", "row")).reshape(TOK, 1024)
-        states.append(x)
-
-    kept = states[0]
-    for layer in range(1, LAYERS):
-        kept = jnp.where(section == layer, states[layer], kept)
+
+    kept = jnp.where(is_section[LAYERS - 1] == 1, x, kept)
     ours = kept[:, :512]
     other = swap(kept[:, 512:])
     final = jnp.where(core == 0, jnp.stack([ours, other]), jnp.stack([other, ours]))

time: 366 us -> 337 us (0.921)
  local copies, waits for them, and re-layouts: 24.1 us -> 8.74 us
  waiting for transfers between devices: 72.4 us -> 62 us
  blocking collectives: 205 us -> 197 us
  other arithmetic: 3.53 us -> 7.51 us
  Pallas kernels: 12.4 us -> 16.3 us
    all_to_all x5 -> x3, waiting for transfers between devices: 70.1 us -> 57 us  [exchange(): return lax.all_to_all(value, axis, 0, 0, tiled=True)]
    pallas_call x0 -> x9, Pallas kernels: none -> 11.9 us  [the longest x4 5.71 us: project(): pl.pallas_call(project_kernel if kept is not None else first_project_kern...]
    squeeze x4 -> x1, local copies, waits for them, and re-layouts: 11.7 us -> 2.88 us  [local(): lax.dynamic_slice(w_out, (0, 512 * ((section + k) % 4), 0), (1, 512, 512))]
    all_to_all x5 -> x3, starting transfers between devices: 25.2 us -> 16.7 us  [exchange(): return lax.all_to_all(value, axis, 0, 0, tiled=True)]
    all_to_all x13 -> x14, blocking collectives: 205 us -> 197 us  [exchange(): return lax.all_to_all(value, axis, 0, 0, tiled=True)]
    pallas_call x12 -> x4, Pallas kernels: 8.41 us -> 1.2 us  [call(): pl.pallas_call(kernel, out_shape=outs, in_specs=[VMEM] * len(args), out_s...]
    unnamed x37 -> x12, local copies, waits for them, and re-layouts: 7.56 us -> 1.55 us
    another operation x3 -> x1, local copies, waits for them, and re-layouts: 4.41 us -> 0.09 us  [the longest x1 4.19 us: local(): queries_w = w_query[0].reshape(512, 4, 512).transpose(1, 0, 2)]
  transfers between devices with their start and end apart: 9 -> 11, of which waited for: 7 -> 6; matrix products, arithmetic and copies ran while one was open for 4% -> 4% of each run, Pallas kernels for 1% -> 1%
where the time goes in v3:
time: 337 us; the launch traced here: 336 us
  blocking collectives  197 us (58%)
  waiting for transfers between devices  62 us (18%)
  starting transfers between devices  44 us (13%)
  Pallas kernels  16.3 us (5%)
  local copies, waits for them, and re-layouts  8.74 us (3%)
  other arithmetic  7.51 us (2%)
    all_to_all x14, blocking collectives, exchange(): return lax.all_to_all(value, axis, 0, 0, tiled=True)  197 us
    all_to_all x3, waiting for transfers between devices, exchange(): return lax.all_to_all(value, axis, 0, 0, tiled=True)  57 us
    ppermute x5, starting transfers between devices, swap(): return lax.ppermute(value, 'core', [(0, 1), (1, 0)])  24.5 us
    all_to_all x3, starting transfers between devices, exchange(): return lax.all_to_all(value, axis, 0, 0, tiled=True)  16.7 us
  transfers between devices with their start and end apart: 11, of which 6 were waited for; matrix products, arithmetic and copies ran while one was open for 4% of the time, Pallas kernels for 1%

profile of v3, /device:TPU:1, one launch (start us, length us, event | category | flops | bytes accessed | tf_op | source)
XLA Modules:
  0.0 335.7 jit_solution(14835441251964509678)
XLA Ops:
  0.0 4.4 %shard_map.64 = bf16[4,512,768]{2,1,0:T(8,128)(2,1)} custom-call(bf16[1,512,2048]{2,1,0:T(8,128)(2,1)} %query_ref.1, bf16[1,512,512]{2,1,0:T(8,128)(2,1)} %pair_ref.1, f32[1,512]{1,0:T(1,128)} %gain_ref.1), custom_call_target="tpu_custom_call" | custom-call | flops 2000000 | bytes 6000000 | tf_op jit(solution)/shard_map/pallas_call | solution.py:192
  4.4 5.0 %all-to-all-start = ((bf16[4,512,768]{2,1,0:T(8,128)(2,1)}), bf16[4,512,768]{2,1,0:T(8,128)(2,1)S(1)}, u32[]{:S(2)}, u32[]{:S(2)}) async-start(bf16[4,512,768]{2,1,0:T(8,128)(2,1)} %shard_map.64), calls=%async_computation | async-start | bytes 6291456 | tf_op jit(solution)/shard_map/all_to_all | solution.py:232
  15.3 29.6 %all-to-all-done.near_ref = bf16[4,512,768]{2,1,0:T(8,128)(2,1)S(1)} async-done(((bf16[4,512,768]{2,1,0:T(8,128)(2,1)}), bf16[4,512,768]{2,1,0:T(8,128)(2,1)S(1)}, u32[]{:S(2)}, u32[]{:S(2)}) %all-to-all-start) | async-done | bytes 3145760 | tf_op jit(solution)/shard_map/all_to_all | solution.py:232
  45.9 3.0 collective-permute-start.1
  59.8 8.2 %all-to-all-start.1 = ((bf16[8,160,256]{2,1,0:T(8,128)(2,1)}), bf16[8,160,256]{2,1,0:T(8,128)(2,1)}, u32[]{:S(2)}, u32[]{:S(2)}) async-start(bf16[8,160,256]{2,1,0:T(8,128)(2,1)} %copy-done), calls=%async_computation.1 | async-start | bytes 1310720 | tf_op jit(solution)/shard_map/all_to_all | solution.py:232
  70.7 18.1 %all-to-all-done.1.recv_ref = bf16[8,160,256]{2,1,0:T(8,128)(2,1)} async-done(((bf16[8,160,256]{2,1,0:T(8,128)(2,1)}), bf16[8,160,256]{2,1,0:T(8,128)(2,1)}, u32[]{:S(2)}, u32[]{:S(2)}) %all-to-all-start.1) | async-done | bytes 655392 | tf_op jit(solution)/shard_map/all_to_all | solution.py:232
  90.5 2.9 collective-permute-done.3
  97.8 17.2 %all_to_all.85 = bf16[8,32,512]{2,1,0:T(8,128)(2,1)S(1)} all-to-all(bf16[8,32,512]{2,1,0:T(8,128)(2,1)S(1)} %shard_map.66), channel_id=1, replica_groups=mesh['section'=4,'row'=4,'z'=8,'core'=2] {'z'}, dimensions={0} | all-to-all | bytes 524288 | tf_op jit(solution)/shard_map/all_to_all | solution.py:232
  115.4 15.1 %all_to_all.86.recv_ref = bf16[16,16,1024]{2,1,0:T(8,128)(2,1)S(1)} all-to-all(bf16[16,16,1024]{2,1,0:T(8,128)(2,1)S(1)} %bitcast.49), channel_id=1, replica_groups=mesh['section'=4,'row'=4,'z'=8,'core'=2] {'section','row'}, dimensions={0} | all-to-all | bytes 1048576 | tf_op jit(solution)/shard_map/all_to_all | solution.py:232
  130.6 11.9 %all_to_all.87 = bf16[16,16,1024]{2,1,0:T(8,128)(2,1)S(1)} all-to-all(bf16[16,16,1024]{2,1,0:T(8,128)(2,1)S(1)} %get-tuple-element.77), channel_id=1, replica_groups=mesh['section'=4,'row'=4,'z'=8,'core'=2] {'section','row'}, dimensions={0} | all-to-all | bytes 1048576 | tf_op jit(solution)/shard_map/all_to_all | solution.py:232
  143.7 19.5 %all_to_all.88.recv_ref = bf16[8,160,256]{2,1,0:T(8,128)(2,1)S(1)} all-to-all(bf16[8,160,256]{2,1,0:T(8,128)(2,1)S(1)} %shard_map.69), channel_id=1, replica_groups=mesh['section'=4,'row'=4,'z'=8,'core'=2] {'z'}, dimensions={0} | all-to-all | bytes 1310720 | tf_op jit(solution)/shard_map/all_to_all | solution.py:232
  163.8 12.6 %all_to_all.89 = bf16[8,32,512]{2,1,0:T(8,128)(2,1)S(1)} all-to-all(bf16[8,32,512]{2,1,0:T(8,128)(2,1)S(1)} %shard_map.70), channel_id=1, replica_groups=mesh['section'=4,'row'=4,'z'=8,'core'=2] {'z'}, dimensions={0} | all-to-all | bytes 524288 | tf_op jit(solution)/shard_map/all_to_all | solution.py:232
  176.8 11.9 %all_to_all.90.recv_ref = bf16[16,16,1024]{2,1,0:T(8,128)(2,1)S(1)} all-to-all(bf16[16,16,1024]{2,1,0:T(8,128)(2,1)S(1)} %bitcast.50), channel_id=1, replica_groups=mesh['section'=4,'row'=4,'z'=8,'core'=2] {'section','row'}, dimensions={0} | all-to-all | bytes 1048576 | tf_op jit(solution)/shard_map/all_to_all | solution.py:232
  188.8 11.9 %all_to_all.91 = bf16[16,16,1024]{2,1,0:T(8,128)(2,1)S(1)} all-to-all(bf16[16,16,1024]{2,1,0:T(8,128)(2,1)S(1)} %get-tuple-element.80), channel_id=1, replica_groups=mesh['section'=4,'row'=4,'z'=8,'core'=2] {'section','row'}, dimensions={0} | all-to-all | bytes 1048576 | tf_op jit(solution)/shard_map/all_to_all | solution.py:232
  201.9 16.0 %all_to_all.92.recv_ref = bf16[8,160,256]{2,1,0:T(8,128)(2,1)S(1)} all-to-all(bf16[8,160,256]{2,1,0:T(8,128)(2,1)S(1)} %get-tuple-element.82), channel_id=1, replica_groups=mesh['section'=4,'row'=4,'z'=8,'core'=2] {'z'}, dimensions={0} | all-to-all | bytes 1310720 | tf_op jit(solution)/shard_map/all_to_all | solution.py:232
  218.5 11.7 %all_to_all.93 = bf16[8,32,512]{2,1,0:T(8,128)(2,1)S(1)} all-to-all(bf16[8,32,512]{2,1,0:T(8,128)(2,1)S(1)} %shard_map.74), channel_id=1, replica_groups=mesh['section'=4,'row'=4,'z'=8,'core'=2] {'z'}, dimensions={0} | all-to-all | bytes 524288 | tf_op jit(solution)/shard_map/all_to_all | solution.py:232
  230.7 11.9 %all_to_all.94.recv_ref = bf16[16,16,1024]{2,1,0:T(8,128)(2,1)S(1)} all-to-all(bf16[16,16,1024]{2,1,0:T(8,128)(2,1)S(1)} %bitcast.51), channel_id=1, replica_groups=mesh['section'=4,'row'=4,'z'=8,'core'=2] {'section','row'}, dimensions={0} | all-to-all | bytes 1048576 | tf_op jit(solution)/shard_map/all_to_all | solution.py:232
  242.7 14.0 %all_to_all.95 = bf16[16,16,1024]{2,1,0:T(8,128)(2,1)S(1)} all-to-all(bf16[16,16,1024]{2,1,0:T(8,128)(2,1)S(1)} %get-tuple-element.84), channel_id=1, replica_groups=mesh['section'=4,'row'=4,'z'=8,'core'=2] {'section','row'}, dimensions={0} | all-to-all | bytes 1048576 | tf_op jit(solution)/shard_map/all_to_all | solution.py:232
  257.9 15.9 %all_to_all.96.recv_ref = bf16[8,160,256]{2,1,0:T(8,128)(2,1)S(1)} all-to-all(bf16[8,160,256]{2,1,0:T(8,128)(2,1)S(1)} %get-tuple-element.87), channel_id=1, replica_groups=mesh['section'=4,'row'=4,'z'=8,'core'=2] {'z'}, dimensions={0} | all-to-all | bytes 1310720 | tf_op jit(solution)/shard_map/all_to_all | solution.py:232
  274.4 14.9 %all_to_all.97 = bf16[8,32,512]{2,1,0:T(8,128)(2,1)S(1)} all-to-all(bf16[8,32,512]{2,1,0:T(8,128)(2,1)S(1)} %shard_map.78), channel_id=1, replica_groups=mesh['section'=4,'row'=4,'z'=8,'core'=2] {'z'}, dimensions={0} | all-to-all | bytes 524288 | tf_op jit(solution)/shard_map/all_to_all | solution.py:232
  289.8 12.1 %all_to_all.98.recv_ref = bf16[16,16,1024]{2,1,0:T(8,128)(2,1)S(1)} all-to-all(bf16[16,16,1024]{2,1,0:T(8,128)(2,1)S(1)} %bitcast.48), channel_id=1, replica_groups=mesh['section'=4,'row'=4,'z'=8,'core'=2] {'section','row'}, dimensions={0} | all-to-all | bytes 1048576 | tf_op jit(solution)/shard_map/all_to_all | solution.py:232
  302.8 3.6 %all-to-all-start.16 = ((bf16[16,16,1024]{2,1,0:T(8,128)(2,1)}), bf16[16,16,1024]{2,1,0:T(8,128)(2,1)S(1)}, u32[]{:S(2)}, u32[]{:S(2)}) async-start(bf16[16,16,1024]{2,1,0:T(8,128)(2,1)} %get-tuple-element.89), calls=%async_computation.16 | async-start | bytes 1048576 | tf_op jit(solution)/shard_map/all_to_all | solution.py:232
  306.3 9.3 %all-to-all-done.16 = bf16[16,16,1024]{2,1,0:T(8,128)(2,1)S(1)} async-done(((bf16[16,16,1024]{2,1,0:T(8,128)(2,1)}), bf16[16,16,1024]{2,1,0:T(8,128)(2,1)S(1)}, u32[]{:S(2)}, u32[]{:S(2)}) %all-to-all-start.16) | async-done | bytes 524320 | tf_op jit(solution)/shard_map/all_to_all | solution.py:232
  315.8 17.9 %collective-permute-start.7 = (bf16[256,512]{1,0:T(8,128)(2,1)S(1)}, bf16[256,512]{1,0:T(8,128)(2,1)S(1)}, u32[]{:S(2)}, u32[]{:S(2)}) collective-permute-start(bf16[256,512]{1,0:T(8,128)(2,1)S(1)} %get-tuple-element.104), channel_id=1, source_target_pairs={{0,1},{1,0},{2,3},{3,2},{4,5},{5,4},{6,7},{7,6},{8,9},{9,8},{10,11... | collective-permute-start | bytes 786440 | tf_op jit(solution)/shard_map/ppermute | solution.py:228
  (66 shorter events, 36.6 us)
Async XLA Ops:
  4.4 9.0 %copy-start.5 = (s32[2,32]{1,0:T(2,128)S(1)}, s32[2,32]{1,0:T(2,128)}, u32[]{:S(2)}) copy-start(s32[2,32]{1,0:T(2,128)} %param.7) | copy-start | bytes 772
  4.4 40.5 %all-to-all-start = ((bf16[4,512,768]{2,1,0:T(8,128)(2,1)}), bf16[4,512,768]{2,1,0:T(8,128)(2,1)S(1)}, u32[]{:S(2)}, u32[]{:S(2)}) async-start(bf16[4,512,768]{2,1,0:T(8,128)(2,1)} %shard_map.64), calls=%async_computation | async-start | bytes 6291456 | tf_op jit(solution)/shard_map/all_to_all | solution.py:232
  11.3 42.9 %collective-permute-start = (bf16[256,512]{1,0:T(8,128)(2,1)}, bf16[256,512]{1,0:T(8,128)(2,1)S(1)}, u32[]{:S(2)}, u32[]{:S(2)}) collective-permute-start(bf16[256,512]{1,0:T(8,128)(2,1)} %get-tuple-element.106), channel_id=1, source_target_pairs={{0,1},{1,0},{2,3},{3,2},{4,5},{5,4},{6,7},{7,6},{8,9},{9,8},{10,11... | collective-permute-start | bytes 786440 | tf_op jit(solution)/shard_map/ppermute | solution.py:228
  45.9 10.8 %collective-permute-start.1 = (bf16[1,512,768]{2,1,0:T(8,128)(2,1)}, bf16[1,512,768]{2,1,0:T(8,128)(2,1)}, u32[]{:S(2)}, u32[]{:S(2)}) collective-permute-start(bf16[1,512,768]{2,1,0:T(8,128)(2,1)} %slice.20), channel_id=1, source_target_pairs={{0,1},{1,0},{2,3},{3,2},{4,5},{5,4},{6,7},{7,6},{8,9},{9,8},{10,11... | collective-permute-start | bytes 2359304 | tf_op jit(solution)/shard_map/ppermute | solution.py:228
  49.0 2.9 copy-start.4
  54.2 0.7 copy-start.3
  58.9 0.8 copy-start
  59.8 29.1 %all-to-all-start.1 = ((bf16[8,160,256]{2,1,0:T(8,128)(2,1)}), bf16[8,160,256]{2,1,0:T(8,128)(2,1)}, u32[]{:S(2)}, u32[]{:S(2)}) async-start(bf16[8,160,256]{2,1,0:T(8,128)(2,1)} %copy-done), calls=%async_computation.1 | async-start | bytes 1310720 | tf_op jit(solution)/shard_map/all_to_all | solution.py:232
  67.9 22.5 %collective-permute-start.2 = (bf16[512,512]{1,0:T(8,128)(2,1)}, bf16[512,512]{1,0:T(8,128)(2,1)}, u32[]{:S(2)}, u32[]{:S(2)}) collective-permute-start(bf16[512,512]{1,0:T(8,128)(2,1)} %get-tuple-element.56), channel_id=1, source_target_pairs={{0,64},{64,128},{128,192},{192,0},{1,65},{65,129},{129,193},{193,1... | collective-permute-start | bytes 1572872 | tf_op jit(solution)/shard_map/ppermute | solution.py:215
  68.2 25.1 %collective-permute-start.3 = (bf16[512,512]{1,0:T(8,128)(2,1)}, bf16[512,512]{1,0:T(8,128)(2,1)}, u32[]{:S(2)}, u32[]{:S(2)}) collective-permute-start(bf16[512,512]{1,0:T(8,128)(2,1)} %get-tuple-element.57), channel_id=1, source_target_pairs={{0,128},{64,192},{128,0},{192,64},{1,129},{65,193},{129,1},{193,65... | collective-permute-start | bytes 1572872 | tf_op jit(solution)/shard_map/ppermute | solution.py:215
  70.0 24.3 %collective-permute-start.4 = (bf16[512,512]{1,0:T(8,128)(2,1)}, bf16[512,512]{1,0:T(8,128)(2,1)}, u32[]{:S(2)}, u32[]{:S(2)}) collective-permute-start(bf16[512,512]{1,0:T(8,128)(2,1)} %get-tuple-element.58), channel_id=1, source_target_pairs={{0,192},{64,0},{128,64},{192,128},{1,193},{65,1},{129,65},{193,129... | collective-permute-start | bytes 1572872 | tf_op jit(solution)/shard_map/ppermute | solution.py:215
  94.3 48.3 %collective-permute-start.6 = (bf16[4,512,768]{2,1,0:T(8,128)(2,1)S(1)}, bf16[4,512,768]{2,1,0:T(8,128)(2,1)S(1)}, u32[]{:S(2)}, u32[]{:S(2)}) collective-permute-start(bf16[4,512,768]{2,1,0:T(8,128)(2,1)S(1)} %all-to-all-done.near_ref), channel_id=1, source_target_pairs={{0,1},{1,0},{2,3},{3,2},{4,5},{5,4},{6,7},{7,6},{8,9},{9,8},{10,11... | collective-permute-start | bytes 9437192 | tf_op jit(solution)/shard_map/ppermute | solution.py:228
  97.7 17.3 %collective-permute-start.5 = (bf16[4,512,512]{2,1,0:T(8,128)(2,1)S(1)}, bf16[4,512,512]{2,1,0:T(8,128)(2,1)S(1)}, u32[]{:S(2)}, u32[]{:S(2)}) collective-permute-start(bf16[4,512,512]{2,1,0:T(8,128)(2,1)S(1)} %pad_maximum_fusion.near_ref), channel_id=1, source_target_pairs={{0,1},{1,0},{2,3},{3,2},{4,5},{5,4},{6,7},{7,6},{8,9},{9,8},{10,11... | collective-permute-start | bytes 6291464 | tf_op jit(solution)/shard_map/ppermute | solution.py:228
  257.9 31.8 %copy-start.1 = (bf16[256,1024]{1,0:T(8,128)(2,1)}, bf16[256,1024]{1,0:T(8,128)(2,1)S(1)}, u32[]{:S(2)}) copy-start(bf16[256,1024]{1,0:T(8,128)(2,1)S(1)} %get-tuple-element.90) | copy-start | bytes 1572868
  289.8 25.9 %copy-start.2 = (bf16[256,1024]{1,0:T(8,128)(2,1)S(1)}, bf16[256,1024]{1,0:T(8,128)(2,1)}, u32[]{:S(2)}) copy-start(bf16[256,1024]{1,0:T(8,128)(2,1)} %copy-done.1) | copy-start | bytes 1572868
  302.8 12.9 %all-to-all-start.16 = ((bf16[16,16,1024]{2,1,0:T(8,128)(2,1)}), bf16[16,16,1024]{2,1,0:T(8,128)(2,1)S(1)}, u32[]{:S(2)}, u32[]{:S(2)}) async-start(bf16[16,16,1024]{2,1,0:T(8,128)(2,1)} %get-tuple-element.89), calls=%async_computation.16 | async-start | bytes 1048576 | tf_op jit(solution)/shard_map/all_to_all | solution.py:232
  315.8 19.1 %collective-permute-start.7 = (bf16[256,512]{1,0:T(8,128)(2,1)S(1)}, bf16[256,512]{1,0:T(8,128)(2,1)S(1)}, u32[]{:S(2)}, u32[]{:S(2)}) collective-permute-start(bf16[256,512]{1,0:T(8,128)(2,1)S(1)} %get-tuple-element.104), channel_id=1, source_target_pairs={{0,1},{1,0},{2,3},{3,2},{4,5},{5,4},{6,7},{7,6},{8,9},{9,8},{10,11... | collective-permute-start | bytes 786440 | tf_op jit(solution)/shard_map/ppermute | solution.py:228

commit v4 on v3

--- a/solution.py
+++ b/solution.py
@@ -239,7 +239,6 @@
     grid_place = section * 4 + lax.axis_index("row")
 
     near_in = exchange(weigh(w_query, w_pair, gain), "section")
-    far_first = swap(near_in[:1])
     blocks_out = [lax.dynamic_slice(w_out, (0, 512 * ((section + k) % 4), 0), (1, 512, 512))[0] for k in range(4)]
     turn = [(section - layer) % 4 for layer in range(LAYERS)]
 
@@ -277,6 +276,10 @@
     near_in, x, held, cosine, sine, mask, place_arg, is_section, is_turn, blocks_out = lax.optimization_barrier(
         (near_in, x, held, cosine, sine, mask, place_arg, is_section, is_turn, blocks_out)
     )
+    far_first = swap(near_in[:1])
+    def mix(packed):
+        return attend(exchange(packed, "z"))
+
     moved_out = [blocks_out[0]] + [rotated(blocks_out[k], k) for k in range(1, 4)]
     kept = None
     for layer in range(LAYERS):
@@ -287,12 +290,15 @@
             kept = x
         else:
             packed, kept = project(x, near_in, far_in, layer, layer, kept, is_section[layer - 1])
-        copies = attend(exchange(packed, "z"))
         if layer == 0:
+            copies = lax.cond(lengths[0, 0] > 0, mix, lambda value: jnp.zeros((CHIPS, OWN, 512), bf16), packed)
             copies, moved_out, rest = lax.optimization_barrier((copies, moved_out, near_in))
             near_out = jnp.stack([choose(moved_out, is_turn[each]) for each in range(LAYERS)])
+            copies, near_out = lax.optimization_barrier((copies, near_out))
             far_out = swap(near_out)
             far_in = swap(rest)
+        else:
+            copies = mix(packed)
         mixed = exchange(copies, "z").reshape(TOK, 512)
         branch = spread(mixed, near_out, far_out, layer)
         copies, held = call(

time: 337 us -> 328 us (0.973)
  waiting for transfers between devices: 62 us -> 34.2 us
  blocking collectives: 197 us -> 223 us
  starting transfers between devices: 44 us -> 37 us
    all_to_all x14 -> x15, blocking collectives: 197 us -> 223 us  [exchange(): return lax.all_to_all(value, axis, 0, 0, tiled=True)]
    all_to_all x3 -> x2, waiting for transfers between devices: 57 us -> 33 us  [exchange(): return lax.all_to_all(value, axis, 0, 0, tiled=True)]
    all_to_all x3 -> x2, starting transfers between devices: 16.7 us -> 8.55 us  [exchange(): return lax.all_to_all(value, axis, 0, 0, tiled=True)]
    ppermute x3, waiting for transfers between devices: 3.81 us -> 0.01 us  [rotated(): lax.ppermute(value, 'section', [(s, (s + steps) % 4) for s in range(4)])]
  transfers between devices with their start and end apart: 11 -> 10, of which waited for: 6 -> 3; matrix products, arithmetic and copies ran while one was open for 4% -> 4% of each run, Pallas kernels for 1% -> 1%
where the time goes in v4:
time: 328 us; the launch traced here: 327 us
  blocking collectives  223 us (68%)
  starting transfers between devices  37 us (11%)
  waiting for transfers between devices  34.2 us (10%)
  Pallas kernels  15.8 us (5%)
  local copies, waits for them, and re-layouts  7.99 us (2%)
  other arithmetic  7.58 us (2%)
    all_to_all x15, blocking collectives, exchange(): return lax.all_to_all(value, axis, 0, 0, tiled=True)  223 us
    all_to_all x2, waiting for transfers between devices, exchange(): return lax.all_to_all(value, axis, 0, 0, tiled=True)  33 us
    ppermute x5, starting transfers between devices, swap(): return lax.ppermute(value, 'core', [(0, 1), (1, 0)])  25.7 us
    all_to_all x2, starting transfers between devices, exchange(): return lax.all_to_all(value, axis, 0, 0, tiled=True)  8.55 us
  transfers between devices with their start and end apart: 10, of which 3 were waited for; matrix products, arithmetic and copies ran while one was open for 4% of the time, Pallas kernels for 1%

profile of v4, /device:TPU:1, one launch (start us, length us, event | category | flops | bytes accessed | tf_op | source)
XLA Modules:
  0.0 326.8 jit_solution(3770130330547014127)
XLA Ops:
  0.0 4.4 %shard_map.64 = bf16[4,512,768]{2,1,0:T(8,128)(2,1)} custom-call(bf16[1,512,2048]{2,1,0:T(8,128)(2,1)} %query_ref.1, bf16[1,512,512]{2,1,0:T(8,128)(2,1)} %pair_ref.1, f32[1,512]{1,0:T(1,128)} %gain_ref.1), custom_call_target="tpu_custom_call" | custom-call | flops 2000000 | bytes 6000000 | tf_op jit(solution)/shard_map/pallas_call | solution.py:192
  4.4 5.0 %all-to-all-start.1 = ((bf16[4,512,768]{2,1,0:T(8,128)(2,1)}), bf16[4,512,768]{2,1,0:T(8,128)(2,1)S(1)}, u32[]{:S(2)}, u32[]{:S(2)}) async-start(bf16[4,512,768]{2,1,0:T(8,128)(2,1)} %shard_map.64), calls=%async_computation.1 | async-start | bytes 6291456 | tf_op jit(solution)/shard_map/all_to_all | solution.py:232
  14.1 2.9 dynamic-slice_bitcast_fusion
  21.1 23.8 %all-to-all-done.1.near_ref = bf16[4,512,768]{2,1,0:T(8,128)(2,1)S(1)} async-done(((bf16[4,512,768]{2,1,0:T(8,128)(2,1)}), bf16[4,512,768]{2,1,0:T(8,128)(2,1)S(1)}, u32[]{:S(2)}, u32[]{:S(2)}) %all-to-all-start.1) | async-done | bytes 3145760 | tf_op jit(solution)/shard_map/all_to_all | solution.py:232
  45.7 3.1 collective-permute-start.1
  56.3 28.5 %conditional.1 = (bf16[8,32,512]{2,1,0:T(8,128)(2,1)}) conditional(s32[]{:T(128)} %bitcast.14, () %tuple.16, (bf16[8,160,256]{2,1,0:T(8,128)(2,1)}, s32[1]{0:T(128)}, f32[96,128]{1,0:T(8,128)S(1)}, f32[96,128]{1,0:T(8,128)S(1)}, f32[128,96]{1,0:T(8,128)S(1)}) %tuple.37), branch_computations={%region_3.4_spmd, %region_4.5_spmd} | conditional | flops 10000000 | bytes 2310728 | solution.py:294
  56.3 27.2 %all_to_all.84.recv_ref = bf16[8,160,256]{2,1,0:T(8,128)(2,1)S(1)} all-to-all(bf16[8,160,256]{2,1,0:T(8,128)(2,1)} %get-tuple-element.19), channel_id=1, replica_groups=mesh['section'=4,'row'=4,'z'=8,'core'=2] {'z'}, dimensions={0} | all-to-all | bytes 1310720 | tf_op jit(solution)/shard_map/cond/branch_1_fun/all_to_all | solution.py:232
  89.3 15.5 %all_to_all.85 = bf16[8,32,512]{2,1,0:T(8,128)(2,1)S(1)} all-to-all(bf16[8,32,512]{2,1,0:T(8,128)(2,1)} %get-tuple-element.135), channel_id=1, replica_groups=mesh['section'=4,'row'=4,'z'=8,'core'=2] {'z'}, dimensions={0} | all-to-all | bytes 524288 | tf_op jit(solution)/shard_map/all_to_all | solution.py:232
  105.3 16.5 %all_to_all.86.recv_ref = bf16[16,16,1024]{2,1,0:T(8,128)(2,1)S(1)} all-to-all(bf16[16,16,1024]{2,1,0:T(8,128)(2,1)S(1)} %bitcast.50), channel_id=1, replica_groups=mesh['section'=4,'row'=4,'z'=8,'core'=2] {'section','row'}, dimensions={0} | all-to-all | bytes 1048576 | tf_op jit(solution)/shard_map/all_to_all | solution.py:232
  121.9 12.6 %all_to_all.87 = bf16[16,16,1024]{2,1,0:T(8,128)(2,1)S(1)} all-to-all(bf16[16,16,1024]{2,1,0:T(8,128)(2,1)S(1)} %get-tuple-element.99), channel_id=1, replica_groups=mesh['section'=4,'row'=4,'z'=8,'core'=2] {'section','row'}, dimensions={0} | all-to-all | bytes 1048576 | tf_op jit(solution)/shard_map/all_to_all | solution.py:232
  135.6 19.1 %all_to_all.88.recv_ref = bf16[8,160,256]{2,1,0:T(8,128)(2,1)S(1)} all-to-all(bf16[8,160,256]{2,1,0:T(8,128)(2,1)S(1)} %shard_map.68), channel_id=1, replica_groups=mesh['section'=4,'row'=4,'z'=8,'core'=2] {'z'}, dimensions={0} | all-to-all | bytes 1310720 | tf_op jit(solution)/shard_map/all_to_all | solution.py:232
  155.3 12.2 %all_to_all.89 = bf16[8,32,512]{2,1,0:T(8,128)(2,1)S(1)} all-to-all(bf16[8,32,512]{2,1,0:T(8,128)(2,1)S(1)} %shard_map.69), channel_id=1, replica_groups=mesh['section'=4,'row'=4,'z'=8,'core'=2] {'z'}, dimensions={0} | all-to-all | bytes 524288 | tf_op jit(solution)/shard_map/all_to_all | solution.py:232
  167.9 12.2 %all_to_all.90.recv_ref = bf16[16,16,1024]{2,1,0:T(8,128)(2,1)S(1)} all-to-all(bf16[16,16,1024]{2,1,0:T(8,128)(2,1)S(1)} %bitcast.51), channel_id=1, replica_groups=mesh['section'=4,'row'=4,'z'=8,'core'=2] {'section','row'}, dimensions={0} | all-to-all | bytes 1048576 | tf_op jit(solution)/shard_map/all_to_all | solution.py:232
  180.2 11.9 %all_to_all.91 = bf16[16,16,1024]{2,1,0:T(8,128)(2,1)S(1)} all-to-all(bf16[16,16,1024]{2,1,0:T(8,128)(2,1)S(1)} %get-tuple-element.102), channel_id=1, replica_groups=mesh['section'=4,'row'=4,'z'=8,'core'=2] {'section','row'}, dimensions={0} | all-to-all | bytes 1048576 | tf_op jit(solution)/shard_map/all_to_all | solution.py:232
  193.3 16.1 %all_to_all.92.recv_ref = bf16[8,160,256]{2,1,0:T(8,128)(2,1)S(1)} all-to-all(bf16[8,160,256]{2,1,0:T(8,128)(2,1)S(1)} %get-tuple-element.104), channel_id=1, replica_groups=mesh['section'=4,'row'=4,'z'=8,'core'=2] {'z'}, dimensions={0} | all-to-all | bytes 1310720 | tf_op jit(solution)/shard_map/all_to_all | solution.py:232
  210.0 11.7 %all_to_all.93 = bf16[8,32,512]{2,1,0:T(8,128)(2,1)S(1)} all-to-all(bf16[8,32,512]{2,1,0:T(8,128)(2,1)S(1)} %shard_map.73), channel_id=1, replica_groups=mesh['section'=4,'row'=4,'z'=8,'core'=2] {'z'}, dimensions={0} | all-to-all | bytes 524288 | tf_op jit(solution)/shard_map/all_to_all | solution.py:232
  222.2 11.9 %all_to_all.94.recv_ref = bf16[16,16,1024]{2,1,0:T(8,128)(2,1)S(1)} all-to-all(bf16[16,16,1024]{2,1,0:T(8,128)(2,1)S(1)} %bitcast.52), channel_id=1, replica_groups=mesh['section'=4,'row'=4,'z'=8,'core'=2] {'section','row'}, dimensions={0} | all-to-all | bytes 1048576 | tf_op jit(solution)/shard_map/all_to_all | solution.py:232
  234.2 13.8 %all_to_all.95 = bf16[16,16,1024]{2,1,0:T(8,128)(2,1)S(1)} all-to-all(bf16[16,16,1024]{2,1,0:T(8,128)(2,1)S(1)} %get-tuple-element.106), channel_id=1, replica_groups=mesh['section'=4,'row'=4,'z'=8,'core'=2] {'section','row'}, dimensions={0} | all-to-all | bytes 1048576 | tf_op jit(solution)/shard_map/all_to_all | solution.py:232
  249.2 15.9 %all_to_all.96.recv_ref = bf16[8,160,256]{2,1,0:T(8,128)(2,1)S(1)} all-to-all(bf16[8,160,256]{2,1,0:T(8,128)(2,1)S(1)} %get-tuple-element.109), channel_id=1, replica_groups=mesh['section'=4,'row'=4,'z'=8,'core'=2] {'z'}, dimensions={0} | all-to-all | bytes 1310720 | tf_op jit(solution)/shard_map/all_to_all | solution.py:232
  265.7 14.5 %all_to_all.97 = bf16[8,32,512]{2,1,0:T(8,128)(2,1)S(1)} all-to-all(bf16[8,32,512]{2,1,0:T(8,128)(2,1)S(1)} %shard_map.77), channel_id=1, replica_groups=mesh['section'=4,'row'=4,'z'=8,'core'=2] {'z'}, dimensions={0} | all-to-all | bytes 524288 | tf_op jit(solution)/shard_map/all_to_all | solution.py:232
  280.7 12.0 %all_to_all.98.recv_ref = bf16[16,16,1024]{2,1,0:T(8,128)(2,1)S(1)} all-to-all(bf16[16,16,1024]{2,1,0:T(8,128)(2,1)S(1)} %bitcast.49), channel_id=1, replica_groups=mesh['section'=4,'row'=4,'z'=8,'core'=2] {'section','row'}, dimensions={0} | all-to-all | bytes 1048576 | tf_op jit(solution)/shard_map/all_to_all | solution.py:232
  293.7 3.6 %all-to-all-start.16 = ((bf16[16,16,1024]{2,1,0:T(8,128)(2,1)}), bf16[16,16,1024]{2,1,0:T(8,128)(2,1)S(1)}, u32[]{:S(2)}, u32[]{:S(2)}) async-start(bf16[16,16,1024]{2,1,0:T(8,128)(2,1)} %get-tuple-element.111), calls=%async_computation.16 | async-start | bytes 1048576 | tf_op jit(solution)/shard_map/all_to_all | solution.py:232
  297.3 9.2 %all-to-all-done.16 = bf16[16,16,1024]{2,1,0:T(8,128)(2,1)S(1)} async-done(((bf16[16,16,1024]{2,1,0:T(8,128)(2,1)}), bf16[16,16,1024]{2,1,0:T(8,128)(2,1)S(1)}, u32[]{:S(2)}, u32[]{:S(2)}) %all-to-all-start.16) | async-done | bytes 524320 | tf_op jit(solution)/shard_map/all_to_all | solution.py:232
  306.6 18.2 %collective-permute-start.7 = (bf16[256,512]{1,0:T(8,128)(2,1)S(1)}, bf16[256,512]{1,0:T(8,128)(2,1)S(1)}, u32[]{:S(2)}, u32[]{:S(2)}) collective-permute-start(bf16[256,512]{1,0:T(8,128)(2,1)S(1)} %get-tuple-element.126), channel_id=1, source_target_pairs={{0,1},{1,0},{2,3},{3,2},{4,5},{5,4},{6,7},{7,6},{8,9},{9,8},{10,11... | collective-permute-start | bytes 786440 | tf_op jit(solution)/shard_map/ppermute | solution.py:228
  (67 shorter events, 32.4 us)
Async XLA Ops:
  4.4 8.9 %copy-start.5 = (s32[2,32]{1,0:T(2,128)S(1)}, s32[2,32]{1,0:T(2,128)}, u32[]{:S(2)}) copy-start(s32[2,32]{1,0:T(2,128)} %param.9) | copy-start | bytes 772
  4.4 40.5 %all-to-all-start.1 = ((bf16[4,512,768]{2,1,0:T(8,128)(2,1)}), bf16[4,512,768]{2,1,0:T(8,128)(2,1)S(1)}, u32[]{:S(2)}, u32[]{:S(2)}) async-start(bf16[4,512,768]{2,1,0:T(8,128)(2,1)} %shard_map.64), calls=%async_computation.1 | async-start | bytes 6291456 | tf_op jit(solution)/shard_map/all_to_all | solution.py:232
  11.2 7.4 %collective-permute-start = (bf16[256,512]{1,0:T(8,128)(2,1)}, bf16[256,512]{1,0:T(8,128)(2,1)}, u32[]{:S(2)}, u32[]{:S(2)}) collective-permute-start(bf16[256,512]{1,0:T(8,128)(2,1)} %get-tuple-element.128), channel_id=1, source_target_pairs={{0,1},{1,0},{2,3},{3,2},{4,5},{5,4},{6,7},{7,6},{8,9},{9,8},{10,11... | collective-permute-start | bytes 786440 | tf_op jit(solution)/shard_map/ppermute | solution.py:228
  45.7 7.6 %collective-permute-start.1 = (bf16[1,512,768]{2,1,0:T(8,128)(2,1)S(1)}, bf16[1,512,768]{2,1,0:T(8,128)(2,1)S(1)}, u32[]{:S(2)}, u32[]{:S(2)}) collective-permute-start(bf16[1,512,768]{2,1,0:T(8,128)(2,1)S(1)} %slice.21), channel_id=1, source_target_pairs={{0,1},{1,0},{2,3},{3,2},{4,5},{5,4},{6,7},{7,6},{8,9},{9,8},{10,11... | collective-permute-start | bytes 2359304 | tf_op jit(solution)/shard_map/ppermute | solution.py:228
  48.8 36.0 %collective-permute-start.2 = (bf16[512,512]{1,0:T(8,128)(2,1)}, bf16[512,512]{1,0:T(8,128)(2,1)}, u32[]{:S(2)}, u32[]{:S(2)}) collective-permute-start(bf16[512,512]{1,0:T(8,128)(2,1)} %get-tuple-element.76), channel_id=1, source_target_pairs={{0,64},{64,128},{128,192},{192,0},{1,65},{65,129},{129,193},{193,1... | collective-permute-start | bytes 1572872 | tf_op jit(solution)/shard_map/ppermute | solution.py:215
  49.1 35.8 %collective-permute-start.3 = (bf16[512,512]{1,0:T(8,128)(2,1)}, bf16[512,512]{1,0:T(8,128)(2,1)}, u32[]{:S(2)}, u32[]{:S(2)}) collective-permute-start(bf16[512,512]{1,0:T(8,128)(2,1)} %get-tuple-element.77), channel_id=1, source_target_pairs={{0,128},{64,192},{128,0},{192,64},{1,129},{65,193},{129,1},{193,65... | collective-permute-start | bytes 1572872 | tf_op jit(solution)/shard_map/ppermute | solution.py:215
  50.9 34.0 %collective-permute-start.4 = (bf16[512,512]{1,0:T(8,128)(2,1)}, bf16[512,512]{1,0:T(8,128)(2,1)}, u32[]{:S(2)}, u32[]{:S(2)}) collective-permute-start(bf16[512,512]{1,0:T(8,128)(2,1)} %get-tuple-element.78), channel_id=1, source_target_pairs={{0,192},{64,0},{128,64},{192,128},{1,193},{65,1},{129,65},{193,129... | collective-permute-start | bytes 1572872 | tf_op jit(solution)/shard_map/ppermute | solution.py:215
  53.3 1.0 copy-start
  54.3 2.0 copy-start.3
  84.9 49.6 %collective-permute-start.6 = (bf16[4,512,768]{2,1,0:T(8,128)(2,1)S(1)}, bf16[4,512,768]{2,1,0:T(8,128)(2,1)S(1)}, u32[]{:S(2)}, u32[]{:S(2)}) collective-permute-start(bf16[4,512,768]{2,1,0:T(8,128)(2,1)S(1)} %all-to-all-done.1.near_ref), channel_id=1, source_target_pairs={{0,1},{1,0},{2,3},{3,2},{4,5},{5,4},{6,7},{7,6},{8,9},{9,8},{10,11... | collective-permute-start | bytes 9437192 | tf_op jit(solution)/shard_map/ppermute | solution.py:228
  89.2 15.7 %collective-permute-start.5 = (bf16[4,512,512]{2,1,0:T(8,128)(2,1)S(1)}, bf16[4,512,512]{2,1,0:T(8,128)(2,1)S(1)}, u32[]{:S(2)}, u32[]{:S(2)}) collective-permute-start(bf16[4,512,512]{2,1,0:T(8,128)(2,1)S(1)} %pad_maximum_fusion.near_ref), channel_id=1, source_target_pairs={{0,1},{1,0},{2,3},{3,2},{4,5},{5,4},{6,7},{7,6},{8,9},{9,8},{10,11... | collective-permute-start | bytes 6291464 | tf_op jit(solution)/shard_map/ppermute | solution.py:228
  134.4 20.3 %copy-start.4 = (f32[96,128]{1,0:T(8,128)S(1)}, f32[96,128]{1,0:T(8,128)}, u32[]{:S(2)}) copy-start(f32[96,128]{1,0:T(8,128)} %pad_maximum_fusion.3.sin_ref) | copy-start | bytes 147460
  249.2 31.5 %copy-start.1 = (bf16[256,1024]{1,0:T(8,128)(2,1)}, bf16[256,1024]{1,0:T(8,128)(2,1)S(1)}, u32[]{:S(2)}) copy-start(bf16[256,1024]{1,0:T(8,128)(2,1)S(1)} %get-tuple-element.112) | copy-start | bytes 1572868
  280.7 25.7 %copy-start.2 = (bf16[256,1024]{1,0:T(8,128)(2,1)S(1)}, bf16[256,1024]{1,0:T(8,128)(2,1)}, u32[]{:S(2)}) copy-start(bf16[256,1024]{1,0:T(8,128)(2,1)} %copy-done.1) | copy-start | bytes 1572868
  293.7 12.7 %all-to-all-start.16 = ((bf16[16,16,1024]{2,1,0:T(8,128)(2,1)}), bf16[16,16,1024]{2,1,0:T(8,128)(2,1)S(1)}, u32[]{:S(2)}, u32[]{:S(2)}) async-start(bf16[16,16,1024]{2,1,0:T(8,128)(2,1)} %get-tuple-element.111), calls=%async_computation.16 | async-start | bytes 1048576 | tf_op jit(solution)/shard_map/all_to_all | solution.py:232
  306.6 19.3 %collective-permute-start.7 = (bf16[256,512]{1,0:T(8,128)(2,1)S(1)}, bf16[256,512]{1,0:T(8,128)(2,1)S(1)}, u32[]{:S(2)}, u32[]{:S(2)}) collective-permute-start(bf16[256,512]{1,0:T(8,128)(2,1)S(1)} %get-tuple-element.126), channel_id=1, source_target_pairs={{0,1},{1,0},{2,3},{3,2},{4,5},{5,4},{6,7},{7,6},{8,9},{9,8},{10,11... | collective-permute-start | bytes 786440 | tf_op jit(solution)/shard_map/ppermute | solution.py:228

commit v5 on v4

--- a/solution.py
+++ b/solution.py
@@ -140,7 +140,8 @@
         queries.append(rope(total[rows, lanes] * own_inverse, cosine[HALO:], sine[HALO:]))
     queries = jnp.concatenate(queries, axis=0)
     scores = lax.dot_general(queries, keys, (((1,), (1,)), ((), ())), preferred_element_type=f32)
-    raised = jnp.where(mask_ref[...] > 0.0, jnp.exp(scores * (HEAD**-0.5)), 0.0)
+    mask = jnp.concatenate([mask_ref[...]] * 4, axis=0)
+    raised = jnp.where(mask > 0.0, jnp.exp(scores * (HEAD**-0.5)), 0.0)
     weights = (raised / jnp.sum(raised, axis=1, keepdims=True)).astype(bf16)
     mixed = jnp.dot(weights, values, preferred_element_type=f32).astype(bf16)
     for d in range(CHIPS):
@@ -178,27 +179,27 @@
 
 
 def weigh_kernel(query_ref, pair_ref, gain_ref, out_ref):
-    rows = lax.broadcasted_iota(jnp.int32, (128, 128), 0)
-    cols = lax.broadcasted_iota(jnp.int32, (128, 128), 1)
+    rows = lax.broadcasted_iota(jnp.int32, (256, 256), 0)
+    cols = lax.broadcasted_iota(jnp.int32, (256, 256), 1)
     scale = jnp.sum(jnp.where(rows == cols, gain_ref[...], 0.0), axis=1, keepdims=True)
+    pair = (pair_ref[0].astype(f32) * scale).astype(bf16)
     for d in range(4):
         query = query_ref[0, :, 512 * d : 512 * (d + 1)]
-        pair = pair_ref[0, :, 256 * (d // 2) : 256 * (d // 2 + 1)]
         out_ref[d, :, :512] = (query.astype(f32) * scale).astype(bf16)
-        out_ref[d, :, 512:] = (pair.astype(f32) * scale).astype(bf16)
+        out_ref[d, :, 512:] = pair[:, 256 * (d // 2) : 256 * (d // 2 + 1)]
 
 
 def weigh(w_query, w_pair, gain):
     return pl.pallas_call(
         weigh_kernel,
         out_shape=jax.ShapeDtypeStruct((4, 512, 768), bf16),
-        grid=(4,),
+        grid=(2,),
         in_specs=[
-            pl.BlockSpec((1, 128, 2048), lambda i: (0, i, 0)),
-            pl.BlockSpec((1, 128, 512), lambda i: (0, i, 0)),
-            pl.BlockSpec((1, 128), lambda i: (0, i)),
+            pl.BlockSpec((1, 256, 2048), lambda i: (0, i, 0)),
+            pl.BlockSpec((1, 256, 512), lambda i: (0, i, 0)),
+            pl.BlockSpec((1, 256), lambda i: (0, i)),
         ],
-        out_specs=pl.BlockSpec((4, 128, 768), lambda i: (0, i, 0)),
+        out_specs=pl.BlockSpec((4, 256, 768), lambda i: (0, i, 0)),
         compiler_params=STREAM,
         cost_estimate=pl.CostEstimate(flops=2_000_000, bytes_accessed=6_000_000, transcendentals=0),
     )(w_query, w_pair, gain)
@@ -258,7 +259,7 @@
     cosine = jnp.concatenate([cosine, cosine], axis=1)
     sine = jnp.concatenate([-sine, sine], axis=1)
     allowed = (seg_window[HALO:, None] == seg_window[None, :]) & (pos_window[None, :] <= pos_window[HALO:, None])
-    mask = jnp.tile(allowed.astype(f32), (4, 1))
+    mask = allowed.astype(f32)
     place_arg = place.reshape(1).astype(jnp.int32)
 
     def attend(recv):
@@ -273,25 +274,32 @@
 
     is_section = [(section == layer).astype(jnp.int32).reshape(1) for layer in range(LAYERS)]
     is_turn = [[turn[layer] == k for k in range(4)] for layer in range(LAYERS)]
-    near_in, x, held, cosine, sine, mask, place_arg, is_section, is_turn, blocks_out = lax.optimization_barrier(
-        (near_in, x, held, cosine, sine, mask, place_arg, is_section, is_turn, blocks_out)
+    is_first = lengths[0, 0] > 0
+    is_last = section == LAYERS - 1
+    is_core = core == 0
+    near_in, x, held, cosine, sine, mask, place_arg, is_first, is_last, is_core, is_section, is_turn, blocks_out = (
+        lax.optimization_barrier(
+            (near_in, x, held, cosine, sine, mask, place_arg, is_first, is_last, is_core, is_section, is_turn, blocks_out)
+        )
     )
-    far_first = swap(near_in[:1])
     def mix(packed):
         return attend(exchange(packed, "z"))
 
+    def begin(x, near_in, far_first):
+        (packed,) = project(x, near_in, far_first, 0, 0, None, None)
+        return mix(packed)
+
+    far_first = swap(near_in[:1])
     moved_out = [blocks_out[0]] + [rotated(blocks_out[k], k) for k in range(1, 4)]
     kept = None
     for layer in range(LAYERS):
-        if layer == 0:
-            (packed,) = project(x, near_in, far_first, 0, 0, None, None)
-        elif layer == 1:
+        if layer == 1:
             (packed,) = project(x, near_in, far_in, layer, layer, None, None)
             kept = x
-        else:
+        elif layer > 1:
             packed, kept = project(x, near_in, far_in, layer, layer, kept, is_section[layer - 1])
         if layer == 0:
-            copies = lax.cond(lengths[0, 0] > 0, mix, lambda value: jnp.zeros((CHIPS, OWN, 512), bf16), packed)
+            copies = lax.cond(is_first, begin, lambda *_: jnp.zeros((CHIPS, OWN, 512), bf16), x, near_in, far_first)
             copies, moved_out, rest = lax.optimization_barrier((copies, moved_out, near_in))
             near_out = jnp.stack([choose(moved_out, is_turn[each]) for each in range(LAYERS)])
             copies, near_out = lax.optimization_barrier((copies, near_out))
@@ -309,10 +317,10 @@
         )
         x = exchange(copies, ("section", "row")).reshape(TOK, 1024)
 
-    kept = jnp.where(is_section[LAYERS - 1] == 1, x, kept)
+    kept = jnp.where(is_last, x, kept)
     ours = kept[:, :512]
     other = swap(kept[:, 512:])
-    final = jnp.where(core == 0, jnp.stack([ours, other]), jnp.stack([other, ours]))
+    final = jnp.where(is_core, jnp.stack([ours, other]), jnp.stack([other, ours]))
     return final[None]
 
 

time: 328 us -> 323 us (0.985)
  blocking collectives: 223 us -> 235 us
  waiting for transfers between devices: 34.2 us -> 25.1 us
    all_to_all x15 -> x16, blocking collectives: 223 us -> 235 us  [exchange(): return lax.all_to_all(value, axis, 0, 0, tiled=True)]
    all_to_all x2 -> x1, waiting for transfers between devices: 33 us -> 23.9 us  [exchange(): return lax.all_to_all(value, axis, 0, 0, tiled=True)]
    all_to_all x2 -> x1, starting transfers between devices: 8.55 us -> 4.97 us  [exchange(): return lax.all_to_all(value, axis, 0, 0, tiled=True)]
  transfers between devices with their start and end apart: 10 -> 9, of which waited for: 3 -> 2; matrix products, arithmetic and copies ran while one was open for 4% -> 3% of each run, Pallas kernels for 1% -> 1%
where the time goes in v5:
time: 323 us; the launch traced here: 322 us
  blocking collectives  235 us (73%)
  starting transfers between devices  33.8 us (10%)
  waiting for transfers between devices  25.1 us (8%)
  Pallas kernels  14.1 us (4%)
  local copies, waits for them, and re-layouts  7.07 us (2%)
  other arithmetic  6.3 us (2%)
    all_to_all x16, blocking collectives, exchange(): return lax.all_to_all(value, axis, 0, 0, tiled=True)  235 us
    ppermute x5, starting transfers between devices, swap(): return lax.ppermute(value, 'core', [(0, 1), (1, 0)])  26.1 us
    all_to_all x1, waiting for transfers between devices, exchange(): return lax.all_to_all(value, axis, 0, 0, tiled=True)  23.9 us
  transfers between devices with their start and end apart: 9, of which 2 were waited for; matrix products, arithmetic and copies ran while one was open for 3% of the time, Pallas kernels for 1%

profile of v5, /device:TPU:1, one launch (start us, length us, event | category | flops | bytes accessed | tf_op | source)
XLA Modules:
  0.0 321.8 jit_solution(9821673496683593030)
XLA Ops:
  0.0 3.3 %shard_map.64 = bf16[4,512,768]{2,1,0:T(8,128)(2,1)} custom-call(bf16[1,512,2048]{2,1,0:T(8,128)(2,1)} %query_ref.1, bf16[1,512,512]{2,1,0:T(8,128)(2,1)} %pair_ref.1, f32[1,512]{1,0:T(1,128)} %gain_ref.1), custom_call_target="tpu_custom_call" | custom-call | flops 2000000 | bytes 6000000 | tf_op jit(solution)/shard_map/pallas_call | solution.py:193
  3.3 5.0 %all-to-all-start.1 = ((bf16[4,512,768]{2,1,0:T(8,128)(2,1)}), bf16[4,512,768]{2,1,0:T(8,128)(2,1)S(1)}, u32[]{:S(2)}, u32[]{:S(2)}) async-start(bf16[4,512,768]{2,1,0:T(8,128)(2,1)} %shard_map.64), calls=%async_computation.1 | async-start | bytes 6291456 | tf_op jit(solution)/shard_map/all_to_all | solution.py:233
  13.0 2.9 dynamic-slice_bitcast_fusion
  19.9 23.9 %all-to-all-done.1.near_ref = bf16[4,512,768]{2,1,0:T(8,128)(2,1)S(1)} async-done(((bf16[4,512,768]{2,1,0:T(8,128)(2,1)}), bf16[4,512,768]{2,1,0:T(8,128)(2,1)S(1)}, u32[]{:S(2)}, u32[]{:S(2)}) %all-to-all-start.1) | async-done | bytes 3145760 | tf_op jit(solution)/shard_map/all_to_all | solution.py:233
  44.7 3.0 collective-permute-start.1
  50.4 30.0 %conditional.1 = (bf16[8,32,512]{2,1,0:T(8,128)(2,1)S(1)}) conditional(s32[]{:T(128)} %convert_element_type.19, () %tuple.16, (bf16[256,1024]{1,0:T(8,128)(2,1)}, bf16[4,512,768]{2,1,0:T(8,128)(2,1)S(1)}, bf16[1,512,768]{2,1,0:T(8,128)(2,1)}, s32[1]{0:T(128)}, f32[96,128]{1,0:T(8,128)S(1)}, /*index=5*/f32[96,128]{1,0:T(8,128)S(1)}, ...), branch_computations={%region_3.4_spmd, %region_4.5_spmd} | conditional | flops 546870912 | bytes 5310728 | solution.py:302
  50.4 2.3 branch_1_fun.2
  52.8 27.1 %all_to_all.84.recv_ref = bf16[8,160,256]{2,1,0:T(8,128)(2,1)S(1)} all-to-all(bf16[8,160,256]{2,1,0:T(8,128)(2,1)S(1)} %branch_1_fun.2), channel_id=1, replica_groups=mesh['section'=4,'row'=4,'z'=8,'core'=2] {'z'}, dimensions={0} | all-to-all | bytes 1310720 | tf_op jit(solution)/shard_map/cond/branch_1_fun/all_to_all | solution.py:233
  85.4 14.8 %all_to_all.85 = bf16[8,32,512]{2,1,0:T(8,128)(2,1)S(1)} all-to-all(bf16[8,32,512]{2,1,0:T(8,128)(2,1)S(1)} %copy-done.1), channel_id=1, replica_groups=mesh['section'=4,'row'=4,'z'=8,'core'=2] {'z'}, dimensions={0} | all-to-all | bytes 524288 | tf_op jit(solution)/shard_map/all_to_all | solution.py:233
  100.6 16.5 %all_to_all.86.recv_ref = bf16[16,16,1024]{2,1,0:T(8,128)(2,1)S(1)} all-to-all(bf16[16,16,1024]{2,1,0:T(8,128)(2,1)S(1)} %bitcast.47), channel_id=1, replica_groups=mesh['section'=4,'row'=4,'z'=8,'core'=2] {'section','row'}, dimensions={0} | all-to-all | bytes 1048576 | tf_op jit(solution)/shard_map/all_to_all | solution.py:233
  117.2 12.7 %all_to_all.87 = bf16[16,16,1024]{2,1,0:T(8,128)(2,1)S(1)} all-to-all(bf16[16,16,1024]{2,1,0:T(8,128)(2,1)S(1)} %get-tuple-element.109), channel_id=1, replica_groups=mesh['section'=4,'row'=4,'z'=8,'core'=2] {'section','row'}, dimensions={0} | all-to-all | bytes 1048576 | tf_op jit(solution)/shard_map/all_to_all | solution.py:233
  131.1 19.2 %all_to_all.88.recv_ref = bf16[8,160,256]{2,1,0:T(8,128)(2,1)S(1)} all-to-all(bf16[8,160,256]{2,1,0:T(8,128)(2,1)S(1)} %shard_map.67), channel_id=1, replica_groups=mesh['section'=4,'row'=4,'z'=8,'core'=2] {'z'}, dimensions={0} | all-to-all | bytes 1310720 | tf_op jit(solution)/shard_map/all_to_all | solution.py:233
  150.8 12.2 %all_to_all.89 = bf16[8,32,512]{2,1,0:T(8,128)(2,1)S(1)} all-to-all(bf16[8,32,512]{2,1,0:T(8,128)(2,1)S(1)} %shard_map.68), channel_id=1, replica_groups=mesh['section'=4,'row'=4,'z'=8,'core'=2] {'z'}, dimensions={0} | all-to-all | bytes 524288 | tf_op jit(solution)/shard_map/all_to_all | solution.py:233
  163.4 12.3 %all_to_all.90.recv_ref = bf16[16,16,1024]{2,1,0:T(8,128)(2,1)S(1)} all-to-all(bf16[16,16,1024]{2,1,0:T(8,128)(2,1)S(1)} %bitcast.48), channel_id=1, replica_groups=mesh['section'=4,'row'=4,'z'=8,'core'=2] {'section','row'}, dimensions={0} | all-to-all | bytes 1048576 | tf_op jit(solution)/shard_map/all_to_all | solution.py:233
  175.8 11.9 %all_to_all.91 = bf16[16,16,1024]{2,1,0:T(8,128)(2,1)S(1)} all-to-all(bf16[16,16,1024]{2,1,0:T(8,128)(2,1)S(1)} %get-tuple-element.112), channel_id=1, replica_groups=mesh['section'=4,'row'=4,'z'=8,'core'=2] {'section','row'}, dimensions={0} | all-to-all | bytes 1048576 | tf_op jit(solution)/shard_map/all_to_all | solution.py:233
  189.0 16.1 %all_to_all.92.recv_ref = bf16[8,160,256]{2,1,0:T(8,128)(2,1)S(1)} all-to-all(bf16[8,160,256]{2,1,0:T(8,128)(2,1)S(1)} %get-tuple-element.114), channel_id=1, replica_groups=mesh['section'=4,'row'=4,'z'=8,'core'=2] {'z'}, dimensions={0} | all-to-all | bytes 1310720 | tf_op jit(solution)/shard_map/all_to_all | solution.py:233
  205.7 11.7 %all_to_all.93 = bf16[8,32,512]{2,1,0:T(8,128)(2,1)S(1)} all-to-all(bf16[8,32,512]{2,1,0:T(8,128)(2,1)S(1)} %shard_map.72), channel_id=1, replica_groups=mesh['section'=4,'row'=4,'z'=8,'core'=2] {'z'}, dimensions={0} | all-to-all | bytes 524288 | tf_op jit(solution)/shard_map/all_to_all | solution.py:233
  217.8 11.9 %all_to_all.94.recv_ref = bf16[16,16,1024]{2,1,0:T(8,128)(2,1)S(1)} all-to-all(bf16[16,16,1024]{2,1,0:T(8,128)(2,1)S(1)} %bitcast.49), channel_id=1, replica_groups=mesh['section'=4,'row'=4,'z'=8,'core'=2] {'section','row'}, dimensions={0} | all-to-all | bytes 1048576 | tf_op jit(solution)/shard_map/all_to_all | solution.py:233
  229.9 13.8 %all_to_all.95 = bf16[16,16,1024]{2,1,0:T(8,128)(2,1)S(1)} all-to-all(bf16[16,16,1024]{2,1,0:T(8,128)(2,1)S(1)} %get-tuple-element.116), channel_id=1, replica_groups=mesh['section'=4,'row'=4,'z'=8,'core'=2] {'section','row'}, dimensions={0} | all-to-all | bytes 1048576 | tf_op jit(solution)/shard_map/all_to_all | solution.py:233
  244.9 15.9 %all_to_all.96.recv_ref = bf16[8,160,256]{2,1,0:T(8,128)(2,1)S(1)} all-to-all(bf16[8,160,256]{2,1,0:T(8,128)(2,1)S(1)} %get-tuple-element.119), channel_id=1, replica_groups=mesh['section'=4,'row'=4,'z'=8,'core'=2] {'z'}, dimensions={0} | all-to-all | bytes 1310720 | tf_op jit(solution)/shard_map/all_to_all | solution.py:233
  261.4 14.6 %all_to_all.97 = bf16[8,32,512]{2,1,0:T(8,128)(2,1)S(1)} all-to-all(bf16[8,32,512]{2,1,0:T(8,128)(2,1)S(1)} %shard_map.76), channel_id=1, replica_groups=mesh['section'=4,'row'=4,'z'=8,'core'=2] {'z'}, dimensions={0} | all-to-all | bytes 524288 | tf_op jit(solution)/shard_map/all_to_all | solution.py:233
  276.4 11.9 %all_to_all.98.recv_ref = bf16[16,16,1024]{2,1,0:T(8,128)(2,1)S(1)} all-to-all(bf16[16,16,1024]{2,1,0:T(8,128)(2,1)S(1)} %bitcast.46), channel_id=1, replica_groups=mesh['section'=4,'row'=4,'z'=8,'core'=2] {'section','row'}, dimensions={0} | all-to-all | bytes 1048576 | tf_op jit(solution)/shard_map/all_to_all | solution.py:233
  289.0 11.9 %all_to_all.99 = bf16[16,16,1024]{2,1,0:T(8,128)(2,1)S(1)} all-to-all(bf16[16,16,1024]{2,1,0:T(8,128)(2,1)S(1)} %get-tuple-element.121), channel_id=1, replica_groups=mesh['section'=4,'row'=4,'z'=8,'core'=2] {'section','row'}, dimensions={0} | all-to-all | bytes 1048576 | tf_op jit(solution)/shard_map/all_to_all | solution.py:233
  301.1 18.7 %collective-permute-start.7 = (bf16[256,512]{1,0:T(8,128)(2,1)S(1)}, bf16[256,512]{1,0:T(8,128)(2,1)S(1)}, u32[]{:S(2)}, u32[]{:S(2)}) collective-permute-start(bf16[256,512]{1,0:T(8,128)(2,1)S(1)} %get-tuple-element.136), channel_id=1, source_target_pairs={{0,1},{1,0},{2,3},{3,2},{4,5},{5,4},{6,7},{7,6},{8,9},{9,8},{10,11... | collective-permute-start | bytes 786440 | tf_op jit(solution)/shard_map/ppermute | solution.py:229
  (59 shorter events, 27.2 us)
Async XLA Ops:
  3.3 8.9 %copy-start.2 = (s32[2,32]{1,0:T(2,128)S(1)}, s32[2,32]{1,0:T(2,128)}, u32[]{:S(2)}) copy-start(s32[2,32]{1,0:T(2,128)} %param.9) | copy-start | bytes 772
  3.3 40.5 %all-to-all-start.1 = ((bf16[4,512,768]{2,1,0:T(8,128)(2,1)}), bf16[4,512,768]{2,1,0:T(8,128)(2,1)S(1)}, u32[]{:S(2)}, u32[]{:S(2)}) async-start(bf16[4,512,768]{2,1,0:T(8,128)(2,1)} %shard_map.64), calls=%async_computation.1 | async-start | bytes 6291456 | tf_op jit(solution)/shard_map/all_to_all | solution.py:233
  10.0 7.3 %collective-permute-start = (bf16[256,512]{1,0:T(8,128)(2,1)}, bf16[256,512]{1,0:T(8,128)(2,1)}, u32[]{:S(2)}, u32[]{:S(2)}) collective-permute-start(bf16[256,512]{1,0:T(8,128)(2,1)} %get-tuple-element.138), channel_id=1, source_target_pairs={{0,1},{1,0},{2,3},{3,2},{4,5},{5,4},{6,7},{7,6},{8,9},{9,8},{10,11... | collective-permute-start | bytes 786440 | tf_op jit(solution)/shard_map/ppermute | solution.py:229
  44.7 5.7 %collective-permute-start.1 = (bf16[1,512,768]{2,1,0:T(8,128)(2,1)}, bf16[1,512,768]{2,1,0:T(8,128)(2,1)}, u32[]{:S(2)}, u32[]{:S(2)}) collective-permute-start(bf16[1,512,768]{2,1,0:T(8,128)(2,1)} %slice.21), channel_id=1, source_target_pairs={{0,1},{1,0},{2,3},{3,2},{4,5},{5,4},{6,7},{7,6},{8,9},{9,8},{10,11... | collective-permute-start | bytes 2359304 | tf_op jit(solution)/shard_map/ppermute | solution.py:229
  47.7 32.7 %collective-permute-start.2 = (bf16[512,512]{1,0:T(8,128)(2,1)}, bf16[512,512]{1,0:T(8,128)(2,1)}, u32[]{:S(2)}, u32[]{:S(2)}) collective-permute-start(bf16[512,512]{1,0:T(8,128)(2,1)} %get-tuple-element.86), channel_id=1, source_target_pairs={{0,64},{64,128},{128,192},{192,0},{1,65},{65,129},{129,193},{193,1... | collective-permute-start | bytes 1572872 | tf_op jit(solution)/shard_map/ppermute | solution.py:216
  48.0 32.4 %collective-permute-start.3 = (bf16[512,512]{1,0:T(8,128)(2,1)}, bf16[512,512]{1,0:T(8,128)(2,1)}, u32[]{:S(2)}, u32[]{:S(2)}) collective-permute-start(bf16[512,512]{1,0:T(8,128)(2,1)} %get-tuple-element.87), channel_id=1, source_target_pairs={{0,128},{64,192},{128,0},{192,64},{1,129},{65,193},{129,1},{193,65... | collective-permute-start | bytes 1572872 | tf_op jit(solution)/shard_map/ppermute | solution.py:216
  49.8 30.7 %collective-permute-start.4 = (bf16[512,512]{1,0:T(8,128)(2,1)}, bf16[512,512]{1,0:T(8,128)(2,1)}, u32[]{:S(2)}, u32[]{:S(2)}) collective-permute-start(bf16[512,512]{1,0:T(8,128)(2,1)} %get-tuple-element.88), channel_id=1, source_target_pairs={{0,192},{64,0},{128,64},{192,128},{1,193},{65,1},{129,65},{193,129... | collective-permute-start | bytes 1572872 | tf_op jit(solution)/shard_map/ppermute | solution.py:216
  80.4 4.0 %copy-start = (bf16[8,32,512]{2,1,0:T(8,128)(2,1)}, bf16[8,32,512]{2,1,0:T(8,128)(2,1)S(1)}, u32[]{:S(2)}) copy-start(bf16[8,32,512]{2,1,0:T(8,128)(2,1)S(1)} %get-tuple-element.146) | copy-start | bytes 786436
  80.5 49.5 %collective-permute-start.6 = (bf16[4,512,768]{2,1,0:T(8,128)(2,1)S(1)}, bf16[4,512,768]{2,1,0:T(8,128)(2,1)S(1)}, u32[]{:S(2)}, u32[]{:S(2)}) collective-permute-start(bf16[4,512,768]{2,1,0:T(8,128)(2,1)S(1)} %all-to-all-done.1.near_ref), channel_id=1, source_target_pairs={{0,1},{1,0},{2,3},{3,2},{4,5},{5,4},{6,7},{7,6},{8,9},{9,8},{10,11... | collective-permute-start | bytes 9437192 | tf_op jit(solution)/shard_map/ppermute | solution.py:229
  84.4 1.0 copy-start.1
  84.7 15.5 %collective-permute-start.5 = (bf16[4,512,512]{2,1,0:T(8,128)(2,1)S(1)}, bf16[4,512,512]{2,1,0:T(8,128)(2,1)S(1)}, u32[]{:S(2)}, u32[]{:S(2)}) collective-permute-start(bf16[4,512,512]{2,1,0:T(8,128)(2,1)S(1)} %pad_maximum_fusion.near_ref), channel_id=1, source_target_pairs={{0,1},{1,0},{2,3},{3,2},{4,5},{5,4},{6,7},{7,6},{8,9},{9,8},{10,11... | collective-permute-start | bytes 6291464 | tf_op jit(solution)/shard_map/ppermute | solution.py:229
  301.1 19.9 %collective-permute-start.7 = (bf16[256,512]{1,0:T(8,128)(2,1)S(1)}, bf16[256,512]{1,0:T(8,128)(2,1)S(1)}, u32[]{:S(2)}, u32[]{:S(2)}) collective-permute-start(bf16[256,512]{1,0:T(8,128)(2,1)S(1)} %get-tuple-element.136), channel_id=1, source_target_pairs={{0,1},{1,0},{2,3},{3,2},{4,5},{5,4},{6,7},{7,6},{8,9},{9,8},{10,11... | collective-permute-start | bytes 786440 | tf_op jit(solution)/shard_map/ppermute | solution.py:229

commit v6 on v5

--- a/solution.py
+++ b/solution.py
@@ -25,6 +25,7 @@
 f32 = jnp.float32
 VMEM = pl.BlockSpec(memory_space=pltpu.VMEM)
 PARAMS = pltpu.CompilerParams(vmem_limit_bytes=12 * 1024 * 1024)
+PROJECT = pltpu.CompilerParams(vmem_limit_bytes=24 * 1024 * 1024)
 STREAM = pltpu.CompilerParams(vmem_limit_bytes=56 * 1024 * 1024)
 
 
@@ -41,56 +42,34 @@
 
 
 def project(x, near, far, layer, far_layer, kept, flag):
-    rows = 256
     outs = [jax.ShapeDtypeStruct((CHIPS, PACK, 256), bf16)]
     args = [x, near, far]
-    in_specs = [
-        VMEM,
-        pl.BlockSpec((1, rows, 768), lambda i: (layer, i, 0)),
-        pl.BlockSpec((1, rows, 768), lambda i: (far_layer, i, 0)),
-    ]
+    in_specs = [VMEM] * 3
     if kept is not None:
         outs.append(jax.ShapeDtypeStruct(kept.shape, bf16))
         args += [kept, flag]
         in_specs += [VMEM, pl.BlockSpec(memory_space=pltpu.SMEM)]
+
+    def kernel(x_ref, near_ref, far_ref, *refs):
+        x = x_ref[...]
+        half = x.shape[1] // 2
+        y = jnp.dot(x[:, :half], near_ref[layer], preferred_element_type=f32)
+        y = y + jnp.dot(x[:, half:], far_ref[far_layer], preferred_element_type=f32)
+        if kept is None:
+            (out_ref,) = refs
+        else:
+            kept_ref, flag_ref, out_ref, next_ref = refs
+            next_ref[...] = jnp.where(flag_ref[0] == 1, x, kept_ref[...])
+        pack(x, y, out_ref)
+
     return pl.pallas_call(
-        project_kernel if kept is not None else first_project_kernel,
+        kernel,
         out_shape=outs,
-        grid=(2,),
         in_specs=in_specs,
         out_specs=[VMEM] * len(outs),
-        scratch_shapes=[pltpu.VMEM((TOK, 768), f32)],
-        compiler_params=PARAMS,
+        compiler_params=PROJECT,
         cost_estimate=pl.CostEstimate(flops=2 * 256 * 1024 * 1024, bytes_accessed=3_000_000, transcendentals=0),
     )(*args)
-
-
-def first_project_kernel(x_ref, near_ref, far_ref, out_ref, sum_ref):
-    project_step(x_ref, near_ref, far_ref, out_ref, sum_ref)
-
-
-def project_kernel(x_ref, near_ref, far_ref, kept_ref, flag_ref, out_ref, next_ref, sum_ref):
-    project_step(x_ref, near_ref, far_ref, out_ref, sum_ref)
-
-    @pl.when(pl.program_id(0) == 0)
-    def _():
-        next_ref[...] = jnp.where(flag_ref[0] == 1, x_ref[...], kept_ref[...])
-
-
-def project_step(x_ref, near_ref, far_ref, out_ref, sum_ref):
-    step = pl.program_id(0)
-    near_x = x_ref[:, pl.ds(pl.multiple_of(step * 256, 256), 256)]
-    far_x = x_ref[:, pl.ds(pl.multiple_of(512 + step * 256, 256), 256)]
-    part = jnp.dot(near_x, near_ref[0], preferred_element_type=f32)
-    part = part + jnp.dot(far_x, far_ref[0], preferred_element_type=f32)
-
-    @pl.when(step == 0)
-    def _():
-        sum_ref[...] = part
-
-    @pl.when(step == 1)
-    def _():
-        pack(x_ref[...], sum_ref[...] + part, out_ref)
 
 
 def pack(x, y, out_ref):

time: 323 us -> 321 us (level)
  no operation moved by 1% of the time
where the time goes in v6:
time: 321 us; the launch traced here: 320 us
  blocking collectives  235 us (73%)
  starting transfers between devices  33.8 us (11%)
  waiting for transfers between devices  25.1 us (8%)
  Pallas kernels  12.4 us (4%)
  local copies, waits for them, and re-layouts  7.07 us (2%)
  other arithmetic  6.3 us (2%)
    all_to_all x16, blocking collectives, exchange(): return lax.all_to_all(value, axis, 0, 0, tiled=True)  235 us
    ppermute x5, starting transfers between devices, swap(): return lax.ppermute(value, 'core', [(0, 1), (1, 0)])  26.1 us
    all_to_all x1, waiting for transfers between devices, exchange(): return lax.all_to_all(value, axis, 0, 0, tiled=True)  23.9 us
  transfers between devices with their start and end apart: 9, of which 2 were waited for; matrix products, arithmetic and copies ran while one was open for 3% of the time, Pallas kernels for 1%

profile of v6, /device:TPU:1, one launch (start us, length us, event | category | flops | bytes accessed | tf_op | source)
XLA Modules:
  0.0 320.1 jit_solution(11541528344763199206)
XLA Ops:
  0.0 3.3 %shard_map.64 = bf16[4,512,768]{2,1,0:T(8,128)(2,1)} custom-call(bf16[1,512,2048]{2,1,0:T(8,128)(2,1)} %query_ref.1, bf16[1,512,512]{2,1,0:T(8,128)(2,1)} %pair_ref.1, f32[1,512]{1,0:T(1,128)} %gain_ref.1), custom_call_target="tpu_custom_call" | custom-call | flops 2000000 | bytes 6000000 | tf_op jit(solution)/shard_map/pallas_call | solution.py:172
  3.3 5.0 %all-to-all-start.1 = ((bf16[4,512,768]{2,1,0:T(8,128)(2,1)}), bf16[4,512,768]{2,1,0:T(8,128)(2,1)S(1)}, u32[]{:S(2)}, u32[]{:S(2)}) async-start(bf16[4,512,768]{2,1,0:T(8,128)(2,1)} %shard_map.64), calls=%async_computation.1 | async-start | bytes 6291456 | tf_op jit(solution)/shard_map/all_to_all | solution.py:212
  13.0 2.9 dynamic-slice_bitcast_fusion
  19.9 23.9 %all-to-all-done.1.near_ref = bf16[4,512,768]{2,1,0:T(8,128)(2,1)S(1)} async-done(((bf16[4,512,768]{2,1,0:T(8,128)(2,1)}), bf16[4,512,768]{2,1,0:T(8,128)(2,1)S(1)}, u32[]{:S(2)}, u32[]{:S(2)}) %all-to-all-start.1) | async-done | bytes 3145760 | tf_op jit(solution)/shard_map/all_to_all | solution.py:212
  44.7 3.0 collective-permute-start.1
  50.4 29.7 %conditional.1 = (bf16[8,32,512]{2,1,0:T(8,128)(2,1)S(1)}) conditional(s32[]{:T(128)} %convert_element_type.19, () %tuple.16, (bf16[256,1024]{1,0:T(8,128)(2,1)}, bf16[4,512,768]{2,1,0:T(8,128)(2,1)S(1)}, bf16[1,512,768]{2,1,0:T(8,128)(2,1)}, s32[1]{0:T(128)}, f32[96,128]{1,0:T(8,128)S(1)}, /*index=5*/f32[96,128]{1,0:T(8,128)S(1)}, ...), branch_computations={%region_3.4_spmd, %region_4.5_spmd} | conditional | flops 546870912 | bytes 5310728 | solution.py:281
  52.4 27.1 %all_to_all.84.recv_ref = bf16[8,160,256]{2,1,0:T(8,128)(2,1)S(1)} all-to-all(bf16[8,160,256]{2,1,0:T(8,128)(2,1)S(1)} %branch_1_fun.2), channel_id=1, replica_groups=mesh['section'=4,'row'=4,'z'=8,'core'=2] {'z'}, dimensions={0} | all-to-all | bytes 1310720 | tf_op jit(solution)/shard_map/cond/branch_1_fun/all_to_all | solution.py:212
  80.2 2.2 collective-permute-start.6
  85.1 14.8 %all_to_all.85 = bf16[8,32,512]{2,1,0:T(8,128)(2,1)S(1)} all-to-all(bf16[8,32,512]{2,1,0:T(8,128)(2,1)S(1)} %copy-done.1), channel_id=1, replica_groups=mesh['section'=4,'row'=4,'z'=8,'core'=2] {'z'}, dimensions={0} | all-to-all | bytes 524288 | tf_op jit(solution)/shard_map/all_to_all | solution.py:212
  100.3 16.5 %all_to_all.86.recv_ref = bf16[16,16,1024]{2,1,0:T(8,128)(2,1)S(1)} all-to-all(bf16[16,16,1024]{2,1,0:T(8,128)(2,1)S(1)} %bitcast.47), channel_id=1, replica_groups=mesh['section'=4,'row'=4,'z'=8,'core'=2] {'section','row'}, dimensions={0} | all-to-all | bytes 1048576 | tf_op jit(solution)/shard_map/all_to_all | solution.py:212
  116.9 12.7 %all_to_all.87 = bf16[16,16,1024]{2,1,0:T(8,128)(2,1)S(1)} all-to-all(bf16[16,16,1024]{2,1,0:T(8,128)(2,1)S(1)} %get-tuple-element.109), channel_id=1, replica_groups=mesh['section'=4,'row'=4,'z'=8,'core'=2] {'section','row'}, dimensions={0} | all-to-all | bytes 1048576 | tf_op jit(solution)/shard_map/all_to_all | solution.py:212
  130.4 19.2 %all_to_all.88.recv_ref = bf16[8,160,256]{2,1,0:T(8,128)(2,1)S(1)} all-to-all(bf16[8,160,256]{2,1,0:T(8,128)(2,1)S(1)} %shard_map.67), channel_id=1, replica_groups=mesh['section'=4,'row'=4,'z'=8,'core'=2] {'z'}, dimensions={0} | all-to-all | bytes 1310720 | tf_op jit(solution)/shard_map/all_to_all | solution.py:212
  150.1 12.2 %all_to_all.89 = bf16[8,32,512]{2,1,0:T(8,128)(2,1)S(1)} all-to-all(bf16[8,32,512]{2,1,0:T(8,128)(2,1)S(1)} %shard_map.68), channel_id=1, replica_groups=mesh['section'=4,'row'=4,'z'=8,'core'=2] {'z'}, dimensions={0} | all-to-all | bytes 524288 | tf_op jit(solution)/shard_map/all_to_all | solution.py:212
  162.7 12.3 %all_to_all.90.recv_ref = bf16[16,16,1024]{2,1,0:T(8,128)(2,1)S(1)} all-to-all(bf16[16,16,1024]{2,1,0:T(8,128)(2,1)S(1)} %bitcast.48), channel_id=1, replica_groups=mesh['section'=4,'row'=4,'z'=8,'core'=2] {'section','row'}, dimensions={0} | all-to-all | bytes 1048576 | tf_op jit(solution)/shard_map/all_to_all | solution.py:212
  175.1 11.9 %all_to_all.91 = bf16[16,16,1024]{2,1,0:T(8,128)(2,1)S(1)} all-to-all(bf16[16,16,1024]{2,1,0:T(8,128)(2,1)S(1)} %get-tuple-element.112), channel_id=1, replica_groups=mesh['section'=4,'row'=4,'z'=8,'core'=2] {'section','row'}, dimensions={0} | all-to-all | bytes 1048576 | tf_op jit(solution)/shard_map/all_to_all | solution.py:212
  187.7 16.1 %all_to_all.92.recv_ref = bf16[8,160,256]{2,1,0:T(8,128)(2,1)S(1)} all-to-all(bf16[8,160,256]{2,1,0:T(8,128)(2,1)S(1)} %get-tuple-element.114), channel_id=1, replica_groups=mesh['section'=4,'row'=4,'z'=8,'core'=2] {'z'}, dimensions={0} | all-to-all | bytes 1310720 | tf_op jit(solution)/shard_map/all_to_all | solution.py:212
  204.4 11.7 %all_to_all.93 = bf16[8,32,512]{2,1,0:T(8,128)(2,1)S(1)} all-to-all(bf16[8,32,512]{2,1,0:T(8,128)(2,1)S(1)} %shard_map.72), channel_id=1, replica_groups=mesh['section'=4,'row'=4,'z'=8,'core'=2] {'z'}, dimensions={0} | all-to-all | bytes 524288 | tf_op jit(solution)/shard_map/all_to_all | solution.py:212
  216.6 11.9 %all_to_all.94.recv_ref = bf16[16,16,1024]{2,1,0:T(8,128)(2,1)S(1)} all-to-all(bf16[16,16,1024]{2,1,0:T(8,128)(2,1)S(1)} %bitcast.49), channel_id=1, replica_groups=mesh['section'=4,'row'=4,'z'=8,'core'=2] {'section','row'}, dimensions={0} | all-to-all | bytes 1048576 | tf_op jit(solution)/shard_map/all_to_all | solution.py:212
  228.6 13.8 %all_to_all.95 = bf16[16,16,1024]{2,1,0:T(8,128)(2,1)S(1)} all-to-all(bf16[16,16,1024]{2,1,0:T(8,128)(2,1)S(1)} %get-tuple-element.116), channel_id=1, replica_groups=mesh['section'=4,'row'=4,'z'=8,'core'=2] {'section','row'}, dimensions={0} | all-to-all | bytes 1048576 | tf_op jit(solution)/shard_map/all_to_all | solution.py:212
  243.2 15.9 %all_to_all.96.recv_ref = bf16[8,160,256]{2,1,0:T(8,128)(2,1)S(1)} all-to-all(bf16[8,160,256]{2,1,0:T(8,128)(2,1)S(1)} %get-tuple-element.119), channel_id=1, replica_groups=mesh['section'=4,'row'=4,'z'=8,'core'=2] {'z'}, dimensions={0} | all-to-all | bytes 1310720 | tf_op jit(solution)/shard_map/all_to_all | solution.py:212
  259.7 14.6 %all_to_all.97 = bf16[8,32,512]{2,1,0:T(8,128)(2,1)S(1)} all-to-all(bf16[8,32,512]{2,1,0:T(8,128)(2,1)S(1)} %shard_map.76), channel_id=1, replica_groups=mesh['section'=4,'row'=4,'z'=8,'core'=2] {'z'}, dimensions={0} | all-to-all | bytes 524288 | tf_op jit(solution)/shard_map/all_to_all | solution.py:212
  274.6 11.9 %all_to_all.98.recv_ref = bf16[16,16,1024]{2,1,0:T(8,128)(2,1)S(1)} all-to-all(bf16[16,16,1024]{2,1,0:T(8,128)(2,1)S(1)} %bitcast.46), channel_id=1, replica_groups=mesh['section'=4,'row'=4,'z'=8,'core'=2] {'section','row'}, dimensions={0} | all-to-all | bytes 1048576 | tf_op jit(solution)/shard_map/all_to_all | solution.py:212
  287.3 11.9 %all_to_all.99 = bf16[16,16,1024]{2,1,0:T(8,128)(2,1)S(1)} all-to-all(bf16[16,16,1024]{2,1,0:T(8,128)(2,1)S(1)} %get-tuple-element.121), channel_id=1, replica_groups=mesh['section'=4,'row'=4,'z'=8,'core'=2] {'section','row'}, dimensions={0} | all-to-all | bytes 1048576 | tf_op jit(solution)/shard_map/all_to_all | solution.py:212
  299.3 18.7 %collective-permute-start.7 = (bf16[256,512]{1,0:T(8,128)(2,1)S(1)}, bf16[256,512]{1,0:T(8,128)(2,1)S(1)}, u32[]{:S(2)}, u32[]{:S(2)}) collective-permute-start(bf16[256,512]{1,0:T(8,128)(2,1)S(1)} %get-tuple-element.136), channel_id=1, source_target_pairs={{0,1},{1,0},{2,3},{3,2},{4,5},{5,4},{6,7},{7,6},{8,9},{9,8},{10,11... | collective-permute-start | bytes 786440 | tf_op jit(solution)/shard_map/ppermute | solution.py:208
  (59 shorter events, 25.6 us)
Async XLA Ops:
  3.3 8.9 %copy-start.2 = (s32[2,32]{1,0:T(2,128)S(1)}, s32[2,32]{1,0:T(2,128)}, u32[]{:S(2)}) copy-start(s32[2,32]{1,0:T(2,128)} %param.9) | copy-start | bytes 772
  3.3 40.5 %all-to-all-start.1 = ((bf16[4,512,768]{2,1,0:T(8,128)(2,1)}), bf16[4,512,768]{2,1,0:T(8,128)(2,1)S(1)}, u32[]{:S(2)}, u32[]{:S(2)}) async-start(bf16[4,512,768]{2,1,0:T(8,128)(2,1)} %shard_map.64), calls=%async_computation.1 | async-start | bytes 6291456 | tf_op jit(solution)/shard_map/all_to_all | solution.py:212
  10.0 7.3 %collective-permute-start = (bf16[256,512]{1,0:T(8,128)(2,1)}, bf16[256,512]{1,0:T(8,128)(2,1)}, u32[]{:S(2)}, u32[]{:S(2)}) collective-permute-start(bf16[256,512]{1,0:T(8,128)(2,1)} %get-tuple-element.138), channel_id=1, source_target_pairs={{0,1},{1,0},{2,3},{3,2},{4,5},{5,4},{6,7},{7,6},{8,9},{9,8},{10,11... | collective-permute-start | bytes 786440 | tf_op jit(solution)/shard_map/ppermute | solution.py:208
  44.7 5.7 %collective-permute-start.1 = (bf16[1,512,768]{2,1,0:T(8,128)(2,1)}, bf16[1,512,768]{2,1,0:T(8,128)(2,1)}, u32[]{:S(2)}, u32[]{:S(2)}) collective-permute-start(bf16[1,512,768]{2,1,0:T(8,128)(2,1)} %slice.21), channel_id=1, source_target_pairs={{0,1},{1,0},{2,3},{3,2},{4,5},{5,4},{6,7},{7,6},{8,9},{9,8},{10,11... | collective-permute-start | bytes 2359304 | tf_op jit(solution)/shard_map/ppermute | solution.py:208
  47.7 32.4 %collective-permute-start.2 = (bf16[512,512]{1,0:T(8,128)(2,1)}, bf16[512,512]{1,0:T(8,128)(2,1)}, u32[]{:S(2)}, u32[]{:S(2)}) collective-permute-start(bf16[512,512]{1,0:T(8,128)(2,1)} %get-tuple-element.86), channel_id=1, source_target_pairs={{0,64},{64,128},{128,192},{192,0},{1,65},{65,129},{129,193},{193,1... | collective-permute-start | bytes 1572872 | tf_op jit(solution)/shard_map/ppermute | solution.py:195
  48.0 32.1 %collective-permute-start.3 = (bf16[512,512]{1,0:T(8,128)(2,1)}, bf16[512,512]{1,0:T(8,128)(2,1)}, u32[]{:S(2)}, u32[]{:S(2)}) collective-permute-start(bf16[512,512]{1,0:T(8,128)(2,1)} %get-tuple-element.87), channel_id=1, source_target_pairs={{0,128},{64,192},{128,0},{192,64},{1,129},{65,193},{129,1},{193,65... | collective-permute-start | bytes 1572872 | tf_op jit(solution)/shard_map/ppermute | solution.py:195
  49.8 30.3 %collective-permute-start.4 = (bf16[512,512]{1,0:T(8,128)(2,1)}, bf16[512,512]{1,0:T(8,128)(2,1)}, u32[]{:S(2)}, u32[]{:S(2)}) collective-permute-start(bf16[512,512]{1,0:T(8,128)(2,1)} %get-tuple-element.88), channel_id=1, source_target_pairs={{0,192},{64,0},{128,64},{192,128},{1,193},{65,1},{129,65},{193,129... | collective-permute-start | bytes 1572872 | tf_op jit(solution)/shard_map/ppermute | solution.py:195
  80.1 4.0 %copy-start = (bf16[8,32,512]{2,1,0:T(8,128)(2,1)}, bf16[8,32,512]{2,1,0:T(8,128)(2,1)S(1)}, u32[]{:S(2)}) copy-start(bf16[8,32,512]{2,1,0:T(8,128)(2,1)S(1)} %get-tuple-element.146) | copy-start | bytes 786436
  80.2 49.5 %collective-permute-start.6 = (bf16[4,512,768]{2,1,0:T(8,128)(2,1)S(1)}, bf16[4,512,768]{2,1,0:T(8,128)(2,1)S(1)}, u32[]{:S(2)}, u32[]{:S(2)}) collective-permute-start(bf16[4,512,768]{2,1,0:T(8,128)(2,1)S(1)} %all-to-all-done.1.near_ref), channel_id=1, source_target_pairs={{0,1},{1,0},{2,3},{3,2},{4,5},{5,4},{6,7},{7,6},{8,9},{9,8},{10,11... | collective-permute-start | bytes 9437192 | tf_op jit(solution)/shard_map/ppermute | solution.py:208
  84.1 1.0 copy-start.1
  84.4 15.5 %collective-permute-start.5 = (bf16[4,512,512]{2,1,0:T(8,128)(2,1)S(1)}, bf16[4,512,512]{2,1,0:T(8,128)(2,1)S(1)}, u32[]{:S(2)}, u32[]{:S(2)}) collective-permute-start(bf16[4,512,512]{2,1,0:T(8,128)(2,1)S(1)} %pad_maximum_fusion.near_ref), channel_id=1, source_target_pairs={{0,1},{1,0},{2,3},{3,2},{4,5},{5,4},{6,7},{7,6},{8,9},{9,8},{10,11... | collective-permute-start | bytes 6291464 | tf_op jit(solution)/shard_map/ppermute | solution.py:208
  299.3 19.9 %collective-permute-start.7 = (bf16[256,512]{1,0:T(8,128)(2,1)S(1)}, bf16[256,512]{1,0:T(8,128)(2,1)S(1)}, u32[]{:S(2)}, u32[]{:S(2)}) collective-permute-start(bf16[256,512]{1,0:T(8,128)(2,1)S(1)} %get-tuple-element.136), channel_id=1, source_target_pairs={{0,1},{1,0},{2,3},{3,2},{4,5},{5,4},{6,7},{7,6},{8,9},{9,8},{10,11... | collective-permute-start | bytes 786440 | tf_op jit(solution)/shard_map/ppermute | solution.py:208

commit v7 on v6

--- a/solution.py
+++ b/solution.py
@@ -191,8 +191,8 @@
     return chosen
 
 
-def rotated(value, steps):
-    return lax.ppermute(value, "section", [(s, (s + steps) % 4) for s in range(4)])
+def traded(value, bits):
+    return lax.ppermute(value, "section", [(s, s ^ bits) for s in range(4)])
 
 
 def segment_info(lengths_row, total):
@@ -219,8 +219,8 @@
     grid_place = section * 4 + lax.axis_index("row")
 
     near_in = exchange(weigh(w_query, w_pair, gain), "section")
-    blocks_out = [lax.dynamic_slice(w_out, (0, 512 * ((section + k) % 4), 0), (1, 512, 512))[0] for k in range(4)]
-    turn = [(section - layer) % 4 for layer in range(LAYERS)]
+    blocks_out = [lax.dynamic_slice(w_out, (0, 512 * (section ^ k), 0), (1, 512, 512))[0] for k in range(4)]
+    turn = [section ^ layer for layer in range(LAYERS)]
 
     mine = lax.dynamic_index_in_dim(hidden_in, core, 0, keepdims=False)
     theirs = lax.dynamic_index_in_dim(hidden_in, 1 - core, 0, keepdims=False)
@@ -269,7 +269,7 @@
         return mix(packed)
 
     far_first = swap(near_in[:1])
-    moved_out = [blocks_out[0]] + [rotated(blocks_out[k], k) for k in range(1, 4)]
+    moved_out = [blocks_out[0]] + [traded(blocks_out[k], k) for k in range(1, 4)]
     kept = None
     for layer in range(LAYERS):
         if layer == 1:

time: 321 us -> 318 us (level)
  blocking collectives: 235 us -> 231 us
    all_to_all x16, blocking collectives: 235 us -> 231 us  [exchange(): return lax.all_to_all(value, axis, 0, 0, tiled=True)]
where the time goes in v7:
time: 318 us; the launch traced here: 317 us
  blocking collectives  231 us (73%)
  starting transfers between devices  35 us (11%)
  waiting for transfers between devices  25 us (8%)
  Pallas kernels  12.3 us (4%)
  local copies, waits for them, and re-layouts  6.55 us (2%)
  other arithmetic  6.29 us (2%)
    all_to_all x16, blocking collectives, exchange(): return lax.all_to_all(value, axis, 0, 0, tiled=True)  231 us
    ppermute x5, starting transfers between devices, swap(): return lax.ppermute(value, 'core', [(0, 1), (1, 0)])  26.2 us
    all_to_all x1, waiting for transfers between devices, exchange(): return lax.all_to_all(value, axis, 0, 0, tiled=True)  23.8 us
  transfers between devices with their start and end apart: 9, of which 2 were waited for; matrix products, arithmetic and copies ran while one was open for 3% of the time, Pallas kernels for 1%

profile of v7, /device:TPU:1, one launch (start us, length us, event | category | flops | bytes accessed | tf_op | source)
XLA Modules:
  0.0 317.2 jit_solution(12400141938284956326)
XLA Ops:
  0.0 3.3 %shard_map.64 = bf16[4,512,768]{2,1,0:T(8,128)(2,1)} custom-call(bf16[1,512,2048]{2,1,0:T(8,128)(2,1)} %query_ref.1, bf16[1,512,512]{2,1,0:T(8,128)(2,1)} %pair_ref.1, f32[1,512]{1,0:T(1,128)} %gain_ref.1), custom_call_target="tpu_custom_call" | custom-call | flops 2000000 | bytes 6000000 | tf_op jit(solution)/shard_map/pallas_call | solution.py:172
  3.3 5.0 %all-to-all-start.1 = ((bf16[4,512,768]{2,1,0:T(8,128)(2,1)}), bf16[4,512,768]{2,1,0:T(8,128)(2,1)S(1)}, u32[]{:S(2)}, u32[]{:S(2)}) async-start(bf16[4,512,768]{2,1,0:T(8,128)(2,1)} %shard_map.64), calls=%async_computation.1 | async-start | bytes 6291456 | tf_op jit(solution)/shard_map/all_to_all | solution.py:212
  13.0 2.9 dynamic-slice_bitcast_fusion
  19.9 23.8 %all-to-all-done.1.near_ref = bf16[4,512,768]{2,1,0:T(8,128)(2,1)S(1)} async-done(((bf16[4,512,768]{2,1,0:T(8,128)(2,1)}), bf16[4,512,768]{2,1,0:T(8,128)(2,1)S(1)}, u32[]{:S(2)}, u32[]{:S(2)}) %all-to-all-start.1) | async-done | bytes 3145760 | tf_op jit(solution)/shard_map/all_to_all | solution.py:212
  44.7 3.0 collective-permute-start.1
  51.6 29.6 %conditional.1 = (bf16[8,32,512]{2,1,0:T(8,128)(2,1)S(1)}) conditional(s32[]{:T(128)} %convert_element_type.19, () %tuple.17, (bf16[256,1024]{1,0:T(8,128)(2,1)}, bf16[4,512,768]{2,1,0:T(8,128)(2,1)S(1)}, bf16[1,512,768]{2,1,0:T(8,128)(2,1)}, s32[1]{0:T(128)}, f32[96,128]{1,0:T(8,128)S(1)}, /*index=5*/f32[96,128]{1,0:T(8,128)S(1)}, ...), branch_computations={%region_3.4_spmd, %region_4.5_spmd} | conditional | flops 546870912 | bytes 5310728 | solution.py:281
  53.6 27.0 %all_to_all.84.recv_ref = bf16[8,160,256]{2,1,0:T(8,128)(2,1)S(1)} all-to-all(bf16[8,160,256]{2,1,0:T(8,128)(2,1)S(1)} %branch_1_fun.2), channel_id=1, replica_groups=mesh['section'=4,'row'=4,'z'=8,'core'=2] {'z'}, dimensions={0} | all-to-all | bytes 1310720 | tf_op jit(solution)/shard_map/cond/branch_1_fun/all_to_all | solution.py:212
  81.2 2.3 collective-permute-start.6
  85.7 14.6 %all_to_all.85 = bf16[8,32,512]{2,1,0:T(8,128)(2,1)S(1)} all-to-all(bf16[8,32,512]{2,1,0:T(8,128)(2,1)S(1)} %get-tuple-element.146), channel_id=1, replica_groups=mesh['section'=4,'row'=4,'z'=8,'core'=2] {'z'}, dimensions={0} | all-to-all | bytes 524288 | tf_op jit(solution)/shard_map/all_to_all | solution.py:212
  100.7 13.1 %all_to_all.86.recv_ref = bf16[16,16,1024]{2,1,0:T(8,128)(2,1)S(1)} all-to-all(bf16[16,16,1024]{2,1,0:T(8,128)(2,1)S(1)} %bitcast.47), channel_id=1, replica_groups=mesh['section'=4,'row'=4,'z'=8,'core'=2] {'section','row'}, dimensions={0} | all-to-all | bytes 1048576 | tf_op jit(solution)/shard_map/all_to_all | solution.py:212
  114.0 13.2 %all_to_all.87 = bf16[16,16,1024]{2,1,0:T(8,128)(2,1)S(1)} all-to-all(bf16[16,16,1024]{2,1,0:T(8,128)(2,1)S(1)} %get-tuple-element.109), channel_id=1, replica_groups=mesh['section'=4,'row'=4,'z'=8,'core'=2] {'section','row'}, dimensions={0} | all-to-all | bytes 1048576 | tf_op jit(solution)/shard_map/all_to_all | solution.py:212
  127.9 18.8 %all_to_all.88.recv_ref = bf16[8,160,256]{2,1,0:T(8,128)(2,1)S(1)} all-to-all(bf16[8,160,256]{2,1,0:T(8,128)(2,1)S(1)} %shard_map.67), channel_id=1, replica_groups=mesh['section'=4,'row'=4,'z'=8,'core'=2] {'z'}, dimensions={0} | all-to-all | bytes 1310720 | tf_op jit(solution)/shard_map/all_to_all | solution.py:212
  147.2 12.5 %all_to_all.89 = bf16[8,32,512]{2,1,0:T(8,128)(2,1)S(1)} all-to-all(bf16[8,32,512]{2,1,0:T(8,128)(2,1)S(1)} %shard_map.68), channel_id=1, replica_groups=mesh['section'=4,'row'=4,'z'=8,'core'=2] {'z'}, dimensions={0} | all-to-all | bytes 524288 | tf_op jit(solution)/shard_map/all_to_all | solution.py:212
  160.2 12.0 %all_to_all.90.recv_ref = bf16[16,16,1024]{2,1,0:T(8,128)(2,1)S(1)} all-to-all(bf16[16,16,1024]{2,1,0:T(8,128)(2,1)S(1)} %bitcast.48), channel_id=1, replica_groups=mesh['section'=4,'row'=4,'z'=8,'core'=2] {'section','row'}, dimensions={0} | all-to-all | bytes 1048576 | tf_op jit(solution)/shard_map/all_to_all | solution.py:212
  172.3 11.9 %all_to_all.91 = bf16[16,16,1024]{2,1,0:T(8,128)(2,1)S(1)} all-to-all(bf16[16,16,1024]{2,1,0:T(8,128)(2,1)S(1)} %get-tuple-element.112), channel_id=1, replica_groups=mesh['section'=4,'row'=4,'z'=8,'core'=2] {'section','row'}, dimensions={0} | all-to-all | bytes 1048576 | tf_op jit(solution)/shard_map/all_to_all | solution.py:212
  185.0 16.1 %all_to_all.92.recv_ref = bf16[8,160,256]{2,1,0:T(8,128)(2,1)S(1)} all-to-all(bf16[8,160,256]{2,1,0:T(8,128)(2,1)S(1)} %get-tuple-element.114), channel_id=1, replica_groups=mesh['section'=4,'row'=4,'z'=8,'core'=2] {'z'}, dimensions={0} | all-to-all | bytes 1310720 | tf_op jit(solution)/shard_map/all_to_all | solution.py:212
  201.6 11.7 %all_to_all.93 = bf16[8,32,512]{2,1,0:T(8,128)(2,1)S(1)} all-to-all(bf16[8,32,512]{2,1,0:T(8,128)(2,1)S(1)} %shard_map.72), channel_id=1, replica_groups=mesh['section'=4,'row'=4,'z'=8,'core'=2] {'z'}, dimensions={0} | all-to-all | bytes 524288 | tf_op jit(solution)/shard_map/all_to_all | solution.py:212
  213.8 11.9 %all_to_all.94.recv_ref = bf16[16,16,1024]{2,1,0:T(8,128)(2,1)S(1)} all-to-all(bf16[16,16,1024]{2,1,0:T(8,128)(2,1)S(1)} %bitcast.49), channel_id=1, replica_groups=mesh['section'=4,'row'=4,'z'=8,'core'=2] {'section','row'}, dimensions={0} | all-to-all | bytes 1048576 | tf_op jit(solution)/shard_map/all_to_all | solution.py:212
  225.8 13.8 %all_to_all.95 = bf16[16,16,1024]{2,1,0:T(8,128)(2,1)S(1)} all-to-all(bf16[16,16,1024]{2,1,0:T(8,128)(2,1)S(1)} %get-tuple-element.116), channel_id=1, replica_groups=mesh['section'=4,'row'=4,'z'=8,'core'=2] {'section','row'}, dimensions={0} | all-to-all | bytes 1048576 | tf_op jit(solution)/shard_map/all_to_all | solution.py:212
  240.4 15.9 %all_to_all.96.recv_ref = bf16[8,160,256]{2,1,0:T(8,128)(2,1)S(1)} all-to-all(bf16[8,160,256]{2,1,0:T(8,128)(2,1)S(1)} %get-tuple-element.119), channel_id=1, replica_groups=mesh['section'=4,'row'=4,'z'=8,'core'=2] {'z'}, dimensions={0} | all-to-all | bytes 1310720 | tf_op jit(solution)/shard_map/all_to_all | solution.py:212
  256.9 14.6 %all_to_all.97 = bf16[8,32,512]{2,1,0:T(8,128)(2,1)S(1)} all-to-all(bf16[8,32,512]{2,1,0:T(8,128)(2,1)S(1)} %shard_map.76), channel_id=1, replica_groups=mesh['section'=4,'row'=4,'z'=8,'core'=2] {'z'}, dimensions={0} | all-to-all | bytes 524288 | tf_op jit(solution)/shard_map/all_to_all | solution.py:212
  271.9 11.9 %all_to_all.98.recv_ref = bf16[16,16,1024]{2,1,0:T(8,128)(2,1)S(1)} all-to-all(bf16[16,16,1024]{2,1,0:T(8,128)(2,1)S(1)} %bitcast.46), channel_id=1, replica_groups=mesh['section'=4,'row'=4,'z'=8,'core'=2] {'section','row'}, dimensions={0} | all-to-all | bytes 1048576 | tf_op jit(solution)/shard_map/all_to_all | solution.py:212
  284.5 11.9 %all_to_all.99 = bf16[16,16,1024]{2,1,0:T(8,128)(2,1)S(1)} all-to-all(bf16[16,16,1024]{2,1,0:T(8,128)(2,1)S(1)} %get-tuple-element.121), channel_id=1, replica_groups=mesh['section'=4,'row'=4,'z'=8,'core'=2] {'section','row'}, dimensions={0} | all-to-all | bytes 1048576 | tf_op jit(solution)/shard_map/all_to_all | solution.py:212
  296.5 18.7 %collective-permute-start.7 = (bf16[256,512]{1,0:T(8,128)(2,1)S(1)}, bf16[256,512]{1,0:T(8,128)(2,1)S(1)}, u32[]{:S(2)}, u32[]{:S(2)}) collective-permute-start(bf16[256,512]{1,0:T(8,128)(2,1)S(1)} %get-tuple-element.136), channel_id=1, source_target_pairs={{0,1},{1,0},{2,3},{3,2},{4,5},{5,4},{6,7},{7,6},{8,9},{9,8},{10,11... | collective-permute-start | bytes 786440 | tf_op jit(solution)/shard_map/ppermute | solution.py:208
  (55 shorter events, 26.2 us)
Async XLA Ops:
  3.3 8.9 %copy-start = (s32[2,32]{1,0:T(2,128)S(1)}, s32[2,32]{1,0:T(2,128)}, u32[]{:S(2)}) copy-start(s32[2,32]{1,0:T(2,128)} %param.9) | copy-start | bytes 772
  3.3 40.5 %all-to-all-start.1 = ((bf16[4,512,768]{2,1,0:T(8,128)(2,1)}), bf16[4,512,768]{2,1,0:T(8,128)(2,1)S(1)}, u32[]{:S(2)}, u32[]{:S(2)}) async-start(bf16[4,512,768]{2,1,0:T(8,128)(2,1)} %shard_map.64), calls=%async_computation.1 | async-start | bytes 6291456 | tf_op jit(solution)/shard_map/all_to_all | solution.py:212
  10.0 7.4 %collective-permute-start = (bf16[256,512]{1,0:T(8,128)(2,1)}, bf16[256,512]{1,0:T(8,128)(2,1)}, u32[]{:S(2)}, u32[]{:S(2)}) collective-permute-start(bf16[256,512]{1,0:T(8,128)(2,1)} %get-tuple-element.138), channel_id=1, source_target_pairs={{0,1},{1,0},{2,3},{3,2},{4,5},{5,4},{6,7},{7,6},{8,9},{9,8},{10,11... | collective-permute-start | bytes 786440 | tf_op jit(solution)/shard_map/ppermute | solution.py:208
  44.7 6.9 %collective-permute-start.1 = (bf16[1,512,768]{2,1,0:T(8,128)(2,1)}, bf16[1,512,768]{2,1,0:T(8,128)(2,1)}, u32[]{:S(2)}, u32[]{:S(2)}) collective-permute-start(bf16[1,512,768]{2,1,0:T(8,128)(2,1)} %slice.21), channel_id=1, source_target_pairs={{0,1},{1,0},{2,3},{3,2},{4,5},{5,4},{6,7},{7,6},{8,9},{9,8},{10,11... | collective-permute-start | bytes 2359304 | tf_op jit(solution)/shard_map/ppermute | solution.py:208
  47.7 33.5 %collective-permute-start.2 = (bf16[512,512]{1,0:T(8,128)(2,1)}, bf16[512,512]{1,0:T(8,128)(2,1)}, u32[]{:S(2)}, u32[]{:S(2)}) collective-permute-start(bf16[512,512]{1,0:T(8,128)(2,1)} %get-tuple-element.86), channel_id=1, source_target_pairs={{0,64},{64,0},{128,192},{192,128},{1,65},{65,1},{129,193},{193,129... | collective-permute-start | bytes 1572872 | tf_op jit(solution)/shard_map/ppermute | solution.py:195
  48.0 33.2 %collective-permute-start.3 = (bf16[512,512]{1,0:T(8,128)(2,1)}, bf16[512,512]{1,0:T(8,128)(2,1)}, u32[]{:S(2)}, u32[]{:S(2)}) collective-permute-start(bf16[512,512]{1,0:T(8,128)(2,1)} %get-tuple-element.87), channel_id=1, source_target_pairs={{0,128},{64,192},{128,0},{192,64},{1,129},{65,193},{129,1},{193,65... | collective-permute-start | bytes 1572872 | tf_op jit(solution)/shard_map/ppermute | solution.py:195
  49.8 31.4 %collective-permute-start.4 = (bf16[512,512]{1,0:T(8,128)(2,1)}, bf16[512,512]{1,0:T(8,128)(2,1)}, u32[]{:S(2)}, u32[]{:S(2)}) collective-permute-start(bf16[512,512]{1,0:T(8,128)(2,1)} %get-tuple-element.88), channel_id=1, source_target_pairs={{0,192},{64,128},{128,64},{192,0},{1,193},{65,129},{129,65},{193,1... | collective-permute-start | bytes 1572872 | tf_op jit(solution)/shard_map/ppermute | solution.py:195
  81.2 46.0 %collective-permute-start.6 = (bf16[4,512,768]{2,1,0:T(8,128)(2,1)S(1)}, bf16[4,512,768]{2,1,0:T(8,128)(2,1)S(1)}, u32[]{:S(2)}, u32[]{:S(2)}) collective-permute-start(bf16[4,512,768]{2,1,0:T(8,128)(2,1)S(1)} %all-to-all-done.1.near_ref), channel_id=1, source_target_pairs={{0,1},{1,0},{2,3},{3,2},{4,5},{5,4},{6,7},{7,6},{8,9},{9,8},{10,11... | collective-permute-start | bytes 9437192 | tf_op jit(solution)/shard_map/ppermute | solution.py:208
  85.6 14.7 %collective-permute-start.5 = (bf16[4,512,512]{2,1,0:T(8,128)(2,1)S(1)}, bf16[4,512,512]{2,1,0:T(8,128)(2,1)S(1)}, u32[]{:S(2)}, u32[]{:S(2)}) collective-permute-start(bf16[4,512,512]{2,1,0:T(8,128)(2,1)S(1)} %pad_maximum_fusion.near_ref), channel_id=1, source_target_pairs={{0,1},{1,0},{2,3},{3,2},{4,5},{5,4},{6,7},{7,6},{8,9},{9,8},{10,11... | collective-permute-start | bytes 6291464 | tf_op jit(solution)/shard_map/ppermute | solution.py:208
  296.5 19.8 %collective-permute-start.7 = (bf16[256,512]{1,0:T(8,128)(2,1)S(1)}, bf16[256,512]{1,0:T(8,128)(2,1)S(1)}, u32[]{:S(2)}, u32[]{:S(2)}) collective-permute-start(bf16[256,512]{1,0:T(8,128)(2,1)S(1)} %get-tuple-element.136), channel_id=1, source_target_pairs={{0,1},{1,0},{2,3},{3,2},{4,5},{5,4},{6,7},{7,6},{8,9},{9,8},{10,11... | collective-permute-start | bytes 786440 | tf_op jit(solution)/shard_map/ppermute | solution.py:208
